TPU v7x, 512 devices: a whole 4x4x16 slice. The times are simulated.
512 devices in a mesh: slab: 16 (over y, z_hi), tile: 32 (over z_lo, x, core).
Axes of the slice: x: 4, y: 4, z: 16 (z_hi: 4, z_lo: 4; z = z_hi * 4 + z_lo), core: 2. Of those that a mesh axis runs over, the one named last changes fastest.
Arguments:
- positions: float32 [16, 32, 32, 3, 128], P('slab', 'tile'), as said below
- charges: float32 [16, 32, 32, 128], P('slab', 'tile'), may hold values from -3 to 3
- radii: float32 [16, 32, 32, 128], P('slab', 'tile'), may hold values from 1.4 to 2
- scales: float32 [16, 32, 32, 128], P('slab', 'tile'), may hold values from 0.7 to 0.95
- neighbours: int32 [16, 32, 32, 8], P('slab', 'tile'), may hold values from 0 to 16383, as said below
- pad_mask: int32 [16, 32, 32, 8], P('slab', 'tile'), may hold values from 0 to 1, as said below
Outputs:
- born_radii: float32 [16, 32, 32, 128], P('slab', 'tile')
- radius_grad: float32 [16, 32, 32, 128], P('slab', 'tile')
- forces: float32 [16, 32, 32, 3, 128], P('slab', 'tile')
Inputs may be any that keep to these rules, and one draw needn't show every extreme that they name: positions: each tile's atoms sit in that tile's own box of a cylindrical shell, at one of two radial levels; any two atoms of different tiles or of one tile lie 0.9 or more apart. `neighbours`: ids count tiles as (slab * 32 + cycle index) * 32 + local index. A tile held by the device at slab s and cycle index t lists only tiles of slabs s - 1, s, s + 1 held at cycle index t or t + 1 (modulo 32); tiles held at cycle index t + 1 are listed only at local index 0 or 1, and only by tiles of local index 30 or 31; slot 0 names the tile itself, other slots name other tiles, and no two tiles list each other on live slots. `pad_mask`: each tile's live slots come first; slot 0 is always live; some tile has all 8 slots live.
All inputs are finite; a program needn't handle non-finite values.
Results may differ from a plain program's by a relative error of at most 0.0003.
Values sent between devices are 32-bit elements; how exact they have to be, the bound alone decides.
No kernel may reach another device: no remote copies, remote signals or barrier semaphores. Data moves between devices by JAX's collectives and lax.ppermute only.
A program may use at most 64 MiB of HBM per device.

v0:
```python
import jax
import jax.numpy as jnp
from jax import lax
from jax.sharding import PartitionSpec as P

radius_offset = 0.09
obc_alpha = 1.0
obc_beta = 0.8
obc_gamma = 4.85
cutoff_len = 14.0


def extended(cells, sides, width):
    for axis, dim in sides:
        count = lax.axis_size(axis)
        ends = count - 1
        head = lax.slice_in_dim(cells, 0, width, axis=dim)
        tail = lax.slice_in_dim(cells, cells.shape[dim] - width, cells.shape[dim], axis=dim)
        cells = jnp.concatenate(
            [
                lax.ppermute(tail, axis, [(i, (i + 1) % count) for i in range(ends)]),
                cells,
                lax.ppermute(head, axis, [((i + 1) % count, i) for i in range(ends)]),
            ],
            axis=dim,
        )
    return cells


def shifted(block, axis, distance):
    devices = range(lax.axis_size(axis))
    route = [((i - distance) % len(devices), i) for i in devices]
    return lax.ppermute(block, axis, route)


def shifted_2(array, axis, by):
    devices = lax.axis_size(axis)
    pairs = [(i, i + by) for i in range(devices) if 0 <= i + by < devices]
    return lax.ppermute(array, axis, pairs)


def gap_squared(coords_one, coords_two, self_flag):
    differ = coords_one[..., :, :, None] - coords_two[..., :, None, :]
    squared = jnp.sum(differ * differ, axis=-3)
    unit_diag = jnp.eye(coords_one.shape[-1], dtype=jnp.float32)
    return squared + self_flag[..., None, None] * unit_diag * (4.0 * cutoff_len * cutoff_len)


def smooth_switch(squared):
    switch_base = jnp.maximum(1.0 - squared / (cutoff_len * cutoff_len), 0.0)
    return switch_base * switch_base


def descreen(distance, radius_own, radius_far):
    upper_end = distance + radius_far
    lower_end = jnp.minimum(jnp.maximum(radius_own, jnp.abs(distance - radius_far)), upper_end)
    inv_lower = 1.0 / lower_end
    inv_upper = 1.0 / upper_end
    return 0.5 * (
        inv_lower
        - inv_upper
        + 0.25 * distance * (inv_upper * inv_upper - inv_lower * inv_lower)
        + 0.5 / distance * jnp.log(lower_end * inv_upper)
        + 0.25
        * radius_far
        * radius_far
        / distance
        * (inv_lower * inv_lower - inv_upper * inv_upper)
    )


def born_pair(data_one, data_two, self_flag, live_weight):
    squared = gap_squared(data_one[..., 0:3, :], data_two[..., 0:3, :], self_flag)
    distance = jnp.sqrt(squared)
    weight = smooth_switch(squared) * live_weight[..., None, None]
    own_part = jnp.sum(
        weight * descreen(distance, data_one[..., 4, :, None], data_two[..., 5, None, :]), axis=-1
    )
    far_part = (1.0 - self_flag)[..., None] * jnp.sum(
        weight * descreen(distance, data_two[..., 4, None, :], data_one[..., 5, :, None]), axis=-2
    )
    return (own_part, far_part)


def screened(squared, radius_one, radius_two, data_one, data_two, self_flag, weight):
    product = radius_one[..., :, None] * radius_two[..., None, :]
    effective = jnp.sqrt(squared + product * jnp.exp(-squared / (4.0 * product)))
    return (
        -(1.0 - 0.5 * self_flag)[..., None, None]
        * weight
        * data_one[..., 3, :, None]
        * data_two[..., 3, None, :]
        / effective
    )


def radius_pair(radius_one, radius_two, data_one, data_two, self_flag, live_weight):
    squared = gap_squared(data_one[..., 0:3, :], data_two[..., 0:3, :], self_flag)
    weight = smooth_switch(squared) * live_weight[..., None, None]

    def energy(first_set, second_set):
        return jnp.sum(
            screened(squared, first_set, second_set, data_one, data_two, self_flag, weight)
        )

    result_value, pullback = jax.vjp(energy, radius_one, radius_two)
    return pullback(jnp.ones_like(result_value))


def force_pair(
    coords_one,
    coords_two,
    data_one,
    data_two,
    radius_one,
    radius_two,
    chain_one,
    chain_two,
    self_flag,
    live_weight,
):

    def total_energy(first_set, second_set):
        squared = gap_squared(first_set, second_set, self_flag)
        distance = jnp.sqrt(squared)
        weight = smooth_switch(squared) * live_weight[..., None, None]
        energy = screened(squared, radius_one, radius_two, data_one, data_two, self_flag, weight)
        screen = chain_one[..., :, None] * descreen(
            distance, data_one[..., 4, :, None], data_two[..., 5, None, :]
        )
        screen = screen + (1.0 - self_flag)[..., None, None] * chain_two[..., None, :] * descreen(
            distance, data_two[..., 4, None, :], data_one[..., 5, :, None]
        )
        return jnp.sum(energy + weight * screen)

    result_value, pullback = jax.vjp(total_energy, coords_one, coords_two)
    grad_one, grad_two = pullback(jnp.ones_like(result_value))
    return (-grad_one, -grad_two)


def born_radius(descreen_sum, radius):
    radius_in = radius - radius_offset
    scaled = radius_in * descreen_sum
    polynomial = scaled * (obc_alpha + scaled * (-obc_beta + obc_gamma * scaled))
    tangent = jnp.tanh(polynomial)
    radii_born = 1.0 / (1.0 / radius_in - tangent / radius)
    radius_slope = (
        radii_born
        * radii_born
        * (1.0 - tangent * tangent)
        / radius
        * (obc_alpha - 2.0 * obc_beta * scaled + 3.0 * obc_gamma * scaled * scaled)
        * radius_in
    )
    return (radii_born, radius_slope)


def take_slot(array, slot):
    return lax.dynamic_index_in_dim(array, slot, 0, keepdims=False)


def slot_flag(slot):
    return (slot == 0).astype(jnp.float32)


def body(positions, charges, radii, scales, neighbours, pad_mask):
    coords = positions[0, 0]
    charge = charges[0, 0]
    radius = radii[0, 0]
    radius_in = radius - radius_offset
    atom_data = jnp.concatenate(
        [coords, charge[:, None], radius_in[:, None], (scales[0, 0] * radius_in)[:, None]], axis=1
    )
    tile_count = coords.shape[0]
    widened_count = tile_count + 2
    cycle_count = lax.axis_size("tile")
    cycle_tiles = cycle_count * tile_count
    listed = neighbours[0, 0]
    slot_count = listed.shape[1]
    live_slots = pad_mask[0, 0].astype(jnp.float32).T
    slab_other = listed // cycle_tiles
    within = listed % cycle_tiles
    cycle_step = (within // tile_count - lax.axis_index("tile")) % cycle_count
    local_place = (
        (slab_other - lax.axis_index("slab") + 1) * widened_count
        + cycle_step * tile_count
        + within % tile_count
    )
    place_slots = local_place.T
    selector = (place_slots.reshape(-1)[:, None] == jnp.arange(3 * widened_count)[None, :]).astype(
        jnp.float32
    )

    def spread(values):
        own_block = values[None]
        widened = extended(own_block, (("slab", 0),), 1)
        assembled = jnp.concatenate([widened, shifted(widened[:, 0:2], "tile", -1)], axis=1)
        return assembled.reshape((3 * widened_count,) + values.shape[1:])[place_slots]

    def collect(parts):
        flattened = parts.reshape(slot_count * tile_count, -1)
        summed = jnp.dot(selector.T, flattened, precision=lax.Precision.HIGHEST).reshape(
            (3, widened_count) + parts.shape[2:]
        )
        middle = summed[1]
        for source_row, offset in ((0, -1), (2, 1)):
            middle = middle + shifted_2(summed[source_row], "slab", offset)
        received = shifted(middle[tile_count:], "tile", 1)
        return jnp.concatenate([middle[0:2] + received, middle[2:tile_count]], axis=0)

    def sweep(slot_work, own_zero, far_zero):

        def advance(slot, carry):
            own_sum, far_all = carry
            own_add, far_add = slot_work(slot)
            return (own_sum + own_add, lax.dynamic_update_index_in_dim(far_all, far_add, slot, 0))

        return lax.fori_loop(0, slot_count, advance, (own_zero, far_zero))

    far_data = spread(atom_data)
    zero_atoms = jnp.zeros_like(charge)
    zero_slots = jnp.zeros((slot_count,) + charge.shape, jnp.float32)
    own_sum, far_all = sweep(
        lambda slot: born_pair(
            atom_data, take_slot(far_data, slot), slot_flag(slot), take_slot(live_slots, slot)
        ),
        zero_atoms,
        zero_slots,
    )
    descreen_sum = own_sum + collect(far_all[:, :, None])[:, 0]
    radii_born, radius_slope = born_radius(descreen_sum, radius)
    far_born = spread(radii_born[:, None])[:, :, 0]
    own_sum, far_all = sweep(
        lambda slot: radius_pair(
            radii_born,
            take_slot(far_born, slot),
            atom_data,
            take_slot(far_data, slot),
            slot_flag(slot),
            take_slot(live_slots, slot),
        ),
        zero_atoms,
        zero_slots,
    )
    gradient = (
        own_sum
        + collect(far_all[:, :, None])[:, 0]
        + 0.5 * charge * charge / (radii_born * radii_born)
    )
    chain_coef = gradient * radius_slope
    far_chain = spread(chain_coef[:, None])[:, :, 0]
    own_sum, far_all = sweep(
        lambda slot: force_pair(
            coords,
            take_slot(far_data, slot)[:, 0:3],
            atom_data,
            take_slot(far_data, slot),
            radii_born,
            take_slot(far_born, slot),
            chain_coef,
            take_slot(far_chain, slot),
            slot_flag(slot),
            take_slot(live_slots, slot),
        ),
        jnp.zeros_like(coords),
        jnp.zeros((slot_count,) + coords.shape, jnp.float32),
    )
    forces = own_sum + collect(far_all)
    return (radii_born[None, None], gradient[None, None], forces[None, None])


def solution(mesh):
    return jax.shard_map(
        body,
        mesh=mesh,
        in_specs=(
            P("slab", "tile", None, None, None),
            P("slab", "tile", None, None),
            P("slab", "tile", None, None),
            P("slab", "tile", None, None),
            P("slab", "tile", None, None),
            P("slab", "tile", None, None),
        ),
        out_specs=(
            P("slab", "tile", None, None),
            P("slab", "tile", None, None),
            P("slab", "tile", None, None, None),
        ),
        check_vma=False,
    )
```

profile of v0, /device:TPU:24, one launch (start us, length us, event | category | flops | bytes accessed | tf_op | source)
XLA Modules:
  0.0 483.4 jit_solution(18253189749795526192)
XLA Ops:
  2.9 9.1 %collective-permute-start = (f32[1,32,6,128]{3,1,2,0:T(8,128)S(1)}, f32[1,32,6,128]{3,1,2,0:T(8,128)S(1)}, u32[]{:S(2)}, u32[]{:S(2)}) collective-permute-start(f32[1,32,6,128]{3,1,2,0:T(8,128)S(1)} %maximum_bitcast_fusion), channel_id=1, source_target_pairs={{0,32},{32,64},{64,96},{96,128},{128,160},{160,192},{192,224},{224... | collective-permute-start | bytes 294920 | tf_op jit(solution)/shard_map/ppermute | solution.py:21
  20.0 10.0 %collective-permute-done.1 = f32[1,32,6,128]{3,1,2,0:T(8,128)S(1)} collective-permute-done((f32[1,32,6,128]{3,1,2,0:T(8,128)S(1)}, f32[1,32,6,128]{3,1,2,0:T(8,128)S(1)}, u32[]{:S(2)}, u32[]{:S(2)}) %collective-permute-start.1) | collective-permute-done | bytes 98336 | tf_op jit(solution)/shard_map/ppermute | solution.py:23
  34.8 67.9 %while.48 = (s32[]{:T(128)}, f32[32,128]{1,0:T(8,128)S(1)}, f32[8,32,128]{2,1,0:T(8,128)S(1)}, f32[1,1,32,3,128]{4,3,2,1,0:T(4,128)S(1)}, f32[8,32,6,128]{3,1,2,...) while((s32[]{:T(128)}, f32[32,128]{1,0:T(8,128)S(1)}, ...), condition=%wide.region_4.5_spmd.clone, body=%wide.region_0.4_spmd.clone.sunk | while | flops 32575492 | bytes 5145116 | solution.py:218
  37.0 6.2 %multiply_reduce_fusion.11 = (f32[32,128]{1,0:T(8,128)S(1)}, f32[32,128]{1,0:T(8,128)S(1)}) fusion(f32[32,128,128]{2,1,0:T(8,128)S(1)} %multiply_reduce_fusion.10, f32[32,128]{1,0:T(8,128)S(1)} %multiply_multiply_fusion.16, f32[32,128]{1,0:T(8,128)S(1)} %get-tuple-element.1020, f32[32,128]{1,0:T(8,128)S(1)} %get-tuple-element.953, f32[32]{0:T(128)S(1)} %fusion.113, ...), kind=kLoop, calls=%fused_computation.4.clone.1 | loop fusion | flops 28303360 | bytes 2293888 | tf_op jit(solution)/shard_map/while/body/eval_jaxpr/reduce_sum | solution.py:79
  45.5 6.2 %multiply_reduce_fusion.11 = (f32[32,128]{1,0:T(8,128)S(1)}, f32[32,128]{1,0:T(8,128)S(1)}) fusion(f32[32,128,128]{2,1,0:T(8,128)S(1)} %multiply_reduce_fusion.10, f32[32,128]{1,0:T(8,128)S(1)} %multiply_multiply_fusion.16, f32[32,128]{1,0:T(8,128)S(1)} %get-tuple-element.1020, f32[32,128]{1,0:T(8,128)S(1)} %get-tuple-element.953, f32[32]{0:T(128)S(1)} %fusion.113, ...), kind=kLoop, calls=%fused_computation.4.clone.1 | loop fusion | flops 28303360 | bytes 2293888 | tf_op jit(solution)/shard_map/while/body/eval_jaxpr/reduce_sum | solution.py:79
  54.0 6.2 %multiply_reduce_fusion.11 = (f32[32,128]{1,0:T(8,128)S(1)}, f32[32,128]{1,0:T(8,128)S(1)}) fusion(f32[32,128,128]{2,1,0:T(8,128)S(1)} %multiply_reduce_fusion.10, f32[32,128]{1,0:T(8,128)S(1)} %multiply_multiply_fusion.16, f32[32,128]{1,0:T(8,128)S(1)} %get-tuple-element.1020, f32[32,128]{1,0:T(8,128)S(1)} %get-tuple-element.953, f32[32]{0:T(128)S(1)} %fusion.113, ...), kind=kLoop, calls=%fused_computation.4.clone.1 | loop fusion | flops 28303360 | bytes 2293888 | tf_op jit(solution)/shard_map/while/body/eval_jaxpr/reduce_sum | solution.py:79
  113.1 6.4 %collective-permute-done.4 = f32[34,1,128]{2,0,1:T(8,128)S(1)} collective-permute-done((f32[34,1,128]{2,0,1:T(8,128)S(1)}, f32[34,1,128]{2,0,1:T(8,128)S(1)}, u32[]{:S(2)}, u32[]{:S(2)}) %collective-permute-start.4) | collective-permute-done | bytes 17440 | tf_op jit(solution)/shard_map/ppermute | solution.py:39
  121.9 6.4 %collective-permute-done.5 = f32[2,1,128]{2,0,1:T(2,128)S(1)} collective-permute-done((f32[2,1,128]{2,0,1:T(2,128)S(1)}, f32[2,1,128]{2,0,1:T(2,128)S(1)}, u32[]{:S(2)}, u32[]{:S(2)}) %collective-permute-start.5) | collective-permute-done | bytes 1056 | tf_op jit(solution)/shard_map/ppermute | solution.py:33
  131.2 7.7 %collective-permute-start.7 = (f32[1,32,1,128]{3,1,2,0:T(8,128)S(1)}, f32[1,32,1,128]{3,1,2,0:T(8,128)S(1)}, u32[]{:S(2)}, u32[]{:S(2)}) collective-permute-start(f32[1,32,1,128]{3,1,2,0:T(8,128)S(1)} %bitcast.212), channel_id=1, source_target_pairs={{32,0},{64,32},{96,64},{128,96},{160,128},{192,160},{224,192},{256... | collective-permute-start | bytes 49160 | tf_op jit(solution)/shard_map/ppermute | solution.py:23
  144.8 51.1 %while.49 = (s32[]{:T(128)}, f32[32,128]{1,0:T(8,128)S(1)}, f32[8,32,128]{2,1,0:T(8,128)S(1)}, f32[1,1,32,3,128]{4,3,2,1,0:T(4,128)S(1)}, f32[8,32,6,128]{3,1,2,...) while((s32[]{:T(128)}, f32[32,128]{1,0:T(8,128)S(1)}, ...), condition=%wide.region_9.10_spmd.clone, body=%wide.region_5.9_spmd.clone.sunk | while | flops 22593544 | bytes 5063245 | solution.py:218
  196.2 7.5 %collective-permute-start.10 = (f32[34,1,128]{2,0,1:T(8,128)S(1)}, f32[34,1,128]{2,0,1:T(8,128)S(1)}, u32[]{:S(2)}, u32[]{:S(2)}) collective-permute-start(f32[34,1,128]{2,0,1:T(8,128)S(1)} %get-tuple-element.771), channel_id=1, source_target_pairs={{0,32},{32,64},{64,96},{96,128},{128,160},{160,192},{192,224},{224... | collective-permute-start | bytes 52232 | tf_op jit(solution)/shard_map/ppermute | solution.py:39
  206.9 6.5 %collective-permute-done.9 = f32[34,1,128]{2,0,1:T(8,128)S(1)} collective-permute-done((f32[34,1,128]{2,0,1:T(8,128)S(1)}, f32[34,1,128]{2,0,1:T(8,128)S(1)}, u32[]{:S(2)}, u32[]{:S(2)}) %collective-permute-start.9) | collective-permute-done | bytes 17440 | tf_op jit(solution)/shard_map/ppermute | solution.py:39
  215.3 6.9 %collective-permute-done.11 = f32[2,1,128]{2,0,1:T(2,128)S(1)} collective-permute-done((f32[2,1,128]{2,0,1:T(2,128)S(1)}, f32[2,1,128]{2,0,1:T(2,128)S(1)}, u32[]{:S(2)}, u32[]{:S(2)}) %collective-permute-start.11) | collective-permute-done | bytes 1056 | tf_op jit(solution)/shard_map/ppermute | solution.py:33
  241.2 213.4 %while.50 = (s32[]{:T(128)}, f32[32,3,128]{2,1,0:T(4,128)S(1)}, f32[8,32,3,128]{3,2,1,0:T(4,128)}, f32[1,1,32,3,128]{4,3,2,1,0:T(4,128)S(1)}, f32[8,32,6,128]{3,...) while((s32[]{:T(128)}, f32[32,3,128]{2,1,0:T(4,128)S(1)}, ...), condition=%wide.region_14.15_spmd.clone, body=%wide.region_10.14_spmd.clone.sunk | while | flops 131686408 | bytes 11011253 | solution.py:218
  244.0 19.3 %fusion.117 = f32[32,128,128]{2,1,0:T(8,128)S(1)} fusion(f32[32,128,128]{2,1,0:T(8,128)S(1)} %fusion.115, f32[32,128]{1,0:T(8,128)S(1)} %get-tuple-element.1112, f32[32,128]{1,0:T(8,128)S(1)} %get-tuple-element.982, f32[32,128]{1,0:T(8,128)S(1)} %get-tuple-element.983, f32[32,128]{1,0:T(8,128)S(1)} %get-tuple-element.984, ...), kind=kLoop, calls=%fused_computation.67.clone.1 | loop fusion | flops 119537664 | bytes 4489348 | tf_op jit(solution)/shard_map/while/body/eval_jaxpr/transpose(jvp())/add_any | solution.py:125
  270.7 19.3 %fusion.117 = f32[32,128,128]{2,1,0:T(8,128)S(1)} fusion(f32[32,128,128]{2,1,0:T(8,128)S(1)} %fusion.115, f32[32,128]{1,0:T(8,128)S(1)} %get-tuple-element.1112, f32[32,128]{1,0:T(8,128)S(1)} %get-tuple-element.982, f32[32,128]{1,0:T(8,128)S(1)} %get-tuple-element.983, f32[32,128]{1,0:T(8,128)S(1)} %get-tuple-element.984, ...), kind=kLoop, calls=%fused_computation.67.clone.1 | loop fusion | flops 119537664 | bytes 4489348 | tf_op jit(solution)/shard_map/while/body/eval_jaxpr/transpose(jvp())/add_any | solution.py:125
  297.3 19.3 %fusion.117 = f32[32,128,128]{2,1,0:T(8,128)S(1)} fusion(f32[32,128,128]{2,1,0:T(8,128)S(1)} %fusion.115, f32[32,128]{1,0:T(8,128)S(1)} %get-tuple-element.1112, f32[32,128]{1,0:T(8,128)S(1)} %get-tuple-element.982, f32[32,128]{1,0:T(8,128)S(1)} %get-tuple-element.983, f32[32,128]{1,0:T(8,128)S(1)} %get-tuple-element.984, ...), kind=kLoop, calls=%fused_computation.67.clone.1 | loop fusion | flops 119537664 | bytes 4489348 | tf_op jit(solution)/shard_map/while/body/eval_jaxpr/transpose(jvp())/add_any | solution.py:125
  324.0 19.3 %fusion.117 = f32[32,128,128]{2,1,0:T(8,128)S(1)} fusion(f32[32,128,128]{2,1,0:T(8,128)S(1)} %fusion.115, f32[32,128]{1,0:T(8,128)S(1)} %get-tuple-element.1112, f32[32,128]{1,0:T(8,128)S(1)} %get-tuple-element.982, f32[32,128]{1,0:T(8,128)S(1)} %get-tuple-element.983, f32[32,128]{1,0:T(8,128)S(1)} %get-tuple-element.984, ...), kind=kLoop, calls=%fused_computation.67.clone.1 | loop fusion | flops 119537664 | bytes 4489348 | tf_op jit(solution)/shard_map/while/body/eval_jaxpr/transpose(jvp())/add_any | solution.py:125
  350.7 19.3 %fusion.117 = f32[32,128,128]{2,1,0:T(8,128)S(1)} fusion(f32[32,128,128]{2,1,0:T(8,128)S(1)} %fusion.115, f32[32,128]{1,0:T(8,128)S(1)} %get-tuple-element.1112, f32[32,128]{1,0:T(8,128)S(1)} %get-tuple-element.982, f32[32,128]{1,0:T(8,128)S(1)} %get-tuple-element.983, f32[32,128]{1,0:T(8,128)S(1)} %get-tuple-element.984, ...), kind=kLoop, calls=%fused_computation.67.clone.1 | loop fusion | flops 119537664 | bytes 4489348 | tf_op jit(solution)/shard_map/while/body/eval_jaxpr/transpose(jvp())/add_any | solution.py:125
  377.4 19.3 %fusion.117 = f32[32,128,128]{2,1,0:T(8,128)S(1)} fusion(f32[32,128,128]{2,1,0:T(8,128)S(1)} %fusion.115, f32[32,128]{1,0:T(8,128)S(1)} %get-tuple-element.1112, f32[32,128]{1,0:T(8,128)S(1)} %get-tuple-element.982, f32[32,128]{1,0:T(8,128)S(1)} %get-tuple-element.983, f32[32,128]{1,0:T(8,128)S(1)} %get-tuple-element.984, ...), kind=kLoop, calls=%fused_computation.67.clone.1 | loop fusion | flops 119537664 | bytes 4489348 | tf_op jit(solution)/shard_map/while/body/eval_jaxpr/transpose(jvp())/add_any | solution.py:125
  404.0 19.3 %fusion.117 = f32[32,128,128]{2,1,0:T(8,128)S(1)} fusion(f32[32,128,128]{2,1,0:T(8,128)S(1)} %fusion.115, f32[32,128]{1,0:T(8,128)S(1)} %get-tuple-element.1112, f32[32,128]{1,0:T(8,128)S(1)} %get-tuple-element.982, f32[32,128]{1,0:T(8,128)S(1)} %get-tuple-element.983, f32[32,128]{1,0:T(8,128)S(1)} %get-tuple-element.984, ...), kind=kLoop, calls=%fused_computation.67.clone.1 | loop fusion | flops 119537664 | bytes 4489348 | tf_op jit(solution)/shard_map/while/body/eval_jaxpr/transpose(jvp())/add_any | solution.py:125
  430.7 19.3 %fusion.117 = f32[32,128,128]{2,1,0:T(8,128)S(1)} fusion(f32[32,128,128]{2,1,0:T(8,128)S(1)} %fusion.115, f32[32,128]{1,0:T(8,128)S(1)} %get-tuple-element.1112, f32[32,128]{1,0:T(8,128)S(1)} %get-tuple-element.982, f32[32,128]{1,0:T(8,128)S(1)} %get-tuple-element.983, f32[32,128]{1,0:T(8,128)S(1)} %get-tuple-element.984, ...), kind=kLoop, calls=%fused_computation.67.clone.1 | loop fusion | flops 119537664 | bytes 4489348 | tf_op jit(solution)/shard_map/while/body/eval_jaxpr/transpose(jvp())/add_any | solution.py:125
  456.1 6.7 %collective-permute-start.15 = (f32[34,3,128]{2,1,0:T(4,128)S(1)}, f32[34,3,128]{2,1,0:T(4,128)S(1)}, u32[]{:S(2)}, u32[]{:S(2)}) collective-permute-start(f32[34,3,128]{2,1,0:T(4,128)S(1)} %squeeze.117), channel_id=1, source_target_pairs={{32,0},{64,32},{96,64},{128,96},{160,128},{192,160},{224,192},{256... | collective-permute-start | bytes 156680 | tf_op jit(solution)/shard_map/ppermute | solution.py:39
  475.8 6.9 %collective-permute-done.17 = f32[2,3,128]{2,1,0:T(4,128)S(1)} collective-permute-done((f32[2,3,128]{2,1,0:T(4,128)S(1)}, f32[2,3,128]{2,1,0:T(4,128)S(1)}, u32[]{:S(2)}, u32[]{:S(2)}) %collective-permute-start.17) | collective-permute-done | bytes 3104 | tf_op jit(solution)/shard_map/ppermute | solution.py:33
  (395 shorter events, 232.6 us)
Async XLA Ops:
  2.9 17.1 %collective-permute-start = (f32[1,32,6,128]{3,1,2,0:T(8,128)S(1)}, f32[1,32,6,128]{3,1,2,0:T(8,128)S(1)}, u32[]{:S(2)}, u32[]{:S(2)}) collective-permute-start(f32[1,32,6,128]{3,1,2,0:T(8,128)S(1)} %maximum_bitcast_fusion), channel_id=1, source_target_pairs={{0,32},{32,64},{64,96},{96,128},{128,160},{160,192},{192,224},{224... | collective-permute-start | bytes 294920 | tf_op jit(solution)/shard_map/ppermute | solution.py:21
  12.0 18.0 %collective-permute-start.1 = (f32[1,32,6,128]{3,1,2,0:T(8,128)S(1)}, f32[1,32,6,128]{3,1,2,0:T(8,128)S(1)}, u32[]{:S(2)}, u32[]{:S(2)}) collective-permute-start(f32[1,32,6,128]{3,1,2,0:T(8,128)S(1)} %maximum_bitcast_fusion), channel_id=1, source_target_pairs={{32,0},{64,32},{96,64},{128,96},{160,128},{192,160},{224,192},{256... | collective-permute-start | bytes 294920 | tf_op jit(solution)/shard_map/ppermute | solution.py:23
  30.0 3.4 collective-permute-start.2
  34.7 93.5 %copy-start.2 = (f32[1,1,32,128]{3,2,1,0:T(8,128)S(1)}, f32[1,1,32,128]{3,2,1,0:T(8,128)}, u32[]{:S(2)}) copy-start(f32[1,1,32,128]{3,2,1,0:T(8,128)} %param.14) | copy-start | bytes 49156
  34.7 110.0 %copy-start.1 = (f32[1,1,32,128]{3,2,1,0:T(8,128)S(1)}, f32[1,1,32,128]{3,2,1,0:T(8,128)}, u32[]{:S(2)}) copy-start(f32[1,1,32,128]{3,2,1,0:T(8,128)} %param.13) | copy-start | bytes 49156
  103.1 10.0 %collective-permute-start.3 = (f32[34,1,128]{2,0,1:T(8,128)S(1)}, f32[34,1,128]{2,0,1:T(8,128)S(1)}, u32[]{:S(2)}, u32[]{:S(2)}) collective-permute-start(f32[34,1,128]{2,0,1:T(8,128)S(1)} %get-tuple-element.772), channel_id=1, source_target_pairs={{32,0},{64,32},{96,64},{128,96},{160,128},{192,160},{224,192},{256... | collective-permute-start | bytes 52232 | tf_op jit(solution)/shard_map/ppermute | solution.py:39
  108.8 10.7 %collective-permute-start.4 = (f32[34,1,128]{2,0,1:T(8,128)S(1)}, f32[34,1,128]{2,0,1:T(8,128)S(1)}, u32[]{:S(2)}, u32[]{:S(2)}) collective-permute-start(f32[34,1,128]{2,0,1:T(8,128)S(1)} %get-tuple-element.773), channel_id=1, source_target_pairs={{0,32},{32,64},{64,96},{96,128},{128,160},{160,192},{192,224},{224... | collective-permute-start | bytes 52232 | tf_op jit(solution)/shard_map/ppermute | solution.py:39
  119.5 8.8 %collective-permute-start.5 = (f32[2,1,128]{2,0,1:T(2,128)S(1)}, f32[2,1,128]{2,0,1:T(2,128)S(1)}, u32[]{:S(2)}, u32[]{:S(2)}) collective-permute-start(f32[2,1,128]{2,0,1:T(2,128)S(1)} %slice.184), channel_id=1, source_target_pairs={{31,0},{0,1},{1,2},{2,3},{3,4},{4,5},{5,6},{6,7},{7,8},{8,9},{9,10... | collective-permute-start | bytes 3080 | tf_op jit(solution)/shard_map/ppermute | solution.py:33
  128.3 10.7 %collective-permute-start.6 = (f32[1,32,1,128]{3,1,2,0:T(8,128)S(1)}, f32[1,32,1,128]{3,1,2,0:T(8,128)S(1)}, u32[]{:S(2)}, u32[]{:S(2)}) collective-permute-start(f32[1,32,1,128]{3,1,2,0:T(8,128)S(1)} %bitcast.211), channel_id=1, source_target_pairs={{0,32},{32,64},{64,96},{96,128},{128,160},{160,192},{192,224},{224... | collective-permute-start | bytes 49160 | tf_op jit(solution)/shard_map/ppermute | solution.py:21
  131.2 9.5 %collective-permute-start.7 = (f32[1,32,1,128]{3,1,2,0:T(8,128)S(1)}, f32[1,32,1,128]{3,1,2,0:T(8,128)S(1)}, u32[]{:S(2)}, u32[]{:S(2)}) collective-permute-start(f32[1,32,1,128]{3,1,2,0:T(8,128)S(1)} %bitcast.212), channel_id=1, source_target_pairs={{32,0},{64,32},{96,64},{128,96},{160,128},{192,160},{224,192},{256... | collective-permute-start | bytes 49160 | tf_op jit(solution)/shard_map/ppermute | solution.py:23
  140.8 3.2 collective-permute-start.8
  196.2 10.7 %collective-permute-start.10 = (f32[34,1,128]{2,0,1:T(8,128)S(1)}, f32[34,1,128]{2,0,1:T(8,128)S(1)}, u32[]{:S(2)}, u32[]{:S(2)}) collective-permute-start(f32[34,1,128]{2,0,1:T(8,128)S(1)} %get-tuple-element.771), channel_id=1, source_target_pairs={{0,32},{32,64},{64,96},{96,128},{128,160},{160,192},{192,224},{224... | collective-permute-start | bytes 52232 | tf_op jit(solution)/shard_map/ppermute | solution.py:39
  203.7 9.6 %collective-permute-start.9 = (f32[34,1,128]{2,0,1:T(8,128)S(1)}, f32[34,1,128]{2,0,1:T(8,128)S(1)}, u32[]{:S(2)}, u32[]{:S(2)}) collective-permute-start(f32[34,1,128]{2,0,1:T(8,128)S(1)} %get-tuple-element.770), channel_id=1, source_target_pairs={{32,0},{64,32},{96,64},{128,96},{160,128},{192,160},{224,192},{256... | collective-permute-start | bytes 52232 | tf_op jit(solution)/shard_map/ppermute | solution.py:39
  213.4 8.8 %collective-permute-start.11 = (f32[2,1,128]{2,0,1:T(2,128)S(1)}, f32[2,1,128]{2,0,1:T(2,128)S(1)}, u32[]{:S(2)}, u32[]{:S(2)}) collective-permute-start(f32[2,1,128]{2,0,1:T(2,128)S(1)} %slice.190), channel_id=1, source_target_pairs={{31,0},{0,1},{1,2},{2,3},{3,4},{4,5},{5,6},{6,7},{7,8},{8,9},{9,10... | collective-permute-start | bytes 3080 | tf_op jit(solution)/shard_map/ppermute | solution.py:33
  222.8 10.7 %collective-permute-start.12 = (f32[1,32,1,128]{3,1,2,0:T(8,128)S(1)}, f32[1,32,1,128]{3,1,2,0:T(8,128)S(1)}, u32[]{:S(2)}, u32[]{:S(2)}) collective-permute-start(f32[1,32,1,128]{3,1,2,0:T(8,128)S(1)} %bitcast.216), channel_id=1, source_target_pairs={{0,32},{32,64},{64,96},{96,128},{128,160},{160,192},{192,224},{224... | collective-permute-start | bytes 49160 | tf_op jit(solution)/shard_map/ppermute | solution.py:21
  227.7 9.5 %collective-permute-start.13 = (f32[1,32,1,128]{3,1,2,0:T(8,128)S(1)}, f32[1,32,1,128]{3,1,2,0:T(8,128)S(1)}, u32[]{:S(2)}, u32[]{:S(2)}) collective-permute-start(f32[1,32,1,128]{3,1,2,0:T(8,128)S(1)} %bitcast.217), channel_id=1, source_target_pairs={{32,0},{64,32},{96,64},{128,96},{160,128},{192,160},{224,192},{256... | collective-permute-start | bytes 49160 | tf_op jit(solution)/shard_map/ppermute | solution.py:23
  237.2 3.2 collective-permute-start.14
  316.6 4.6 copy-start.4
  343.3 4.6 copy-start.4
  396.6 4.6 copy-start.4
  454.6 28.8 %copy-start = (f32[32,128]{1,0:T(8,128)}, f32[32,128]{1,0:T(8,128)S(1)}, u32[]{:S(2)}) copy-start(f32[32,128]{1,0:T(8,128)S(1)} %get-tuple-element.1128) | copy-start | bytes 49156
  456.1 11.8 %collective-permute-start.15 = (f32[34,3,128]{2,1,0:T(4,128)S(1)}, f32[34,3,128]{2,1,0:T(4,128)S(1)}, u32[]{:S(2)}, u32[]{:S(2)}) collective-permute-start(f32[34,3,128]{2,1,0:T(4,128)S(1)} %squeeze.117), channel_id=1, source_target_pairs={{32,0},{64,32},{96,64},{128,96},{160,128},{192,160},{224,192},{256... | collective-permute-start | bytes 156680 | tf_op jit(solution)/shard_map/ppermute | solution.py:39
  462.8 11.1 %collective-permute-start.16 = (f32[34,3,128]{2,1,0:T(4,128)S(1)}, f32[34,3,128]{2,1,0:T(4,128)S(1)}, u32[]{:S(2)}, u32[]{:S(2)}) collective-permute-start(f32[34,3,128]{2,1,0:T(4,128)S(1)} %squeeze.118), channel_id=1, source_target_pairs={{0,32},{32,64},{64,96},{96,128},{128,160},{160,192},{192,224},{224... | collective-permute-start | bytes 156680 | tf_op jit(solution)/shard_map/ppermute | solution.py:39
  473.9 8.8 %collective-permute-start.17 = (f32[2,3,128]{2,1,0:T(4,128)S(1)}, f32[2,3,128]{2,1,0:T(4,128)S(1)}, u32[]{:S(2)}, u32[]{:S(2)}) collective-permute-start(f32[2,3,128]{2,1,0:T(4,128)S(1)} %slice.196), channel_id=1, source_target_pairs={{31,0},{0,1},{1,2},{2,3},{3,4},{4,5},{5,6},{6,7},{7,8},{8,9},{9,10... | collective-permute-start | bytes 9224 | tf_op jit(solution)/shard_map/ppermute | solution.py:33
  (13 other events, 28.0 us)
where the time goes:
time: 485 us; the launch traced here: 483 us
  other arithmetic  323 us (67%)
  starting transfers between devices  78.4 us (16%)
  waiting for transfers between devices  59.7 us (12%)
  local copies, waits for them, and re-layouts  15.8 us (3%)
    add_any x8, other arithmetic, total_energy(): distance = jnp.sqrt(squared)  154 us
    reduce_sum x8, other arithmetic, born_pair(): jnp.sum(weight * descreen(distance, data_two[..., 4, None, :], data_one[....  49.7 us
    reduce_sum x24, other arithmetic, gap_squared(): squared = jnp.sum(differ * differ, axis=-3)  49.4 us
    reduce_sum x8, other arithmetic, screened(): product = radius_one[..., :, None] * radius_two[..., None, :]  32.8 us
    reduce_sum x8, other arithmetic, gap_squared(): differ = coords_one[..., :, :, None] - coords_two[..., :, None, :]  31 us
    ppermute x6, starting transfers between devices, shifted_2(): return lax.ppermute(array, axis, pairs)  30.1 us
    ppermute x6, waiting for transfers between devices, shifted(): return lax.ppermute(block, axis, route)  23 us
    ppermute x6, waiting for transfers between devices, shifted_2(): return lax.ppermute(array, axis, pairs)  21.1 us
  transfers between devices with their start and end apart: 18, of which 14 were waited for; matrix products, arithmetic and copies ran while one was open for 1% of the time, Pallas kernels for 0%

commit v1 on v0

v1 whole, which is shorter than its diff:
```python
import functools
import math

import jax
import jax.numpy as jnp
from jax import lax
from jax.experimental import pallas as pl
from jax.experimental.pallas import tpu as pltpu
from jax.sharding import PartitionSpec as P

radius_offset = 0.09
obc_alpha = 1.0
obc_beta = 0.8
obc_gamma = 4.85
cutoff_len = 14.0
cutoff_sq = cutoff_len * cutoff_len

TILES = 32
EDGE = 2
HALF = TILES + EDGE
REGION = 2 * HALF
GROUPS = 2 * TILES
LISTED = 7
ATOMS = 128
RING = 16
LANES = (8, ATOMS)
VMEM_LIMIT = 40 * 1024 * 1024
EXP_SCALE = math.sqrt(0.25 / math.log(2.0))

ROW_X, ROW_Y, ROW_Z, ROW_Q, ROW_IN, ROW_SCALED, ROW_RADIUS, ROW_CODE = range(8)


def row_of(ref, tile, row):
    return jnp.broadcast_to(ref[tile, row : row + 1, :], LANES)


def fill_table(table, first, block, rows):
    columns = block.T
    for slot, row in enumerate(rows):
        table[first + slot] = jnp.broadcast_to(columns[:, row : row + 1], (ATOMS, ATOMS))


def fold_own(own):
    flipped = own.T
    total = flipped[0:8]
    for chunk in range(1, ATOMS // 8):
        total = total + flipped[8 * chunk : 8 * chunk + 8]
    return total


def group_row(group):
    return jnp.where(group < TILES, group, group + EDGE)


def chunk_loop(step, carry, unroll):
    return lax.fori_loop(0, ATOMS // 8, lambda c, s: step(pl.multiple_of(c * 8, 8), s), carry, unroll=unroll)


def diagonal(start):
    rows = lax.broadcasted_iota(jnp.int32, LANES, 0) + start
    lanes = lax.broadcasted_iota(jnp.int32, LANES, 1)
    return jnp.where(rows == lanes, 4.0 * cutoff_sq, 0.0)


def half_descreen(r, own, far):
    upper = r + far
    lower = r - far
    inner = jnp.minimum(jnp.maximum(own, lower), upper)
    ratio = upper * pl.reciprocal(inner, approx=True)
    slope = lower * pl.reciprocal(upper, approx=True)
    rise = ratio - 1.0
    log2x = jnp.log(ratio) * 2.0
    value = rise * (2.0 - slope * rise) - log2x
    deriv = (log2x + log2x) - (ratio * ratio - 1.0) * (slope * slope + 1.0)
    return value, deriv


def pair_shared(r2):
    inv = lax.rsqrt(r2)
    r = r2 * inv
    cut = jnp.maximum(1.0 - r2 * (1.0 / cutoff_sq), 0.0)
    cinv = cut * inv
    weight = cut * cinv
    g_deriv = cinv * cinv * inv
    g_value = cinv * (8.0 / cutoff_sq)
    return r, weight, g_deriv, g_value


def born_kernel(unroll, count, place, data, part, d_self, d_pair, table, own, far, ring, s_ring, sems, s_sems):
    far[...] = jnp.zeros_like(far)

    def separation(start, bx, by, bz):
        rows = pl.ds(start, 8)
        dx = table[0, rows, :] - bx
        dy = table[1, rows, :] - by
        dz = table[2, rows, :] - bz
        return dx * dx + dy * dy + dz * dz

    def group_step(group, done):
        tile = group_row(group)
        fill_table(table, 0, data[tile], (ROW_X, ROW_Y, ROW_Z, ROW_IN, ROW_SCALED))
        own[...] = jnp.zeros_like(own)

        @pl.when(group < TILES)
        def _():
            slot = lax.rem(group, 2)
            copy = pltpu.make_async_copy(s_ring.at[slot], d_self.at[group], s_sems.at[slot])

            @pl.when(group >= 2)
            def _():
                copy.wait()

            bx, by, bz, bs = (row_of(data, tile, row) for row in (ROW_X, ROW_Y, ROW_Z, ROW_SCALED))

            def step(start, carry):
                rows = pl.ds(start, 8)
                r2 = separation(start, bx, by, bz) + diagonal(start)
                r, weight, g_deriv, g_value = pair_shared(r2)
                value, deriv = half_descreen(r, table[3, rows, :], bs)
                own[rows, :] = weight * value
                s_ring[slot, rows, :] = g_deriv * deriv - g_value * value
                return carry

            chunk_loop(step, 0, unroll)
            copy.start()

        number = count[group]

        def pair_step(k, carry):
            index = done + k
            other = place[group, k]
            slot = lax.rem(index, RING)
            copy = pltpu.make_async_copy(ring.at[slot], d_pair.at[index], sems.at[slot])

            @pl.when(index >= RING)
            def _():
                copy.wait()

            bx, by, bz, bp, bs = (
                row_of(data, other, row) for row in (ROW_X, ROW_Y, ROW_Z, ROW_IN, ROW_SCALED)
            )

            def step(start, total):
                rows = pl.ds(start, 8)
                r2 = separation(start, bx, by, bz)
                r, weight, g_deriv, g_value = pair_shared(r2)
                value, deriv = half_descreen(r, table[3, rows, :], bs)
                own[rows, :] += weight * value
                ring[slot, 0, rows, :] = g_deriv * deriv - g_value * value
                value, deriv = half_descreen(r, bp, table[4, rows, :])
                ring[slot, 1, rows, :] = g_deriv * deriv - g_value * value
                return total + weight * value

            total = chunk_loop(step, jnp.zeros(LANES, jnp.float32), unroll)
            far[other] += total
            copy.start()
            return carry

        lax.fori_loop(0, number, pair_step, 0)
        far[tile] += fold_own(own[...])
        return done + number

    done = lax.fori_loop(0, GROUPS, group_step, 0)
    part[...] = jnp.sum(far[...], axis=1) * 0.125
    for slot in range(2):
        pltpu.make_async_copy(s_ring.at[slot], d_self.at[slot], s_sems.at[slot]).wait()
    for slot in range(RING):

        @pl.when(slot < done)
        def _():
            pltpu.make_async_copy(ring.at[slot], d_pair.at[slot], sems.at[slot]).wait()


def energy_kernel(unroll, count, place, data, born, part, force, table, own, far):
    far[...] = jnp.zeros_like(far)
    force[...] = jnp.zeros_like(force)

    def group_step(group, carry):
        tile = group_row(group)
        fill_table(table, 0, data[tile], (ROW_X, ROW_Y, ROW_Z, ROW_Q))
        fill_table(table, 4, born[tile], (0, 1))
        own[...] = jnp.zeros_like(own)

        def pair_block(other, is_self):
            bx, by, bz, bq = (row_of(data, other, row) for row in (ROW_X, ROW_Y, ROW_Z, ROW_Q))
            br, bi = row_of(born, other, 0), -row_of(born, other, 1)

            def step(start, totals):
                rows = pl.ds(start, 8)
                dx = table[0, rows, :] - bx
                dy = table[1, rows, :] - by
                dz = table[2, rows, :] - bz
                r2 = dx * dx + dy * dy + dz * dz
                if is_self:
                    r2 = r2 + diagonal(start)
                cut = jnp.maximum(1.0 - r2 * (1.0 / cutoff_sq), 0.0)
                power = r2 * (table[5, rows, :] * bi)
                decay = lax.exp2(power)
                screen = (table[4, rows, :] * br) * decay
                inv = lax.rsqrt(r2 + screen)
                lead = (cut * (table[3, rows, :] * bq)) * inv
                square = cut * (inv * inv)
                grad = (lead * square) * (screen * (1.0 - math.log(2.0) * power))
                pull = lead * (square * (4.0 - decay) + 16.0 / cutoff_sq)
                fx, fy, fz = pull * dx, pull * dy, pull * dz
                own[0, rows, :] += grad
                own[1, rows, :] += fx
                own[2, rows, :] += fy
                own[3, rows, :] += fz
                if is_self:
                    return totals
                t0, t1, t2, t3 = totals
                return (t0 + grad, t1 + fx, t2 + fy, t3 + fz)

            zero = jnp.zeros(LANES, jnp.float32)
            totals = chunk_loop(step, 0 if is_self else (zero,) * 4, unroll)
            if not is_self:
                far[other] += totals[0]
                for axis in range(3):
                    force[other, axis] -= totals[1 + axis]

        @pl.when(group < TILES)
        def _():
            pair_block(tile, True)

        def pair_step(k, c):
            pair_block(place[group, k], False)
            return c

        lax.fori_loop(0, count[group], pair_step, 0)
        far[tile] += fold_own(own[0])
        for axis in range(3):
            force[tile, axis] += fold_own(own[1 + axis])
        return carry

    lax.fori_loop(0, GROUPS, group_step, 0)
    part[...] = jnp.sum(far[...], axis=1) * 0.5


def force_kernel(unroll, count, place, data, chain, force_in, d_self, d_pair, force, table, own, far, ring, s_ring, sems, s_sems):
    far[...] = force_in[...] * 4.0

    def total_pairs(group, total):
        return total + count[group]

    pairs = lax.fori_loop(0, GROUPS, total_pairs, 0)

    def fetch(index):
        slot = lax.rem(index, RING)
        return pltpu.make_async_copy(d_pair.at[index], ring.at[slot], sems.at[slot])

    def fetch_self(index):
        slot = lax.rem(index, 2)
        return pltpu.make_async_copy(d_self.at[index], s_ring.at[slot], s_sems.at[slot])

    fetch_self(0).start()
    fetch_self(1).start()
    for index in range(RING):

        @pl.when(index < pairs)
        def _():
            fetch(index).start()

    def group_step(group, done):
        tile = group_row(group)
        fill_table(table, 0, data[tile], (ROW_X, ROW_Y, ROW_Z))
        fill_table(table, 3, chain[tile], (0,))
        own[...] = jnp.zeros_like(own)

        def pair_block(other, coefficient):
            bx, by, bz = (row_of(data, other, row) for row in (ROW_X, ROW_Y, ROW_Z))

            def step(start, totals):
                rows = pl.ds(start, 8)
                pull = coefficient(rows)
                fx = pull * (table[0, rows, :] - bx)
                fy = pull * (table[1, rows, :] - by)
                fz = pull * (table[2, rows, :] - bz)
                own[0, rows, :] += fx
                own[1, rows, :] += fy
                own[2, rows, :] += fz
                t0, t1, t2 = totals
                return (t0 + fx, t1 + fy, t2 + fz)

            zero = jnp.zeros(LANES, jnp.float32)
            totals = chunk_loop(step, (zero,) * 3, unroll)
            for axis in range(3):
                far[other, axis] -= totals[axis]

        @pl.when(group < TILES)
        def _():
            fetch_self(group).wait()
            slot = lax.rem(group, 2)
            pair_block(tile, lambda rows: table[3, rows, :] * s_ring[slot, rows, :])

            @pl.when(group < TILES - 2)
            def _():
                fetch_self(group + 2).start()

        number = count[group]

        def pair_step(k, carry):
            index = done + k
            other = place[group, k]
            slot = lax.rem(index, RING)
            fetch(index).wait()
            chain_b = row_of(chain, other, 0)
            pair_block(
                other,
                lambda rows: table[3, rows, :] * ring[slot, 0, rows, :] + chain_b * ring[slot, 1, rows, :],
            )

            @pl.when(index + RING < pairs)
            def _():
                fetch(index + RING).start()

            return carry

        lax.fori_loop(0, number, pair_step, 0)
        for axis in range(3):
            far[tile, axis] += fold_own(own[axis])
        return done + number

    lax.fori_loop(0, GROUPS, group_step, 0)
    force[...] = jnp.sum(far[...], axis=2) * (-1.0 / 16.0)


SMEM = pl.BlockSpec(memory_space=pltpu.SMEM)
VMEM = pl.BlockSpec(memory_space=pltpu.VMEM)
ANY = pl.BlockSpec(memory_space=pl.ANY)
PARAMS = pltpu.CompilerParams(vmem_limit_bytes=VMEM_LIMIT)
BLOCK = (ATOMS, ATOMS)


def f32(*shape):
    return jax.ShapeDtypeStruct(shape, jnp.float32)


def run_born(count, place, data, unroll=4):
    return pl.pallas_call(
        functools.partial(born_kernel, unroll),
        name="born_sums",
        out_shape=(
            f32(REGION, ATOMS),
            f32(TILES, *BLOCK),
            f32(GROUPS * LISTED, 2, *BLOCK),
        ),
        in_specs=[SMEM, SMEM, VMEM],
        out_specs=(VMEM, ANY, ANY),
        scratch_shapes=[
            pltpu.VMEM((5,) + BLOCK, jnp.float32),
            pltpu.VMEM(BLOCK, jnp.float32),
            pltpu.VMEM((REGION,) + LANES, jnp.float32),
            pltpu.VMEM((RING, 2) + BLOCK, jnp.float32),
            pltpu.VMEM((2,) + BLOCK, jnp.float32),
            pltpu.SemaphoreType.DMA((RING,)),
            pltpu.SemaphoreType.DMA((2,)),
        ],
        compiler_params=PARAMS,
    )(count, place, data)


def run_energy(count, place, data, born, unroll=4):
    return pl.pallas_call(
        functools.partial(energy_kernel, unroll),
        name="radius_gradient",
        out_shape=(f32(REGION, ATOMS), f32(REGION, 3, *LANES)),
        in_specs=[SMEM, SMEM, VMEM, VMEM],
        out_specs=(VMEM, VMEM),
        scratch_shapes=[
            pltpu.VMEM((6,) + BLOCK, jnp.float32),
            pltpu.VMEM((4,) + BLOCK, jnp.float32),
            pltpu.VMEM((REGION,) + LANES, jnp.float32),
        ],
        compiler_params=PARAMS,
    )(count, place, data, born)


def run_force(count, place, data, chain, force_in, d_self, d_pair, unroll=4):
    return pl.pallas_call(
        functools.partial(force_kernel, unroll),
        name="forces",
        out_shape=f32(REGION, 3, ATOMS),
        in_specs=[SMEM, SMEM, VMEM, VMEM, VMEM, ANY, ANY],
        out_specs=VMEM,
        scratch_shapes=[
            pltpu.VMEM((4,) + BLOCK, jnp.float32),
            pltpu.VMEM((3,) + BLOCK, jnp.float32),
            pltpu.VMEM((REGION, 3) + LANES, jnp.float32),
            pltpu.VMEM((RING, 2) + BLOCK, jnp.float32),
            pltpu.VMEM((2,) + BLOCK, jnp.float32),
            pltpu.SemaphoreType.DMA((RING,)),
            pltpu.SemaphoreType.DMA((2,)),
        ],
        compiler_params=PARAMS,
    )(count, place, data, chain, force_in, d_self, d_pair)


def born_radius(descreen_sum, radius, radius_in):
    scaled = radius_in * descreen_sum
    polynomial = scaled * (obc_alpha + scaled * (-obc_beta + obc_gamma * scaled))
    tangent = jnp.tanh(polynomial)
    radii_born = 1.0 / (1.0 / radius_in - tangent / radius)
    radius_slope = (
        radii_born
        * radii_born
        * (1.0 - tangent * tangent)
        / radius
        * (obc_alpha - 2.0 * obc_beta * scaled + 3.0 * obc_gamma * scaled * scaled)
        * radius_in
    )
    return (radii_born, radius_slope)


def above_to_here(block):
    ends = lax.axis_size("slab") - 1
    return lax.ppermute(block, "slab", [(i + 1, i) for i in range(ends)])


def here_to_above(block):
    ends = lax.axis_size("slab") - 1
    return lax.ppermute(block, "slab", [(i, i + 1) for i in range(ends)])


def next_to_here(block):
    count = lax.axis_size("tile")
    return lax.ppermute(block, "tile", [((i + 1) % count, i) for i in range(count)])


def here_to_next(block):
    count = lax.axis_size("tile")
    return lax.ppermute(block, "tile", [(i, (i + 1) % count) for i in range(count)])


def swap_sums(part):
    to_next = jnp.concatenate([part[TILES:HALF], part[HALF + TILES :]])
    to_last = jnp.concatenate([part[0:EDGE], part[HALF : HALF + EDGE]])
    from_last = here_to_next(to_next)
    from_next = next_to_here(to_last)
    column = jnp.concatenate(
        [
            part[0:EDGE] + from_last[0:EDGE],
            part[EDGE:TILES],
            part[TILES:HALF] + from_next[0:EDGE],
            part[HALF : HALF + EDGE] + from_last[EDGE:],
            part[HALF + EDGE : HALF + TILES],
            part[HALF + TILES :] + from_next[EDGE:],
        ]
    )
    own, above = column[0:HALF], column[HALF:]
    from_below = here_to_above(above)
    from_above = above_to_here(own)
    return jnp.concatenate([own + from_below, above + from_above])


def pair_lists(neighbours, pad_mask):
    cycle_count = lax.axis_size("tile")
    cycle_tiles = cycle_count * TILES
    slab_step = neighbours // cycle_tiles - lax.axis_index("slab")
    within = neighbours % cycle_tiles
    cycle_step = (within // TILES - lax.axis_index("tile")) % cycle_count
    place = cycle_step * TILES + within % TILES
    live = (pad_mask == 1) & (jnp.arange(neighbours.shape[1]) > 0)[None, :]
    here = jnp.where(live & (slab_step >= 0), slab_step * HALF + place, -1)
    below = jnp.where(live & (slab_step < 0), place, -1)
    return here, below


def packed(place):
    valid = place >= 0
    slots = jnp.arange(place.shape[1])
    rank = jnp.sum(valid[:, None, :] & (slots[None, None, :] < slots[None, :, None]), axis=2)
    chosen = valid[:, :, None] & (rank[:, :, None] == slots[None, None, :])
    listed = jnp.sum(jnp.where(chosen, place[:, :, None], 0), axis=1)
    return jnp.sum(valid, axis=1).astype(jnp.int32), listed.astype(jnp.int32)


def body(positions, charges, radii, scales, neighbours, pad_mask):
    coords = positions[0, 0]
    charge = charges[0, 0]
    radius = radii[0, 0]
    radius_in = radius - radius_offset
    here, below = pair_lists(neighbours[0, 0], pad_mask[0, 0])
    code = jnp.pad(below.astype(jnp.float32), ((0, 0), (0, ATOMS - below.shape[1])))
    own = jnp.concatenate(
        [coords, jnp.stack([charge, radius_in, scales[0, 0] * radius_in, radius, code], axis=1)], axis=1
    )
    own = jnp.concatenate([own, next_to_here(own[0:EDGE])])
    above = above_to_here(own)
    data = jnp.concatenate([own, above])
    from_above = above[0:TILES, ROW_CODE, 0 : below.shape[1]].astype(jnp.int32)
    has_above = lax.axis_index("slab") < lax.axis_size("slab") - 1
    from_above = jnp.where(has_above, from_above, -1)
    count, place = packed(jnp.concatenate([here, from_above]))

    part, d_self, d_pair = run_born(count, place, data)
    radii_born, radius_slope = born_radius(swap_sums(part), data[:, ROW_RADIUS], data[:, ROW_IN])
    inverse = 1.0 / radii_born
    born = jnp.stack([radii_born, EXP_SCALE * inverse], axis=1)
    part, force = run_energy(count, place, data, born)
    own_charge = data[0:TILES, ROW_Q] * inverse[0:TILES]
    part = part * inverse + jnp.pad(0.5 * own_charge * own_charge, ((0, REGION - TILES), (0, 0)))
    gradient = swap_sums(part)
    chain = (gradient * radius_slope)[:, None]
    force = run_force(count, place, data, chain, force, d_self, d_pair)
    back = here_to_above(force[HALF:])
    mine = force[0:HALF] + back
    last = here_to_next(mine[TILES:])
    forces = jnp.concatenate([mine[0:EDGE] + last, mine[EDGE:TILES]])
    return (radii_born[None, None, 0:TILES], gradient[None, None, 0:TILES], forces[None, None])


def solution(mesh):
    return jax.shard_map(
        body,
        mesh=mesh,
        in_specs=(
            P("slab", "tile", None, None, None),
            P("slab", "tile", None, None),
            P("slab", "tile", None, None),
            P("slab", "tile", None, None),
            P("slab", "tile", None, None),
            P("slab", "tile", None, None),
        ),
        out_specs=(
            P("slab", "tile", None, None),
            P("slab", "tile", None, None),
            P("slab", "tile", None, None, None),
        ),
        check_vma=False,
    )
```

time: 485 us -> 312 us (0.64)
  other arithmetic: 323 us -> 3.24 us
  Pallas kernels: 0 us -> 139 us
  starting transfers between devices: 78.4 us -> 97.3 us
  local copies, waits for them, and re-layouts: 15.8 us -> 4.75 us
    reduce_sum x48 -> x3, other arithmetic: 163 us -> 0.24 us  [the longest x1 0.11 us: packed(): jnp.sum(valid[:, None, :] & (slots[None, None, :] < slots[None, :, None])...]
    add_any x8 -> x0, other arithmetic: 154 us -> none  [total_energy(): distance = jnp.sqrt(squared)]
    pallas_call x0 -> x3, Pallas kernels: none -> 139 us  [the longest x1 57.2 us: run_born(): pl.pallas_call(functools.partial(born_kernel, unroll), name='born_sums',...]
    ppermute x18 -> x12, starting transfers between devices: 78.4 us -> 97.3 us  [the longest x3 39.8 us: above_to_here(): return lax.ppermute(block, 'slab', [(i + 1, i) for i in range(ends)])]
    dynamic_update_slice x16 -> x0, local copies, waits for them, and re-layouts: 5.16 us -> none  [advance(): lax.dynamic_update_index_in_dim(far_all, far_add, slot, 0)]
    ppermute x18 -> x12, waiting for transfers between devices: 59.7 us -> 64 us  [the longest x3 29.4 us: here_to_above(): return lax.ppermute(block, 'slab', [(i, i + 1) for i in range(ends)])]
  transfers between devices with their start and end apart: 18 -> 12, of which waited for: 14 -> 10; matrix products, arithmetic and copies ran while one was open for 1% -> 0% of each run, Pallas kernels for 0% -> 0%
where the time goes in v1:
time: 312 us; the launch traced here: 309 us
  Pallas kernels  139 us (45%)
  starting transfers between devices  97.3 us (31%)
  waiting for transfers between devices  64 us (21%)
  local copies, waits for them, and re-layouts  4.75 us (2%)
  other arithmetic  3.24 us (1%)
    pallas_call x1, Pallas kernels, run_born(): pl.pallas_call(functools.partial(born_kernel, unroll), name='born_sums',...  57.2 us
    pallas_call x1, Pallas kernels, run_energy(): pl.pallas_call(functools.partial(energy_kernel, unroll), name='radius_gra...  45.2 us
    ppermute x3, starting transfers between devices, above_to_here(): return lax.ppermute(block, 'slab', [(i + 1, i) for i in range(ends)])  39.8 us
    pallas_call x1, Pallas kernels, run_force(): pl.pallas_call(functools.partial(force_kernel, unroll), name='forces', ou...  36.2 us
    ppermute x3, starting transfers between devices, next_to_here(): lax.ppermute(block, 'tile', [((i + 1) % count, i) for i in range(count)])  34.4 us
    ppermute x3, waiting for transfers between devices, here_to_above(): return lax.ppermute(block, 'slab', [(i, i + 1) for i in range(ends)])  29.4 us
    ppermute x3, waiting for transfers between devices, here_to_next(): lax.ppermute(block, 'tile', [(i, (i + 1) % count) for i in range(count)])  20.1 us
    ppermute x3, starting transfers between devices, here_to_above(): return lax.ppermute(block, 'slab', [(i, i + 1) for i in range(ends)])  17.4 us
  transfers between devices with their start and end apart: 12, of which 10 were waited for; matrix products, arithmetic and copies ran while one was open for 0% of the time, Pallas kernels for 0%

profile of v1, /device:TPU:24, one launch (start us, length us, event | category | flops | bytes accessed | tf_op | source)
XLA Modules:
  0.0 308.8 jit_solution(8810119485554197538)
XLA Ops:
  4.8 8.2 %collective-permute-start = (f32[2,8,128]{2,1,0:T(8,128)S(1)}, f32[2,8,128]{2,1,0:T(8,128)S(1)}, u32[]{:S(2)}, u32[]{:S(2)}) collective-permute-start(f32[2,8,128]{2,1,0:T(8,128)S(1)} %slice.144), channel_id=1, source_target_pairs={{1,0},{2,1},{3,2},{4,3},{5,4},{6,5},{7,6},{8,7},{9,8},{10,9},{11,1... | collective-permute-start | bytes 24584 | tf_op jit(solution)/shard_map/ppermute | solution.py:427
  14.3 10.2 %collective-permute-start.1 = (f32[34,8,128]{2,1,0:T(8,128)S(1)}, f32[34,8,128]{2,1,0:T(8,128)S(1)}, u32[]{:S(2)}, u32[]{:S(2)}) collective-permute-start(f32[34,8,128]{2,1,0:T(8,128)S(1)} %pad_maximum_fusion.1), channel_id=1, source_target_pairs={{32,0},{64,32},{96,64},{128,96},{160,128},{192,160},{224,192},{256... | collective-permute-start | bytes 417800 | tf_op jit(solution)/shard_map/ppermute | solution.py:417
  24.6 10.1 %collective-permute-done.1 = f32[34,8,128]{2,1,0:T(8,128)S(1)} collective-permute-done((f32[34,8,128]{2,1,0:T(8,128)S(1)}, f32[34,8,128]{2,1,0:T(8,128)S(1)}, u32[]{:S(2)}, u32[]{:S(2)}) %collective-permute-start.1) | collective-permute-done | bytes 139296 | tf_op jit(solution)/shard_map/ppermute | solution.py:417
  35.3 57.2 %born_sums.1 = (f32[68,128]{1,0:T(8,128)S(1)}, f32[32,128,128]{2,1,0:T(8,128)S(1)}, f32[448,2,128,128]{3,2,1,0:T(8,128)}) custom-call(s32[64]{0:T(128)S(1)} %get-tuple-element.27.count, s32[64,8]{1,0:T(8,128)S(1)} %copy.48.place, f32[68,8,128]{2,1,0:T(8,128)S(1)} %pad_maximum_fusion.data), custom_call_target="tpu_custom_call" | custom-call | tf_op jit(solution)/shard_map/born_sums/pallas_call | solution.py:340
  92.5 16.9 %collective-permute-start.3 = (f32[4,128]{1,0:T(4,128)S(1)}, f32[4,128]{1,0:T(4,128)S(1)}, u32[]{:S(2)}, u32[]{:S(2)}) collective-permute-start(f32[4,128]{1,0:T(4,128)S(1)} %pad_maximum_fusion.10), channel_id=1, source_target_pairs={{1,0},{2,1},{3,2},{4,3},{5,4},{6,5},{7,6},{8,7},{9,8},{10,9},{11,1... | collective-permute-start | bytes 6152 | tf_op jit(solution)/shard_map/ppermute | solution.py:427
  109.4 1.9 collective-permute-start.2
  111.3 6.9 %collective-permute-done.2 = f32[4,128]{1,0:T(4,128)S(1)} collective-permute-done((f32[4,128]{1,0:T(4,128)S(1)}, f32[4,128]{1,0:T(4,128)S(1)}, u32[]{:S(2)}, u32[]{:S(2)}) %collective-permute-start.2) | collective-permute-done | bytes 2080 | tf_op jit(solution)/shard_map/ppermute | solution.py:432
  118.2 13.6 %collective-permute-start.4 = (f32[34,128]{1,0:T(8,128)S(1)}, f32[34,128]{1,0:T(8,128)S(1)}, u32[]{:S(2)}, u32[]{:S(2)}) collective-permute-start(f32[34,128]{1,0:T(8,128)S(1)} %pad_maximum_fusion.6), channel_id=1, source_target_pairs={{0,32},{32,64},{64,96},{96,128},{128,160},{160,192},{192,224},{224... | collective-permute-start | bytes 52232 | tf_op jit(solution)/shard_map/ppermute | solution.py:422
  131.8 1.9 collective-permute-done.4
  133.7 16.1 %collective-permute-start.5 = (f32[34,128]{1,0:T(8,128)S(1)}, f32[34,128]{1,0:T(8,128)S(1)}, u32[]{:S(2)}, u32[]{:S(2)}) collective-permute-start(f32[34,128]{1,0:T(8,128)S(1)} %get-tuple-element.63), channel_id=1, source_target_pairs={{32,0},{64,32},{96,64},{128,96},{160,128},{192,160},{224,192},{256... | collective-permute-start | bytes 52232 | tf_op jit(solution)/shard_map/ppermute | solution.py:417
  149.8 1.5 collective-permute-done.5
  152.9 45.2 %radius_gradient.1 = (f32[68,128]{1,0:T(8,128)S(1)}, f32[68,3,8,128]{3,2,1,0:T(8,128)S(1)}) custom-call(s32[64]{0:T(128)S(1)} %get-tuple-element.27.count, s32[64,8]{1,0:T(8,128)S(1)} %copy.48.place, f32[68,8,128]{2,1,0:T(8,128)S(1)} %pad_maximum_fusion.data, f32[68,2,128]{2,1,0:T(2,128)S(1)} %pad_maximum_fusion.2.born), custom_call_target="tpu_custom_call" | custom-call | tf_op jit(solution)/shard_map/radius_gradient/pallas_call | solution.py:364
  198.2 9.4 %collective-permute-start.7 = (f32[4,128]{1,0:T(4,128)S(1)}, f32[4,128]{1,0:T(4,128)S(1)}, u32[]{:S(2)}, u32[]{:S(2)}) collective-permute-start(f32[4,128]{1,0:T(4,128)S(1)} %pad_maximum_fusion.12), channel_id=1, source_target_pairs={{1,0},{2,1},{3,2},{4,3},{5,4},{6,5},{7,6},{8,7},{9,8},{10,9},{11,1... | collective-permute-start | bytes 6152 | tf_op jit(solution)/shard_map/ppermute | solution.py:427
  207.6 1.9 collective-permute-start.6
  209.6 7.0 %collective-permute-done.6 = f32[4,128]{1,0:T(4,128)S(1)} collective-permute-done((f32[4,128]{1,0:T(4,128)S(1)}, f32[4,128]{1,0:T(4,128)S(1)}, u32[]{:S(2)}, u32[]{:S(2)}) %collective-permute-start.6) | collective-permute-done | bytes 2080 | tf_op jit(solution)/shard_map/ppermute | solution.py:432
  216.6 13.4 %collective-permute-start.9 = (f32[34,128]{1,0:T(8,128)S(1)}, f32[34,128]{1,0:T(8,128)S(1)}, u32[]{:S(2)}, u32[]{:S(2)}) collective-permute-start(f32[34,128]{1,0:T(8,128)S(1)} %pad_maximum_fusion.7), channel_id=1, source_target_pairs={{32,0},{64,32},{96,64},{128,96},{160,128},{192,160},{224,192},{256... | collective-permute-start | bytes 52232 | tf_op jit(solution)/shard_map/ppermute | solution.py:417
  230.0 1.5 collective-permute-done.9
  231.5 1.9 collective-permute-start.8
  233.4 14.0 %collective-permute-done.8 = f32[34,128]{1,0:T(8,128)S(1)} collective-permute-done((f32[34,128]{1,0:T(8,128)S(1)}, f32[34,128]{1,0:T(8,128)S(1)}, u32[]{:S(2)}, u32[]{:S(2)}) %collective-permute-start.8) | collective-permute-done | bytes 17440 | tf_op jit(solution)/shard_map/ppermute | solution.py:422
  247.6 36.2 %forces.1 = f32[68,3,128]{2,1,0:T(4,128)S(1)} custom-call(s32[64]{0:T(128)S(1)} %get-tuple-element.27.count, s32[64,8]{1,0:T(8,128)S(1)} %copy.48.place, f32[68,8,128]{2,1,0:T(8,128)S(1)} %pad_maximum_fusion.data, f32[68,1,128]{2,1,0:T(1,128)S(1)} %copy_multiply_fusion.chain, f32[68,3,8,128]{3,2,1,0:T(8,128)S(1)} %get-tuple-element.10.force_in, ...), custom_call_target="tpu_custom_call" | custom-call | tf_op jit(solution)/shard_map/forces/pallas_call | solution.py:380
  283.8 1.9 collective-permute-start.10
  285.7 13.6 %collective-permute-done.10 = f32[34,3,128]{2,1,0:T(4,128)S(1)} collective-permute-done((f32[34,3,128]{2,1,0:T(4,128)S(1)}, f32[34,3,128]{2,1,0:T(4,128)S(1)}, u32[]{:S(2)}, u32[]{:S(2)}) %collective-permute-start.10) | collective-permute-done | bytes 52256 | tf_op jit(solution)/shard_map/ppermute | solution.py:422
  299.4 1.9 collective-permute-start.11
  301.9 6.3 %collective-permute-done.11 = f32[2,3,128]{2,1,0:T(4,128)S(1)} collective-permute-done((f32[2,3,128]{2,1,0:T(4,128)S(1)}, f32[2,3,128]{2,1,0:T(4,128)S(1)}, u32[]{:S(2)}, u32[]{:S(2)}) %collective-permute-start.11) | collective-permute-done | bytes 3104 | tf_op jit(solution)/shard_map/ppermute | solution.py:432
  (56 shorter events, 9.3 us)
Async XLA Ops:
  4.8 9.5 %collective-permute-start = (f32[2,8,128]{2,1,0:T(8,128)S(1)}, f32[2,8,128]{2,1,0:T(8,128)S(1)}, u32[]{:S(2)}, u32[]{:S(2)}) collective-permute-start(f32[2,8,128]{2,1,0:T(8,128)S(1)} %slice.144), channel_id=1, source_target_pairs={{1,0},{2,1},{3,2},{4,3},{5,4},{6,5},{7,6},{8,7},{9,8},{10,9},{11,1... | collective-permute-start | bytes 24584 | tf_op jit(solution)/shard_map/ppermute | solution.py:427
  14.3 20.4 %collective-permute-start.1 = (f32[34,8,128]{2,1,0:T(8,128)S(1)}, f32[34,8,128]{2,1,0:T(8,128)S(1)}, u32[]{:S(2)}, u32[]{:S(2)}) collective-permute-start(f32[34,8,128]{2,1,0:T(8,128)S(1)} %pad_maximum_fusion.1), channel_id=1, source_target_pairs={{32,0},{64,32},{96,64},{128,96},{160,128},{192,160},{224,192},{256... | collective-permute-start | bytes 417800 | tf_op jit(solution)/shard_map/ppermute | solution.py:417
  92.5 18.8 %collective-permute-start.3 = (f32[4,128]{1,0:T(4,128)S(1)}, f32[4,128]{1,0:T(4,128)S(1)}, u32[]{:S(2)}, u32[]{:S(2)}) collective-permute-start(f32[4,128]{1,0:T(4,128)S(1)} %pad_maximum_fusion.10), channel_id=1, source_target_pairs={{1,0},{2,1},{3,2},{4,3},{5,4},{6,5},{7,6},{8,7},{9,8},{10,9},{11,1... | collective-permute-start | bytes 6152 | tf_op jit(solution)/shard_map/ppermute | solution.py:427
  109.4 8.8 %collective-permute-start.2 = (f32[4,128]{1,0:T(4,128)S(1)}, f32[4,128]{1,0:T(4,128)S(1)}, u32[]{:S(2)}, u32[]{:S(2)}) collective-permute-start(f32[4,128]{1,0:T(4,128)S(1)} %pad_maximum_fusion.9), channel_id=1, source_target_pairs={{0,1},{1,2},{2,3},{3,4},{4,5},{5,6},{6,7},{7,8},{8,9},{9,10},{10,1... | collective-permute-start | bytes 6152 | tf_op jit(solution)/shard_map/ppermute | solution.py:432
  118.2 15.4 %collective-permute-start.4 = (f32[34,128]{1,0:T(8,128)S(1)}, f32[34,128]{1,0:T(8,128)S(1)}, u32[]{:S(2)}, u32[]{:S(2)}) collective-permute-start(f32[34,128]{1,0:T(8,128)S(1)} %pad_maximum_fusion.6), channel_id=1, source_target_pairs={{0,32},{32,64},{64,96},{96,128},{128,160},{160,192},{192,224},{224... | collective-permute-start | bytes 52232 | tf_op jit(solution)/shard_map/ppermute | solution.py:422
  133.7 17.6 %collective-permute-start.5 = (f32[34,128]{1,0:T(8,128)S(1)}, f32[34,128]{1,0:T(8,128)S(1)}, u32[]{:S(2)}, u32[]{:S(2)}) collective-permute-start(f32[34,128]{1,0:T(8,128)S(1)} %get-tuple-element.63), channel_id=1, source_target_pairs={{32,0},{64,32},{96,64},{128,96},{160,128},{192,160},{224,192},{256... | collective-permute-start | bytes 52232 | tf_op jit(solution)/shard_map/ppermute | solution.py:417
  198.2 11.4 %collective-permute-start.7 = (f32[4,128]{1,0:T(4,128)S(1)}, f32[4,128]{1,0:T(4,128)S(1)}, u32[]{:S(2)}, u32[]{:S(2)}) collective-permute-start(f32[4,128]{1,0:T(4,128)S(1)} %pad_maximum_fusion.12), channel_id=1, source_target_pairs={{1,0},{2,1},{3,2},{4,3},{5,4},{6,5},{7,6},{8,7},{9,8},{10,9},{11,1... | collective-permute-start | bytes 6152 | tf_op jit(solution)/shard_map/ppermute | solution.py:427
  207.6 8.9 %collective-permute-start.6 = (f32[4,128]{1,0:T(4,128)S(1)}, f32[4,128]{1,0:T(4,128)S(1)}, u32[]{:S(2)}, u32[]{:S(2)}) collective-permute-start(f32[4,128]{1,0:T(4,128)S(1)} %pad_maximum_fusion.11), channel_id=1, source_target_pairs={{0,1},{1,2},{2,3},{3,4},{4,5},{5,6},{6,7},{7,8},{8,9},{9,10},{10,1... | collective-permute-start | bytes 6152 | tf_op jit(solution)/shard_map/ppermute | solution.py:432
  216.6 14.9 %collective-permute-start.9 = (f32[34,128]{1,0:T(8,128)S(1)}, f32[34,128]{1,0:T(8,128)S(1)}, u32[]{:S(2)}, u32[]{:S(2)}) collective-permute-start(f32[34,128]{1,0:T(8,128)S(1)} %pad_maximum_fusion.7), channel_id=1, source_target_pairs={{32,0},{64,32},{96,64},{128,96},{160,128},{192,160},{224,192},{256... | collective-permute-start | bytes 52232 | tf_op jit(solution)/shard_map/ppermute | solution.py:417
  231.5 15.9 %collective-permute-start.8 = (f32[34,128]{1,0:T(8,128)S(1)}, f32[34,128]{1,0:T(8,128)S(1)}, u32[]{:S(2)}, u32[]{:S(2)}) collective-permute-start(f32[34,128]{1,0:T(8,128)S(1)} %get-tuple-element.61), channel_id=1, source_target_pairs={{0,32},{32,64},{64,96},{96,128},{128,160},{160,192},{192,224},{224... | collective-permute-start | bytes 52232 | tf_op jit(solution)/shard_map/ppermute | solution.py:422
  283.8 15.5 %collective-permute-start.10 = (f32[34,3,128]{2,1,0:T(4,128)S(1)}, f32[34,3,128]{2,1,0:T(4,128)S(1)}, u32[]{:S(2)}, u32[]{:S(2)}) collective-permute-start(f32[34,3,128]{2,1,0:T(4,128)S(1)} %slice.158), channel_id=1, source_target_pairs={{0,32},{32,64},{64,96},{96,128},{128,160},{160,192},{192,224},{224... | collective-permute-start | bytes 156680 | tf_op jit(solution)/shard_map/ppermute | solution.py:422
  299.4 8.8 %collective-permute-start.11 = (f32[2,3,128]{2,1,0:T(4,128)S(1)}, f32[2,3,128]{2,1,0:T(4,128)S(1)}, u32[]{:S(2)}, u32[]{:S(2)}) collective-permute-start(f32[2,3,128]{2,1,0:T(4,128)S(1)} %slice.160), channel_id=1, source_target_pairs={{0,1},{1,2},{2,3},{3,4},{4,5},{5,6},{6,7},{7,8},{8,9},{9,10},{10,1... | collective-permute-start | bytes 9224 | tf_op jit(solution)/shard_map/ppermute | solution.py:432

commit v2 on v1

v2 whole, which is shorter than its diff:
```python
import functools
import math

import jax
import jax.numpy as jnp
import numpy as np
from jax import lax
from jax.experimental import pallas as pl
from jax.experimental.pallas import tpu as pltpu
from jax.sharding import PartitionSpec as P

radius_offset = 0.09
obc_alpha = 1.0
obc_beta = 0.8
obc_gamma = 4.85
cutoff_len = 14.0
cutoff_sq = cutoff_len * cutoff_len

TILES = 32
EDGE = 2
HALF = TILES + EDGE
REGION = 2 * HALF
OWN_ROWS = HALF + 1
ALL_ROWS = REGION + 1
LISTED = 7
ATOMS = 128
CHUNK = 16
CHUNKS = ATOMS // CHUNK
FULL_WIDTH = 2
PART_WIDTH = 4
FULL_RING = 32
PART_RING = 32
SELF_WIDTH = 4
PAIRS = 2 * TILES * LISTED + 4
ITEMS = 512
DUMMY = HALF * ATOMS + REGION
ROW = (1, ATOMS)
LANES = (8, ATOMS)
ROWS = (CHUNK, ATOMS)
BLOCK = (ATOMS, ATOMS)
PART = ATOMS // 2
VMEM_LIMIT = 56 * 1024 * 1024
SCALE = math.sqrt(8.0) / cutoff_len
CUT = 8.0
EXP_SCALE = math.sqrt(0.25 / math.log(2.0)) / SCALE

ROW_X, ROW_Y, ROW_Z, ROW_Q, ROW_IN, ROW_SCALED, ROW_RADIUS, ROW_CODE = range(8)

F32 = jnp.float32


def fold2(block):
    return block[0:8] + block[8:16]


def fold_own(own):
    flipped = own.T
    total = flipped[0:8]
    for chunk in range(1, ATOMS // 8):
        total = total + flipped[8 * chunk : 8 * chunk + 8]
    return total


def by_fours(step):
    def fours(index, carry):
        start = jnp.minimum(index * 4, HALF - 4)
        for k in range(4):
            step(start + k)
        return carry

    lax.fori_loop(0, (HALF + 3) // 4, fours, 0)


def fill_table(table, tile, first, ref, rows, factor=None):
    for slot, row in enumerate(rows):
        values = ref[tile, row : row + 1, :]
        if factor is not None:
            values = values * factor
        table[tile, first + slot] = jnp.broadcast_to(values, BLOCK).T


def fold_rows(own, target, index):
    def fours(quad, carry):
        for k in range(4):
            tile = quad * 4 + k
            target[(tile,) + index] += fold_own(own[(tile,) + index])
        return carry

    lax.fori_loop(0, TILES // 4, fours, 0)
    for tile in range(TILES, HALF):
        target[(tile,) + index] += fold_own(own[(tile,) + index])


def clear(ref):
    def step(tile, carry):
        ref[tile] = jnp.zeros(ref.shape[1:], F32)
        return carry

    lax.fori_loop(0, ref.shape[0], step, 0)


def diagonal(start):
    rows = lax.broadcasted_iota(jnp.int32, ROWS, 0) + start
    return jnp.where(rows == lax.broadcasted_iota(jnp.int32, ROWS, 1), 4.0 * CUT, 0.0)


def decode(item):
    return lax.shift_right_logical(item, 7), lax.bitwise_and(item, ATOMS - 1)


def span(start):
    return pl.ds(start if isinstance(start, int) else pl.multiple_of(start, CHUNK), CHUNK)


def part_starts(code):
    return [lax.bitwise_and(lax.shift_right_logical(code, 3 * j), 7) * CHUNK for j in range(CHUNKS // 2)]


def row_of(ref, tile, row):
    return jnp.broadcast_to(ref[tile, row : row + 1, :], ROWS)


def differences(table, tile, rows, far):
    return tuple(table[tile, axis, rows, :] - far[axis] for axis in range(3))


def distance_squared(gaps):
    dx, dy, dz = gaps
    return dx * dx + dy * dy + dz * dz


def half_descreen(r, own, far):
    upper = r + far
    lower = r - far
    inner = jnp.minimum(jnp.maximum(own, lower), upper)
    ratio = upper * pl.reciprocal(inner, approx=True)
    slope = lower * pl.reciprocal(upper, approx=True)
    square = ratio * ratio
    rise = ratio - 1.0
    twice = jnp.log(square)
    value = rise * (2.0 - slope * rise) - twice
    deriv = (twice + twice) - (square - 1.0) * (slope * slope + 1.0)
    return value, deriv


def ring_copies(ring, blocks, sems, size, rows):
    def copy(index, place, inward):
        slot = lax.rem(index, size)
        here = ring.at[slot]
        there = blocks.at[place, :, pl.ds(0, rows), :]
        source, target = (there, here) if inward else (here, there)
        return pltpu.make_async_copy(source, target, sems.at[slot])

    return copy


def born_kernel(total, items, reach, data, part, d_self, d_pair, table, own, far, rings, sems):
    full_ring, part_ring, self_ring = rings
    full_sems, part_sems, self_sems = sems
    far[...] = jnp.zeros_like(far)
    fulls, parts = total[0], total[1]

    def prepare(tile):
        fill_table(table, tile, 0, data, (ROW_X, ROW_Y, ROW_Z, ROW_IN, ROW_SCALED))

    by_fours(prepare)
    for tile in range(TILES, OWN_ROWS):
        own[tile] = jnp.zeros(BLOCK, F32)

    def shared(tile, rows, r2):
        inv = lax.rsqrt(r2)
        cut = jnp.maximum(1.0 - r2 * (1.0 / CUT), 0.0)
        cinv = cut * inv
        return r2 * inv, cut, cinv, cinv * cinv * inv

    def self_pair(tile):
        far_xyz = [row_of(data, tile, axis) for axis in range(3)]
        bs = row_of(data, tile, ROW_SCALED)
        for start in range(0, ATOMS, CHUNK):
            rows = span(start)
            r2 = distance_squared(differences(table, tile, rows, far_xyz)) + diagonal(start)
            r, cut, cinv, g_deriv = shared(tile, rows, r2)
            value, deriv = half_descreen(r, table[tile, 3, rows, :], bs)
            value = cinv * value
            own[tile, rows, :] = cut * value
            self_ring[tile, rows, :] = g_deriv * deriv - value

    def self_copy(tile):
        return pltpu.make_async_copy(self_ring.at[tile], d_self.at[tile], self_sems.at[tile])

    def self_step(quad, carry):
        for k in range(SELF_WIDTH):
            self_pair(quad * SELF_WIDTH + k)
        for k in range(SELF_WIDTH):
            self_copy(quad * SELF_WIDTH + k).start()
        return carry

    lax.fori_loop(0, TILES // SELF_WIDTH, self_step, 0)

    def pair(item, ring, slot, starts):
        first, second = item
        far_xyz = [row_of(data, second, axis) for axis in range(3)]
        bp, bs = row_of(data, second, ROW_IN), row_of(data, second, ROW_SCALED)
        sums = jnp.zeros(ROWS, F32)
        for place, start in enumerate(starts):
            rows = span(start)
            kept = span(place * CHUNK)
            r2 = distance_squared(differences(table, first, rows, far_xyz))
            r, cut, cinv, g_deriv = shared(first, rows, r2)
            value, deriv = half_descreen(r, table[first, 3, rows, :], bs)
            value = cinv * value
            own[first, rows, :] += cut * value
            ring[slot, 0, kept, :] = g_deriv * deriv - value
            value, deriv = half_descreen(r, bp, table[first, 4, rows, :])
            value = cinv * value
            ring[slot, 1, kept, :] = g_deriv * deriv - value
            sums = sums + cut * value
        far[second] += fold2(sums)

    def run(width, size, ring, ring_sems, base, number, rows, starts_of):
        copy = ring_copies(ring, d_pair, ring_sems, size, rows)

        def body(index, carry):
            begin = index * width
            for k in range(width):

                @pl.when(begin + k >= size)
                def _():
                    copy(begin + k, base + begin + k, False).wait()

            for k in range(width):
                item = decode(items[base + begin + k])
                pair(item, ring, lax.rem(begin + k, size), starts_of(item))
            for k in range(width):
                copy(begin + k, base + begin + k, False).start()
            return carry

        lax.fori_loop(0, lax.div(number, width), body, 0)

    def drain(size, ring, ring_sems, number, rows):
        copy = ring_copies(ring, d_pair, ring_sems, size, rows)

        def wait(slot, carry):
            copy(slot, slot, False).wait()
            return carry

        lax.fori_loop(0, jnp.minimum(number, size), wait, 0)

    def listed_starts(item):
        return part_starts(reach[item[0] * ALL_ROWS + item[1]])

    run(FULL_WIDTH, FULL_RING, full_ring, full_sems, 0, fulls, ATOMS, lambda item: range(0, ATOMS, CHUNK))
    run(PART_WIDTH, PART_RING, part_ring, part_sems, fulls, parts, PART, listed_starts)
    fold_rows(own, far, ())
    part[...] = jnp.sum(far[0:REGION], axis=1) * (0.125 * SCALE)
    for tile in range(TILES):
        self_copy(tile).wait()
    drain(FULL_RING, full_ring, full_sems, fulls, ATOMS)
    drain(PART_RING, part_ring, part_sems, parts, PART)


def energy_kernel(total, items, reach, data, born, part, force, table, own, far):
    far[...] = jnp.zeros_like(far)
    force[...] = jnp.zeros_like(force)
    fulls, parts = total[0], total[1]

    def prepare(tile):
        fill_table(table, tile, 0, data, (ROW_X, ROW_Y, ROW_Z, ROW_Q))
        fill_table(table, tile, 4, born, (0, 1))

    by_fours(prepare)
    for tile in range(TILES, OWN_ROWS):
        own[tile] = jnp.zeros((4,) + BLOCK, F32)

    def pair(first, second, starts, is_self):
        far_xyz = [row_of(data, second, axis) for axis in range(3)]
        br, bi, bq = row_of(born, second, 0), -row_of(born, second, 1), row_of(data, second, ROW_Q)
        sums = [jnp.zeros(ROWS, F32)] * 4
        for start in starts:
            rows = span(start)
            gaps = differences(table, first, rows, far_xyz)
            r2 = distance_squared(gaps)
            if is_self:
                r2 = r2 + diagonal(start)
            cut = jnp.maximum(1.0 - r2 * (1.0 / CUT), 0.0)
            power = r2 * (table[first, 5, rows, :] * bi)
            decay = lax.exp2(power)
            screen = (table[first, 4, rows, :] * br) * decay
            inv = lax.rsqrt(r2 + screen)
            lead = (cut * (table[first, 3, rows, :] * bq)) * inv
            square = cut * (inv * inv)
            grad = (lead * square) * (screen * (1.0 - math.log(2.0) * power))
            pull = lead * (square * (4.0 - decay) + 16.0 / CUT)
            terms = [grad] + [pull * gap for gap in gaps]
            for which, term in enumerate(terms):
                if is_self:
                    own[first, which, rows, :] = term
                else:
                    own[first, which, rows, :] += term
                    sums[which] = sums[which] + term
        if not is_self:
            far[second] += fold2(sums[0])
            for axis in range(3):
                force[second, axis] -= fold2(sums[1 + axis])

    def self_step(quad, carry):
        for k in range(2):
            pair(quad * 2 + k, quad * 2 + k, range(0, ATOMS, CHUNK), True)
        return carry

    lax.fori_loop(0, TILES // 2, self_step, 0)

    def full_step(index, carry):
        for k in range(FULL_WIDTH):
            first, second = decode(items[index * FULL_WIDTH + k])
            pair(first, second, range(0, ATOMS, CHUNK), False)
        return carry

    def part_step(index, carry):
        for k in range(PART_WIDTH):
            first, second = decode(items[fulls + index * PART_WIDTH + k])
            pair(first, second, part_starts(reach[first * ALL_ROWS + second]), False)
        return carry

    lax.fori_loop(0, lax.div(fulls, FULL_WIDTH), full_step, 0)
    lax.fori_loop(0, lax.div(parts, PART_WIDTH), part_step, 0)

    def fold_step(pairs, carry):
        for k in range(2):
            tile = pairs * 2 + k
            far[tile] += fold_own(own[tile, 0])
            for axis in range(3):
                force[tile, axis] += fold_own(own[tile, 1 + axis])
        return carry

    lax.fori_loop(0, HALF // 2, fold_step, 0)
    part[...] = jnp.sum(far[0:REGION], axis=1) * (0.5 * SCALE)


def force_kernel(total, items, reach, data, chain, force_in, d_self, d_pair, force, table, own, far, rings, sems):
    full_ring, part_ring, self_ring = rings
    full_sems, part_sems, self_sems = sems
    far[...] = force_in[...] * 4.0
    fulls, parts = total[0], total[1]
    full_copy = ring_copies(full_ring, d_pair, full_sems, FULL_RING, ATOMS)
    part_copy = ring_copies(part_ring, d_pair, part_sems, PART_RING, PART)

    def self_copy(tile):
        return pltpu.make_async_copy(d_self.at[tile], self_ring.at[tile], self_sems.at[tile])

    def start(copy, base):
        def step(index, carry):
            copy(index, base + index, True).start()
            return carry

        return step

    for tile in range(TILES):
        self_copy(tile).start()
    lax.fori_loop(0, jnp.minimum(fulls, FULL_RING), start(full_copy, 0), 0)
    lax.fori_loop(0, jnp.minimum(parts, PART_RING), start(part_copy, fulls), 0)

    def prepare(tile):
        fill_table(table, tile, 0, data, (ROW_X, ROW_Y, ROW_Z))
        fill_table(table, tile, 3, chain, (0,))

    by_fours(prepare)
    for tile in range(TILES, OWN_ROWS):
        own[tile] = jnp.zeros((3,) + BLOCK, F32)

    def pair(first, second, starts, pull_of, is_self):
        far_xyz = [row_of(data, second, axis) for axis in range(3)]
        sums = [jnp.zeros(ROWS, F32)] * 3
        for place, start in enumerate(starts):
            rows = span(start)
            pull = pull_of(rows, span(place * CHUNK))
            terms = [pull * gap for gap in differences(table, first, rows, far_xyz)]
            for which, term in enumerate(terms):
                if is_self:
                    own[first, which, rows, :] = term
                else:
                    own[first, which, rows, :] += term
                sums[which] = sums[which] + term
        for axis in range(3):
            far[second, axis] -= fold2(sums[axis])

    def self_step(quad, carry):
        begin = quad * SELF_WIDTH
        for k in range(SELF_WIDTH):
            self_copy(begin + k).wait()
        for k in range(SELF_WIDTH):
            tile = begin + k
            pair(
                tile,
                tile,
                range(0, ATOMS, CHUNK),
                lambda rows, kept: table[tile, 3, rows, :] * self_ring[tile, kept, :],
                True,
            )
        return carry

    lax.fori_loop(0, TILES // SELF_WIDTH, self_step, 0)

    def run(width, size, ring, copy, base, number, starts_of):
        def body(index, carry):
            begin = index * width
            for k in range(width):
                copy(begin + k, base + begin + k, True).wait()
            for k in range(width):
                first, second = decode(items[base + begin + k])
                slot = lax.rem(begin + k, size)
                factor = row_of(chain, second, 0)
                pair(
                    first,
                    second,
                    starts_of(first, second),
                    lambda rows, kept: table[first, 3, rows, :] * ring[slot, 0, kept, :]
                    + factor * ring[slot, 1, kept, :],
                    False,
                )
            for k in range(width):

                @pl.when(begin + k + size < number)
                def _():
                    copy(begin + k + size, base + begin + k + size, True).start()

            return carry

        lax.fori_loop(0, lax.div(number, width), body, 0)

    run(FULL_WIDTH, FULL_RING, full_ring, full_copy, 0, fulls, lambda *_: range(0, ATOMS, CHUNK))
    run(
        PART_WIDTH,
        PART_RING,
        part_ring,
        part_copy,
        fulls,
        parts,
        lambda first, second: part_starts(reach[first * ALL_ROWS + second]),
    )

    def fold_step(pairs, carry):
        for k in range(2):
            tile = pairs * 2 + k
            for axis in range(3):
                far[tile, axis] += fold_own(own[tile, axis])
        return carry

    lax.fori_loop(0, HALF // 2, fold_step, 0)
    force[...] = jnp.sum(far[0:REGION], axis=2) * (-SCALE * SCALE / 16.0)


SMEM = pl.BlockSpec(memory_space=pltpu.SMEM)
VMEM = pl.BlockSpec(memory_space=pltpu.VMEM)
ANY = pl.BlockSpec(memory_space=pl.ANY)
PARAMS = pltpu.CompilerParams(vmem_limit_bytes=VMEM_LIMIT)
RING_BLOCKS = (
    pltpu.VMEM((FULL_RING, 2) + BLOCK, F32),
    pltpu.VMEM((PART_RING, 2, PART, ATOMS), F32),
    pltpu.VMEM((TILES,) + BLOCK, F32),
)
RING_SEMS = (
    pltpu.SemaphoreType.DMA((FULL_RING,)),
    pltpu.SemaphoreType.DMA((PART_RING,)),
    pltpu.SemaphoreType.DMA((TILES,)),
)


def f32(*shape):
    return jax.ShapeDtypeStruct(shape, F32)


def run_born(total, items, reach, data):
    return pl.pallas_call(
        born_kernel,
        name="born_sums",
        out_shape=(f32(REGION, ATOMS), f32(TILES, *BLOCK), f32(PAIRS, 2, *BLOCK)),
        in_specs=[SMEM, SMEM, SMEM, VMEM],
        out_specs=(VMEM, ANY, ANY),
        scratch_shapes=[
            pltpu.VMEM((OWN_ROWS, 5) + BLOCK, F32),
            pltpu.VMEM((OWN_ROWS,) + BLOCK, F32),
            pltpu.VMEM((ALL_ROWS,) + LANES, F32),
            RING_BLOCKS,
            RING_SEMS,
        ],
        compiler_params=PARAMS,
    )(total, items, reach, data)


def run_energy(total, items, reach, data, born):
    return pl.pallas_call(
        energy_kernel,
        name="radius_gradient",
        out_shape=(f32(REGION, ATOMS), f32(ALL_ROWS, 3, *LANES)),
        in_specs=[SMEM, SMEM, SMEM, VMEM, VMEM],
        out_specs=(VMEM, VMEM),
        scratch_shapes=[
            pltpu.VMEM((OWN_ROWS, 6) + BLOCK, F32),
            pltpu.VMEM((OWN_ROWS, 4) + BLOCK, F32),
            pltpu.VMEM((ALL_ROWS,) + LANES, F32),
        ],
        compiler_params=PARAMS,
    )(total, items, reach, data, born)


def run_force(total, items, reach, data, chain, force_in, d_self, d_pair):
    return pl.pallas_call(
        force_kernel,
        name="forces",
        out_shape=f32(REGION, 3, ATOMS),
        in_specs=[SMEM, SMEM, SMEM, VMEM, VMEM, VMEM, ANY, ANY],
        out_specs=VMEM,
        scratch_shapes=[
            pltpu.VMEM((OWN_ROWS, 4) + BLOCK, F32),
            pltpu.VMEM((OWN_ROWS, 3) + BLOCK, F32),
            pltpu.VMEM((ALL_ROWS, 3) + LANES, F32),
            RING_BLOCKS,
            RING_SEMS,
        ],
        compiler_params=PARAMS,
    )(total, items, reach, data, chain, force_in, d_self, d_pair)


def born_radius(descreen_sum, radius, radius_in):
    scaled = radius_in * descreen_sum
    polynomial = scaled * (obc_alpha + scaled * (-obc_beta + obc_gamma * scaled))
    tangent = jnp.tanh(polynomial)
    radii_born = 1.0 / (1.0 / radius_in - tangent / radius)
    radius_slope = (
        radii_born
        * radii_born
        * (1.0 - tangent * tangent)
        / radius
        * (obc_alpha - 2.0 * obc_beta * scaled + 3.0 * obc_gamma * scaled * scaled)
        * radius_in
    )
    return (radii_born, radius_slope)


def above_to_here(block):
    ends = lax.axis_size("slab") - 1
    return lax.ppermute(block, "slab", [(i + 1, i) for i in range(ends)])


def here_to_above(block):
    ends = lax.axis_size("slab") - 1
    return lax.ppermute(block, "slab", [(i, i + 1) for i in range(ends)])


def next_to_here(block):
    count = lax.axis_size("tile")
    return lax.ppermute(block, "tile", [((i + 1) % count, i) for i in range(count)])


def here_to_next(block):
    count = lax.axis_size("tile")
    return lax.ppermute(block, "tile", [(i, (i + 1) % count) for i in range(count)])


def swap_sums(part):
    to_next = jnp.concatenate([part[TILES:HALF], part[HALF + TILES :]])
    to_last = jnp.concatenate([part[0:EDGE], part[HALF : HALF + EDGE]])
    from_last = here_to_next(to_next)
    from_next = next_to_here(to_last)
    column = jnp.concatenate(
        [
            part[0:EDGE] + from_last[0:EDGE],
            part[EDGE:TILES],
            part[TILES:HALF] + from_next[0:EDGE],
            part[HALF : HALF + EDGE] + from_last[EDGE:],
            part[HALF + EDGE : HALF + TILES],
            part[HALF + TILES :] + from_next[EDGE:],
        ]
    )
    own, above = column[0:HALF], column[HALF:]
    from_below = here_to_above(above)
    from_above = above_to_here(own)
    return jnp.concatenate([own + from_below, above + from_above])


def pair_lists(neighbours, pad_mask):
    cycle_count = lax.axis_size("tile")
    cycle_tiles = cycle_count * TILES
    slab_step = neighbours // cycle_tiles - lax.axis_index("slab")
    within = neighbours % cycle_tiles
    cycle_step = (within // TILES - lax.axis_index("tile")) % cycle_count
    place = cycle_step * TILES + within % TILES
    live = (pad_mask == 1) & (jnp.arange(neighbours.shape[1]) > 0)[None, :]
    here = jnp.where(live & (slab_step >= 0), slab_step * HALF + place, -1)
    below = jnp.where(live & (slab_step < 0), place, -1)
    return here, below


def chunk_reach(data, across, along):
    inverse = lax.rsqrt(across * across + along * along)
    across, along = across * inverse, along * inverse
    x, y, z = data[:, ROW_X], data[:, ROW_Y], data[:, ROW_Z]
    turned = jnp.stack([x * across + y * along, y * across - x * along, z])
    pieces = turned.reshape(3, REGION, CHUNKS, CHUNK)
    low, high = jnp.min(pieces, axis=3), jnp.max(pieces, axis=3)
    tile_low, tile_high = jnp.min(low, axis=2), jnp.max(high, axis=2)
    near = []
    for chunk in range(CHUNKS):
        own_low, own_high = low[:, :HALF, chunk, None], high[:, :HALF, chunk, None]
        gap = jnp.maximum(jnp.maximum(tile_low[:, None, :] - own_high, own_low - tile_high[:, None, :]), 0.0)
        far = jnp.sum(gap * gap, axis=0) >= CUT * 1.001
        near.append(jnp.logical_not(far).astype(jnp.int32))
    number = sum(near)
    code = number << (3 * CHUNKS)
    before = jnp.zeros_like(number)
    for chunk in range(CHUNKS):
        rank = jnp.where(near[chunk] == 1, before, number + chunk - before)
        code = code + (chunk << (3 * rank))
        before = before + near[chunk]
    is_part = number <= CHUNKS // 2
    edge = ((0, OWN_ROWS - HALF), (0, ALL_ROWS - REGION))
    return jnp.pad(code, edge).reshape(-1), is_part


def packed(first, second, valid, is_part):
    first, second, valid = first.reshape(-1), second.reshape(-1), valid.reshape(-1)
    mine = (first[:, None] == jnp.arange(HALF)[None, :]).astype(jnp.bfloat16)
    rows = jnp.dot(mine, is_part.astype(jnp.bfloat16), preferred_element_type=F32)
    in_part = jnp.sum(jnp.where(second[:, None] == jnp.arange(REGION)[None, :], rows, 0.0), axis=1) > 0.5
    entry = jnp.arange(valid.shape[0])
    ahead = valid[None, :] & (entry[None, :] < entry[:, None]) & (in_part[None, :] == in_part[:, None])
    rank = jnp.sum(ahead, axis=1)
    fulls = jnp.sum(valid & jnp.logical_not(in_part), dtype=jnp.int32)
    parts = jnp.sum(valid & in_part, dtype=jnp.int32)
    fulls = (fulls + FULL_WIDTH - 1) // FULL_WIDTH * FULL_WIDTH
    parts = (parts + PART_WIDTH - 1) // PART_WIDTH * PART_WIDTH
    rank = jnp.where(in_part, fulls + rank, rank)
    chosen = valid[None, :] & (rank[None, :] == jnp.arange(ITEMS)[:, None])
    value = first * ATOMS + second - DUMMY
    items = DUMMY + jnp.sum(jnp.where(chosen, value[None, :], 0), axis=1)
    return jnp.stack([fulls, parts]), items.astype(jnp.int32)


def region_data(own, above):
    origin = jnp.pad(own[TILES // 2, 0:3, 0:1], ((0, 5), (0, 0)))
    factor = np.ones((1, 8, 1), np.float32)
    factor[0, [ROW_X, ROW_Y, ROW_Z, ROW_IN, ROW_SCALED]] = SCALE
    return jnp.concatenate([own - origin, above - origin, jnp.zeros_like(own[0:1])]) * factor


def body(positions, charges, radii, scales, neighbours, pad_mask):
    coords = positions[0, 0]
    charge = charges[0, 0]
    radius = radii[0, 0]
    radius_in = radius - radius_offset
    here, below = pair_lists(neighbours[0, 0], pad_mask[0, 0])
    code = jnp.pad(below.astype(jnp.float32), ((0, 0), (0, ATOMS - below.shape[1])))
    own = jnp.concatenate(
        [coords, jnp.stack([charge, radius_in, scales[0, 0] * radius_in, radius, code], axis=1)], axis=1
    )
    own = jnp.concatenate([own, next_to_here(own[0:EDGE])])
    above = above_to_here(own)
    data = region_data(own, above)
    listed_above = above[0:TILES, ROW_CODE, 0 : below.shape[1]].astype(jnp.int32)
    has_above = lax.axis_index("slab") < lax.axis_size("slab") - 1
    tiles = jnp.broadcast_to(jnp.arange(TILES, dtype=jnp.int32)[:, None], here.shape)
    reach, is_part = chunk_reach(data[0:REGION], coords[TILES // 2, 0, 0], coords[TILES // 2, 1, 0])
    total, items = packed(
        jnp.concatenate([tiles, listed_above]),
        jnp.concatenate([here, HALF + tiles]),
        jnp.concatenate([here >= 0, (listed_above >= 0) & has_above]),
        is_part,
    )
    region_radius = jnp.concatenate([own[:, ROW_RADIUS], above[:, ROW_RADIUS]])
    region_in = jnp.concatenate([own[:, ROW_IN], above[:, ROW_IN]])

    part, d_self, d_pair = run_born(total, items, reach, data)
    radii_born, radius_slope = born_radius(swap_sums(part), region_radius, region_in)
    inverse = 1.0 / radii_born
    born = jnp.stack([SCALE * radii_born, EXP_SCALE * inverse], axis=1)
    part, force = run_energy(total, items, reach, data, jnp.pad(born, ((0, 1), (0, 0), (0, 0))))
    own_charge = charge * inverse[0:TILES]
    part = part * inverse + jnp.pad(0.5 * own_charge * own_charge, ((0, REGION - TILES), (0, 0)))
    gradient = swap_sums(part)
    chain = jnp.pad((gradient * radius_slope)[:, None], ((0, 1), (0, 0), (0, 0)))
    force = run_force(total, items, reach, data, chain, force, d_self, d_pair)
    back = here_to_above(force[HALF:])
    mine = force[0:HALF] + back
    last = here_to_next(mine[TILES:])
    forces = jnp.concatenate([mine[0:EDGE] + last, mine[EDGE:TILES]])
    return (radii_born[None, None, 0:TILES], gradient[None, None, 0:TILES], forces[None, None])


def solution(mesh):
    return jax.shard_map(
        body,
        mesh=mesh,
        in_specs=(
            P("slab", "tile", None, None, None),
            P("slab", "tile", None, None),
            P("slab", "tile", None, None),
            P("slab", "tile", None, None),
            P("slab", "tile", None, None),
            P("slab", "tile", None, None),
        ),
        out_specs=(
            P("slab", "tile", None, None),
            P("slab", "tile", None, None),
            P("slab", "tile", None, None, None),
        ),
        check_vma=False,
    )
```

time: 312 us -> 223 us (0.71)
  Pallas kernels: 139 us -> 66.1 us
  starting transfers between devices: 97.3 us -> 56.6 us
  local copies, waits for them, and re-layouts: 4.75 us -> 12.6 us
  other arithmetic: 3.24 us -> 10.6 us
  between operations: 0.97 us -> 6.41 us
  waiting for transfers between devices: 64 us -> 68.9 us
    pallas_call x3, Pallas kernels: 139 us -> 66.1 us  [the longest x1 27.5 us: run_born(): pl.pallas_call(born_kernel, name='born_sums', out_shape=(f32(REGION, ATOM...]
    ppermute x3, starting transfers between devices: 39.8 us -> 14.1 us  [above_to_here(): return lax.ppermute(block, 'slab', [(i + 1, i) for i in range(ends)])]
    ppermute x3, waiting for transfers between devices: 13.1 us -> 26.5 us  [above_to_here(): return lax.ppermute(block, 'slab', [(i + 1, i) for i in range(ends)])]
    ppermute x3, starting transfers between devices: 17.4 us -> 8.7 us  [here_to_above(): return lax.ppermute(block, 'slab', [(i, i + 1) for i in range(ends)])]
    ppermute x3, starting transfers between devices: 34.4 us -> 28.1 us  [next_to_here(): lax.ppermute(block, 'tile', [((i + 1) % count, i) for i in range(count)])]
    ppermute x3, waiting for transfers between devices: 29.4 us -> 23.2 us  [here_to_above(): return lax.ppermute(block, 'slab', [(i, i + 1) for i in range(ends)])]
  transfers between devices with their start and end apart: 12 -> 12, of which waited for: 10 -> 9; matrix products, arithmetic and copies ran while one was open for 0% -> 2% of each run, Pallas kernels for 0% -> 0%
where the time goes in v2:
time: 223 us; the launch traced here: 221 us
  waiting for transfers between devices  68.9 us (31%)
  Pallas kernels  66.1 us (30%)
  starting transfers between devices  56.6 us (25%)
  local copies, waits for them, and re-layouts  12.6 us (6%)
  other arithmetic  10.6 us (5%)
  between operations  6.41 us (3%)
    ppermute x3, starting transfers between devices, next_to_here(): lax.ppermute(block, 'tile', [((i + 1) % count, i) for i in range(count)])  28.1 us
    pallas_call x1, Pallas kernels, run_born(): pl.pallas_call(born_kernel, name='born_sums', out_shape=(f32(REGION, ATOM...  27.5 us
    ppermute x3, waiting for transfers between devices, above_to_here(): return lax.ppermute(block, 'slab', [(i + 1, i) for i in range(ends)])  26.5 us
    ppermute x3, waiting for transfers between devices, here_to_above(): return lax.ppermute(block, 'slab', [(i, i + 1) for i in range(ends)])  23.2 us
    pallas_call x1, Pallas kernels, run_energy(): pl.pallas_call(energy_kernel, name='radius_gradient', out_shape=(f32(REGI...  22.9 us
    ppermute x3, waiting for transfers between devices, here_to_next(): lax.ppermute(block, 'tile', [(i, (i + 1) % count) for i in range(count)])  19.2 us
    pallas_call x1, Pallas kernels, run_force(): pl.pallas_call(force_kernel, name='forces', out_shape=f32(REGION, 3, ATOM...  15.6 us
    ppermute x3, starting transfers between devices, above_to_here(): return lax.ppermute(block, 'slab', [(i + 1, i) for i in range(ends)])  14.1 us
  transfers between devices with their start and end apart: 12, of which 9 were waited for; matrix products, arithmetic and copies ran while one was open for 2% of the time, Pallas kernels for 0%

profile of v2, /device:TPU:24, one launch (start us, length us, event | category | flops | bytes accessed | tf_op | source)
XLA Modules:
  0.0 221.5 jit_solution(6392783109792832477)
XLA Ops:
  6.0 8.2 %collective-permute-start = (f32[2,8,128]{2,0,1:T(2,128)S(1)}, f32[2,8,128]{2,0,1:T(2,128)S(1)}, u32[]{:S(2)}, u32[]{:S(2)}) collective-permute-start(f32[2,8,128]{2,0,1:T(2,128)S(1)} %slice.244), channel_id=1, source_target_pairs={{1,0},{2,1},{3,2},{4,3},{5,4},{6,5},{7,6},{8,7},{9,8},{10,9},{11,1... | collective-permute-start | bytes 24584 | tf_op jit(solution)/shard_map/ppermute | solution.py:553
  20.6 10.2 %collective-permute-start.1 = (f32[34,8,128]{2,0,1:T(8,128)S(1)}, f32[34,8,128]{2,0,1:T(8,128)S(1)}, u32[]{:S(2)}, u32[]{:S(2)}) collective-permute-start(f32[34,8,128]{2,0,1:T(8,128)S(1)} %get-tuple-element.65), channel_id=1, source_target_pairs={{32,0},{64,32},{96,64},{128,96},{160,128},{192,160},{224,192},{256... | collective-permute-start | bytes 417800 | tf_op jit(solution)/shard_map/ppermute | solution.py:543
  30.9 11.2 %collective-permute-done.1 = f32[34,8,128]{2,0,1:T(8,128)S(1)} collective-permute-done((f32[34,8,128]{2,0,1:T(8,128)S(1)}, f32[34,8,128]{2,0,1:T(8,128)S(1)}, u32[]{:S(2)}, u32[]{:S(2)}) %collective-permute-start.1) | collective-permute-done | bytes 139296 | tf_op jit(solution)/shard_map/ppermute | solution.py:543
  49.8 27.5 %born_sums.1 = (f32[68,128]{1,0:T(8,128)}, f32[32,128,128]{2,1,0:T(8,128)}, f32[452,2,128,128]{3,2,1,0:T(8,128)}) custom-call(s32[2]{0:T(128)} %pad_add_fusion.4.total, s32[512]{0:T(512)} %broadcast_add_fusion.items, s32[2415]{0:T(1024)} %reshape.477.reach, f32[69,8,128]{2,1,0:T(8,128)} %copy.64.data), custom_call_target="tpu_custom_call" | custom-call | tf_op jit(solution)/shard_map/born_sums/pallas_call | solution.py:474
  78.1 12.8 %collective-permute-start.3 = (f32[4,128]{1,0:T(4,128)S(1)}, f32[4,128]{1,0:T(4,128)S(1)}, u32[]{:S(2)}, u32[]{:S(2)}) collective-permute-start(f32[4,128]{1,0:T(4,128)S(1)} %pad_maximum_fusion.10), channel_id=1, source_target_pairs={{1,0},{2,1},{3,2},{4,3},{5,4},{6,5},{7,6},{8,7},{9,8},{10,9},{11,1... | collective-permute-start | bytes 6152 | tf_op jit(solution)/shard_map/ppermute | solution.py:553
  90.9 1.9 collective-permute-start.2
  93.7 6.1 %collective-permute-done.2 = f32[4,128]{1,0:T(4,128)S(1)} collective-permute-done((f32[4,128]{1,0:T(4,128)S(1)}, f32[4,128]{1,0:T(4,128)S(1)}, u32[]{:S(2)}, u32[]{:S(2)}) %collective-permute-start.2) | collective-permute-done | bytes 2080 | tf_op jit(solution)/shard_map/ppermute | solution.py:558
  100.5 3.1 %collective-permute-start.4 = (f32[34,128]{1,0:T(8,128)S(1)}, f32[34,128]{1,0:T(8,128)S(1)}, u32[]{:S(2)}, u32[]{:S(2)}) collective-permute-start(f32[34,128]{1,0:T(8,128)S(1)} %pad_maximum_fusion.6), channel_id=1, source_target_pairs={{0,32},{32,64},{64,96},{96,128},{128,160},{160,192},{192,224},{224... | collective-permute-start | bytes 52232 | tf_op jit(solution)/shard_map/ppermute | solution.py:548
  103.6 7.4 %collective-permute-done.4 = f32[34,128]{1,0:T(8,128)S(1)} collective-permute-done((f32[34,128]{1,0:T(8,128)S(1)}, f32[34,128]{1,0:T(8,128)S(1)}, u32[]{:S(2)}, u32[]{:S(2)}) %collective-permute-start.4) | collective-permute-done | bytes 17440 | tf_op jit(solution)/shard_map/ppermute | solution.py:548
  111.0 1.9 collective-permute-start.5
  113.0 7.6 %collective-permute-done.5 = f32[34,128]{1,0:T(8,128)S(1)} collective-permute-done((f32[34,128]{1,0:T(8,128)S(1)}, f32[34,128]{1,0:T(8,128)S(1)}, u32[]{:S(2)}, u32[]{:S(2)}) %collective-permute-start.5) | collective-permute-done | bytes 17440 | tf_op jit(solution)/shard_map/ppermute | solution.py:543
  122.9 22.9 %radius_gradient.1 = (f32[68,128]{1,0:T(8,128)}, f32[69,3,8,128]{3,2,1,0:T(8,128)}) custom-call(s32[2]{0:T(128)} %pad_add_fusion.4.total, s32[512]{0:T(512)} %broadcast_add_fusion.items, s32[2415]{0:T(1024)} %reshape.477.reach, f32[69,8,128]{2,1,0:T(8,128)} %copy.64.data, f32[69,2,128]{2,1,0:T(2,128)} %select_maximum_fusion.born), custom_call_target="tpu_custom_call" | custom-call | tf_op jit(solution)/shard_map/radius_gradient/pallas_call | solution.py:492
  146.6 7.1 %collective-permute-start.7 = (f32[4,128]{1,0:T(4,128)S(1)}, f32[4,128]{1,0:T(4,128)S(1)}, u32[]{:S(2)}, u32[]{:S(2)}) collective-permute-start(f32[4,128]{1,0:T(4,128)S(1)} %pad_maximum_fusion.12), channel_id=1, source_target_pairs={{1,0},{2,1},{3,2},{4,3},{5,4},{6,5},{7,6},{8,7},{9,8},{10,9},{11,1... | collective-permute-start | bytes 6152 | tf_op jit(solution)/shard_map/ppermute | solution.py:553
  153.8 1.9 collective-permute-start.6
  155.7 6.9 %collective-permute-done.6 = f32[4,128]{1,0:T(4,128)S(1)} collective-permute-done((f32[4,128]{1,0:T(4,128)S(1)}, f32[4,128]{1,0:T(4,128)S(1)}, u32[]{:S(2)}, u32[]{:S(2)}) %collective-permute-start.6) | collective-permute-done | bytes 2080 | tf_op jit(solution)/shard_map/ppermute | solution.py:558
  162.6 1.9 collective-permute-start.9
  164.5 7.7 %collective-permute-done.9 = f32[34,128]{1,0:T(8,128)S(1)} collective-permute-done((f32[34,128]{1,0:T(8,128)S(1)}, f32[34,128]{1,0:T(8,128)S(1)}, u32[]{:S(2)}, u32[]{:S(2)}) %collective-permute-start.9) | collective-permute-done | bytes 17440 | tf_op jit(solution)/shard_map/ppermute | solution.py:543
  172.2 3.7 %collective-permute-start.8 = (f32[34,128]{1,0:T(8,128)S(1)}, f32[34,128]{1,0:T(8,128)S(1)}, u32[]{:S(2)}, u32[]{:S(2)}) collective-permute-start(f32[34,128]{1,0:T(8,128)S(1)} %get-tuple-element.95), channel_id=1, source_target_pairs={{0,32},{32,64},{64,96},{96,128},{128,160},{160,192},{192,224},{224... | collective-permute-start | bytes 52232 | tf_op jit(solution)/shard_map/ppermute | solution.py:548
  175.9 6.8 %collective-permute-done.8 = f32[34,128]{1,0:T(8,128)S(1)} collective-permute-done((f32[34,128]{1,0:T(8,128)S(1)}, f32[34,128]{1,0:T(8,128)S(1)}, u32[]{:S(2)}, u32[]{:S(2)}) %collective-permute-start.8) | collective-permute-done | bytes 17440 | tf_op jit(solution)/shard_map/ppermute | solution.py:548
  183.6 15.6 %forces.1 = f32[68,3,128]{2,1,0:T(4,128)} custom-call(s32[2]{0:T(128)} %pad_add_fusion.4.total, s32[512]{0:T(512)} %broadcast_add_fusion.items, s32[2415]{0:T(1024)} %reshape.477.reach, f32[69,8,128]{2,1,0:T(8,128)} %copy.64.data, f32[69,1,128]{2,1,0:T(1,128)} %pad.29.chain, f32[69,3,8,128]{3,2,1,0:T(8,128)} %get-tuple-element.10.force_in, ...), custom_call_target="tpu_custom_call" | custom-call | tf_op jit(solution)/shard_map/forces/pallas_call | solution.py:508
  200.1 1.9 collective-permute-start.10
  202.0 9.1 %collective-permute-done.10 = f32[34,3,128]{2,1,0:T(4,128)S(1)} collective-permute-done((f32[34,3,128]{2,1,0:T(4,128)S(1)}, f32[34,3,128]{2,1,0:T(4,128)S(1)}, u32[]{:S(2)}, u32[]{:S(2)}) %collective-permute-start.10) | collective-permute-done | bytes 52256 | tf_op jit(solution)/shard_map/ppermute | solution.py:548
  212.0 1.9 collective-permute-start.11
  214.5 6.3 %collective-permute-done.11 = f32[2,3,128]{2,1,0:T(4,128)S(1)} collective-permute-done((f32[2,3,128]{2,1,0:T(4,128)S(1)}, f32[2,3,128]{2,1,0:T(4,128)S(1)}, u32[]{:S(2)}, u32[]{:S(2)}) %collective-permute-start.11) | collective-permute-done | bytes 3104 | tf_op jit(solution)/shard_map/ppermute | solution.py:558
  (107 shorter events, 23.4 us)
Async XLA Ops:
  6.0 14.5 %collective-permute-start = (f32[2,8,128]{2,0,1:T(2,128)S(1)}, f32[2,8,128]{2,0,1:T(2,128)S(1)}, u32[]{:S(2)}, u32[]{:S(2)}) collective-permute-start(f32[2,8,128]{2,0,1:T(2,128)S(1)} %slice.244), channel_id=1, source_target_pairs={{1,0},{2,1},{3,2},{4,3},{5,4},{6,5},{7,6},{8,7},{9,8},{10,9},{11,1... | collective-permute-start | bytes 24584 | tf_op jit(solution)/shard_map/ppermute | solution.py:553
  20.6 21.5 %collective-permute-start.1 = (f32[34,8,128]{2,0,1:T(8,128)S(1)}, f32[34,8,128]{2,0,1:T(8,128)S(1)}, u32[]{:S(2)}, u32[]{:S(2)}) collective-permute-start(f32[34,8,128]{2,0,1:T(8,128)S(1)} %get-tuple-element.65), channel_id=1, source_target_pairs={{32,0},{64,32},{96,64},{128,96},{160,128},{192,160},{224,192},{256... | collective-permute-start | bytes 417800 | tf_op jit(solution)/shard_map/ppermute | solution.py:543
  78.1 15.6 %collective-permute-start.3 = (f32[4,128]{1,0:T(4,128)S(1)}, f32[4,128]{1,0:T(4,128)S(1)}, u32[]{:S(2)}, u32[]{:S(2)}) collective-permute-start(f32[4,128]{1,0:T(4,128)S(1)} %pad_maximum_fusion.10), channel_id=1, source_target_pairs={{1,0},{2,1},{3,2},{4,3},{5,4},{6,5},{7,6},{8,7},{9,8},{10,9},{11,1... | collective-permute-start | bytes 6152 | tf_op jit(solution)/shard_map/ppermute | solution.py:553
  90.9 8.8 %collective-permute-start.2 = (f32[4,128]{1,0:T(4,128)S(1)}, f32[4,128]{1,0:T(4,128)S(1)}, u32[]{:S(2)}, u32[]{:S(2)}) collective-permute-start(f32[4,128]{1,0:T(4,128)S(1)} %pad_maximum_fusion.9), channel_id=1, source_target_pairs={{0,1},{1,2},{2,3},{3,4},{4,5},{5,6},{6,7},{7,8},{8,9},{9,10},{10,1... | collective-permute-start | bytes 6152 | tf_op jit(solution)/shard_map/ppermute | solution.py:558
  100.5 10.5 %collective-permute-start.4 = (f32[34,128]{1,0:T(8,128)S(1)}, f32[34,128]{1,0:T(8,128)S(1)}, u32[]{:S(2)}, u32[]{:S(2)}) collective-permute-start(f32[34,128]{1,0:T(8,128)S(1)} %pad_maximum_fusion.6), channel_id=1, source_target_pairs={{0,32},{32,64},{64,96},{96,128},{128,160},{160,192},{192,224},{224... | collective-permute-start | bytes 52232 | tf_op jit(solution)/shard_map/ppermute | solution.py:548
  111.0 9.6 %collective-permute-start.5 = (f32[34,128]{1,0:T(8,128)S(1)}, f32[34,128]{1,0:T(8,128)S(1)}, u32[]{:S(2)}, u32[]{:S(2)}) collective-permute-start(f32[34,128]{1,0:T(8,128)S(1)} %get-tuple-element.97), channel_id=1, source_target_pairs={{32,0},{64,32},{96,64},{128,96},{160,128},{192,160},{224,192},{256... | collective-permute-start | bytes 52232 | tf_op jit(solution)/shard_map/ppermute | solution.py:543
  146.6 9.1 %collective-permute-start.7 = (f32[4,128]{1,0:T(4,128)S(1)}, f32[4,128]{1,0:T(4,128)S(1)}, u32[]{:S(2)}, u32[]{:S(2)}) collective-permute-start(f32[4,128]{1,0:T(4,128)S(1)} %pad_maximum_fusion.12), channel_id=1, source_target_pairs={{1,0},{2,1},{3,2},{4,3},{5,4},{6,5},{7,6},{8,7},{9,8},{10,9},{11,1... | collective-permute-start | bytes 6152 | tf_op jit(solution)/shard_map/ppermute | solution.py:553
  153.8 8.8 %collective-permute-start.6 = (f32[4,128]{1,0:T(4,128)S(1)}, f32[4,128]{1,0:T(4,128)S(1)}, u32[]{:S(2)}, u32[]{:S(2)}) collective-permute-start(f32[4,128]{1,0:T(4,128)S(1)} %pad_maximum_fusion.11), channel_id=1, source_target_pairs={{0,1},{1,2},{2,3},{3,4},{4,5},{5,6},{6,7},{7,8},{8,9},{9,10},{10,1... | collective-permute-start | bytes 6152 | tf_op jit(solution)/shard_map/ppermute | solution.py:558
  162.6 9.6 %collective-permute-start.9 = (f32[34,128]{1,0:T(8,128)S(1)}, f32[34,128]{1,0:T(8,128)S(1)}, u32[]{:S(2)}, u32[]{:S(2)}) collective-permute-start(f32[34,128]{1,0:T(8,128)S(1)} %pad_maximum_fusion.7), channel_id=1, source_target_pairs={{32,0},{64,32},{96,64},{128,96},{160,128},{192,160},{224,192},{256... | collective-permute-start | bytes 52232 | tf_op jit(solution)/shard_map/ppermute | solution.py:543
  172.2 10.5 %collective-permute-start.8 = (f32[34,128]{1,0:T(8,128)S(1)}, f32[34,128]{1,0:T(8,128)S(1)}, u32[]{:S(2)}, u32[]{:S(2)}) collective-permute-start(f32[34,128]{1,0:T(8,128)S(1)} %get-tuple-element.95), channel_id=1, source_target_pairs={{0,32},{32,64},{64,96},{96,128},{128,160},{160,192},{192,224},{224... | collective-permute-start | bytes 52232 | tf_op jit(solution)/shard_map/ppermute | solution.py:548
  200.1 11.0 %collective-permute-start.10 = (f32[34,3,128]{2,1,0:T(4,128)S(1)}, f32[34,3,128]{2,1,0:T(4,128)S(1)}, u32[]{:S(2)}, u32[]{:S(2)}) collective-permute-start(f32[34,3,128]{2,1,0:T(4,128)S(1)} %slice.284), channel_id=1, source_target_pairs={{0,32},{32,64},{64,96},{96,128},{128,160},{160,192},{192,224},{224... | collective-permute-start | bytes 156680 | tf_op jit(solution)/shard_map/ppermute | solution.py:548
  212.0 8.8 %collective-permute-start.11 = (f32[2,3,128]{2,1,0:T(4,128)S(1)}, f32[2,3,128]{2,1,0:T(4,128)S(1)}, u32[]{:S(2)}, u32[]{:S(2)}) collective-permute-start(f32[2,3,128]{2,1,0:T(4,128)S(1)} %slice.286), channel_id=1, source_target_pairs={{0,1},{1,2},{2,3},{3,4},{4,5},{5,6},{6,7},{7,8},{8,9},{9,10},{10,1... | collective-permute-start | bytes 9224 | tf_op jit(solution)/shard_map/ppermute | solution.py:558

commit v3 on v2

--- a/solution.py
+++ b/solution.py
@@ -18,10 +18,11 @@
 
 TILES = 32
 EDGE = 2
-HALF = TILES + EDGE
+LIVE = TILES + EDGE
+HALF = 40
 REGION = 2 * HALF
-OWN_ROWS = HALF + 1
-ALL_ROWS = REGION + 1
+OWN_ROWS = LIVE + 1
+SENT_ROWS = 6 * TILES + 8
 LISTED = 7
 ATOMS = 128
 CHUNK = 16
@@ -33,7 +34,7 @@
 SELF_WIDTH = 4
 PAIRS = 2 * TILES * LISTED + 4
 ITEMS = 512
-DUMMY = HALF * ATOMS + REGION
+DUMMY = LIVE * ATOMS + LIVE
 ROW = (1, ATOMS)
 LANES = (8, ATOMS)
 ROWS = (CHUNK, ATOMS)
@@ -44,7 +45,8 @@
 CUT = 8.0
 EXP_SCALE = math.sqrt(0.25 / math.log(2.0)) / SCALE
 
-ROW_X, ROW_Y, ROW_Z, ROW_Q, ROW_IN, ROW_SCALED, ROW_RADIUS, ROW_CODE = range(8)
+ROW_X, ROW_Y, ROW_Z, ROW_Q, ROW_IN, ROW_SCALED = range(6)
+AT_Q, AT_RADIUS, AT_SCALED = 3, 4, 5
 
 F32 = jnp.float32
 
@@ -63,12 +65,12 @@
 
 def by_fours(step):
     def fours(index, carry):
-        start = jnp.minimum(index * 4, HALF - 4)
+        start = jnp.minimum(index * 4, LIVE - 4)
         for k in range(4):
             step(start + k)
         return carry
 
-    lax.fori_loop(0, (HALF + 3) // 4, fours, 0)
+    lax.fori_loop(0, (LIVE + 3) // 4, fours, 0)
 
 
 def fill_table(table, tile, first, ref, rows, factor=None):
@@ -87,16 +89,8 @@
         return carry
 
     lax.fori_loop(0, TILES // 4, fours, 0)
-    for tile in range(TILES, HALF):
+    for tile in range(TILES, LIVE):
         target[(tile,) + index] += fold_own(own[(tile,) + index])
-
-
-def clear(ref):
-    def step(tile, carry):
-        ref[tile] = jnp.zeros(ref.shape[1:], F32)
-        return carry
-
-    lax.fori_loop(0, ref.shape[0], step, 0)
 
 
 def diagonal(start):
@@ -154,11 +148,64 @@
     return copy
 
 
-def born_kernel(total, items, reach, data, part, d_self, d_pair, table, own, far, rings, sems):
+def edge_rows(target, values, first, second):
+    target[...] = jnp.zeros_like(target)
+    target[0:EDGE, :] = values[first : first + EDGE]
+    target[EDGE : 2 * EDGE, :] = values[second : second + EDGE]
+
+
+def pack_kernel(positions, charges, radii, scales, neighbours, pad_mask, sent, edges, here):
+    radius = radii[...]
+    values = [positions[0], positions[1], positions[2], charges[...], radius, scales[...] * (radius - radius_offset)]
+    edges[...] = jnp.zeros_like(edges)
+    for index, value in enumerate(values):
+        sent[index * TILES : (index + 1) * TILES, :] = value
+        edges[EDGE * index : EDGE * (index + 1), :] = value[0:EDGE]
+    cycle_count = lax.axis_size("tile")
+    cycle_tiles = cycle_count * TILES
+    listed = neighbours[...]
+    slab_step = lax.div(listed, cycle_tiles) - lax.axis_index("slab")
+    within = lax.rem(listed, cycle_tiles)
+    cycle_step = lax.rem(lax.div(within, TILES) - lax.axis_index("tile") + cycle_count, cycle_count)
+    place = cycle_step * TILES + lax.rem(within, TILES)
+    slots = lax.broadcasted_iota(jnp.int32, listed.shape, 0)
+    live = (pad_mask[...] == 1) & (slots > 0)
+    here[...] = jnp.where(live & (slab_step >= 0), slab_step * HALF + place, -1)
+    sent[6 * TILES :, :] = jnp.full(LANES, -1.0, F32)
+    sent[6 * TILES :, 0:TILES] = jnp.where(live & (slab_step < 0), place, -1).astype(F32)
+
+
+def born_kernel(
+    total, items, reach, sent, edges, above, above_edges,
+    own_part, above_part, to_next, to_last, data, plain, d_self, d_pair,
+    table, own, far, rings, sems,
+):
     full_ring, part_ring, self_ring = rings
     full_sems, part_sems, self_sems = sems
     far[...] = jnp.zeros_like(far)
+    data[...] = jnp.zeros_like(data)
+    plain[...] = jnp.ones_like(plain)
     fulls, parts = total[0], total[1]
+
+    for index in range(6):
+        origin = sent[index * TILES + TILES // 2 : index * TILES + TILES // 2 + 1, 0:1]
+        for start, source, edge in ((0, sent, edges), (HALF, above, above_edges)):
+            for place, values in (
+                (start, source[index * TILES : (index + 1) * TILES, :]),
+                (start + TILES, edge[EDGE * index : EDGE * (index + 1), :]),
+            ):
+                rows = slice(place, place + values.shape[0])
+                if index < AT_Q:
+                    data[rows, index, :] = (values - origin) * SCALE
+                elif index == AT_Q:
+                    data[rows, ROW_Q, :] = values
+                    plain[2, rows, :] = values if place == 0 else jnp.zeros_like(values)
+                elif index == AT_RADIUS:
+                    data[rows, ROW_IN, :] = (values - radius_offset) * SCALE
+                    plain[0, rows, :] = values
+                    plain[1, rows, :] = values - radius_offset
+                else:
+                    data[rows, ROW_SCALED, :] = values * SCALE
 
     def prepare(tile):
         fill_table(table, tile, 0, data, (ROW_X, ROW_Y, ROW_Z, ROW_IN, ROW_SCALED))
@@ -247,22 +294,37 @@
         lax.fori_loop(0, jnp.minimum(number, size), wait, 0)
 
     def listed_starts(item):
-        return part_starts(reach[item[0] * ALL_ROWS + item[1]])
+        return part_starts(reach[item[0] * REGION + item[1]])
 
     run(FULL_WIDTH, FULL_RING, full_ring, full_sems, 0, fulls, ATOMS, lambda item: range(0, ATOMS, CHUNK))
     run(PART_WIDTH, PART_RING, part_ring, part_sems, fulls, parts, PART, listed_starts)
     fold_rows(own, far, ())
-    part[...] = jnp.sum(far[0:REGION], axis=1) * (0.125 * SCALE)
+    sums = jnp.sum(far[...], axis=1) * (0.125 * SCALE)
+    own_part[...] = sums[0:HALF]
+    above_part[...] = sums[HALF:]
+    edge_rows(to_next, sums, TILES, HALF + TILES)
+    edge_rows(to_last, sums, 0, HALF)
     for tile in range(TILES):
         self_copy(tile).wait()
     drain(FULL_RING, full_ring, full_sems, fulls, ATOMS)
     drain(PART_RING, part_ring, part_sems, parts, PART)
 
 
-def energy_kernel(total, items, reach, data, born, part, force, table, own, far):
+def energy_kernel(
+    total, items, reach, data, plain, own_part, above_part, from_below, from_above,
+    radii_born, slope, own_grad, above_grad, to_next, to_last, force,
+    table, own, far, born,
+):
     far[...] = jnp.zeros_like(far)
     force[...] = jnp.zeros_like(force)
     fulls, parts = total[0], total[1]
+    sums = jnp.concatenate([own_part[...] + from_below[...], above_part[...] + from_above[...]])
+    all_radii, all_slopes = born_radius(sums, plain[0], plain[1])
+    inverse = 1.0 / all_radii
+    radii_born[...] = all_radii[0:TILES]
+    slope[...] = all_slopes
+    born[:, 0, :] = SCALE * all_radii
+    born[:, 1, :] = EXP_SCALE * inverse
 
     def prepare(tile):
         fill_table(table, tile, 0, data, (ROW_X, ROW_Y, ROW_Z, ROW_Q))
@@ -319,7 +381,7 @@
     def part_step(index, carry):
         for k in range(PART_WIDTH):
             first, second = decode(items[fulls + index * PART_WIDTH + k])
-            pair(first, second, part_starts(reach[first * ALL_ROWS + second]), False)
+            pair(first, second, part_starts(reach[first * REGION + second]), False)
         return carry
 
     lax.fori_loop(0, lax.div(fulls, FULL_WIDTH), full_step, 0)
@@ -333,14 +395,22 @@
                 force[tile, axis] += fold_own(own[tile, 1 + axis])
         return carry
 
-    lax.fori_loop(0, HALF // 2, fold_step, 0)
-    part[...] = jnp.sum(far[0:REGION], axis=1) * (0.5 * SCALE)
-
-
-def force_kernel(total, items, reach, data, chain, force_in, d_self, d_pair, force, table, own, far, rings, sems):
+    lax.fori_loop(0, LIVE // 2, fold_step, 0)
+    charge = plain[2] * inverse
+    sums = jnp.sum(far[...], axis=1) * (0.5 * SCALE) * inverse + 0.5 * charge * charge
+    own_grad[...] = sums[0:HALF]
+    above_grad[...] = sums[HALF:]
+    edge_rows(to_next, sums, TILES, HALF + TILES)
+    edge_rows(to_last, sums, 0, HALF)
+
+
+def force_kernel(
+    total, items, reach, data, slope, own_grad, above_grad, from_below, from_above, force_in, d_self, d_pair,
+    gradient, own_force, above_force, to_next,
+    table, own, far, chain, rings, sems,
+):
     full_ring, part_ring, self_ring = rings
     full_sems, part_sems, self_sems = sems
-    far[...] = force_in[...] * 4.0
     fulls, parts = total[0], total[1]
     full_copy = ring_copies(full_ring, d_pair, full_sems, FULL_RING, ATOMS)
     part_copy = ring_copies(part_ring, d_pair, part_sems, PART_RING, PART)
@@ -359,6 +429,11 @@
         self_copy(tile).start()
     lax.fori_loop(0, jnp.minimum(fulls, FULL_RING), start(full_copy, 0), 0)
     lax.fori_loop(0, jnp.minimum(parts, PART_RING), start(part_copy, fulls), 0)
+
+    far[...] = force_in[...] * 4.0
+    grads = jnp.concatenate([own_grad[...] + from_below[...], above_grad[...] + from_above[...]])
+    gradient[...] = grads[0:TILES]
+    chain[:, 0, :] = grads * slope[...]
 
     def prepare(tile):
         fill_table(table, tile, 0, data, (ROW_X, ROW_Y, ROW_Z))
@@ -436,7 +511,7 @@
         part_copy,
         fulls,
         parts,
-        lambda first, second: part_starts(reach[first * ALL_ROWS + second]),
+        lambda first, second: part_starts(reach[first * REGION + second]),
     )
 
     def fold_step(pairs, carry):
@@ -446,8 +521,12 @@
                 far[tile, axis] += fold_own(own[tile, axis])
         return carry
 
-    lax.fori_loop(0, HALF // 2, fold_step, 0)
-    force[...] = jnp.sum(far[0:REGION], axis=2) * (-SCALE * SCALE / 16.0)
+    lax.fori_loop(0, LIVE // 2, fold_step, 0)
+    for axis in range(3):
+        sums = jnp.sum(far[:, axis], axis=1) * (-SCALE * SCALE / 16.0)
+        own_force[axis] = sums[0:HALF]
+        above_force[axis] = sums[HALF:]
+        edge_rows(to_next.at[axis], sums, TILES, HALF + TILES)
 
 
 SMEM = pl.BlockSpec(memory_space=pltpu.SMEM)
@@ -470,56 +549,90 @@
     return jax.ShapeDtypeStruct(shape, F32)
 
 
-def run_born(total, items, reach, data):
+def run_pack(positions, charges, radii, scales, neighbours, pad_mask):
+    return pl.pallas_call(
+        pack_kernel,
+        name="pack_atoms",
+        out_shape=(
+            f32(SENT_ROWS, ATOMS),
+            f32(16, ATOMS),
+            jax.ShapeDtypeStruct(neighbours.shape, jnp.int32),
+        ),
+        in_specs=[VMEM] * 6,
+        out_specs=(VMEM,) * 3,
+        compiler_params=PARAMS,
+    )(positions, charges, radii, scales, neighbours, pad_mask)
+
+
+def run_born(total, items, reach, sent, edges, above, above_edges):
     return pl.pallas_call(
         born_kernel,
         name="born_sums",
-        out_shape=(f32(REGION, ATOMS), f32(TILES, *BLOCK), f32(PAIRS, 2, *BLOCK)),
-        in_specs=[SMEM, SMEM, SMEM, VMEM],
-        out_specs=(VMEM, ANY, ANY),
+        out_shape=(
+            f32(HALF, ATOMS),
+            f32(HALF, ATOMS),
+            f32(*LANES),
+            f32(*LANES),
+            f32(REGION, *LANES),
+            f32(3, REGION, ATOMS),
+            f32(TILES, *BLOCK),
+            f32(PAIRS, 2, *BLOCK),
+        ),
+        in_specs=[SMEM] * 3 + [VMEM] * 4,
+        out_specs=(VMEM,) * 6 + (ANY,) * 2,
         scratch_shapes=[
             pltpu.VMEM((OWN_ROWS, 5) + BLOCK, F32),
             pltpu.VMEM((OWN_ROWS,) + BLOCK, F32),
-            pltpu.VMEM((ALL_ROWS,) + LANES, F32),
+            pltpu.VMEM((REGION,) + LANES, F32),
             RING_BLOCKS,
             RING_SEMS,
         ],
         compiler_params=PARAMS,
-    )(total, items, reach, data)
-
-
-def run_energy(total, items, reach, data, born):
+    )(total, items, reach, sent, edges, above, above_edges)
+
+
+def run_energy(total, items, reach, data, plain, shares):
     return pl.pallas_call(
         energy_kernel,
         name="radius_gradient",
-        out_shape=(f32(REGION, ATOMS), f32(ALL_ROWS, 3, *LANES)),
-        in_specs=[SMEM, SMEM, SMEM, VMEM, VMEM],
-        out_specs=(VMEM, VMEM),
+        out_shape=(
+            f32(TILES, ATOMS),
+            f32(REGION, ATOMS),
+            f32(HALF, ATOMS),
+            f32(HALF, ATOMS),
+            f32(*LANES),
+            f32(*LANES),
+            f32(REGION, 3, *LANES),
+        ),
+        in_specs=[SMEM] * 3 + [VMEM] * 6,
+        out_specs=(VMEM,) * 7,
         scratch_shapes=[
             pltpu.VMEM((OWN_ROWS, 6) + BLOCK, F32),
             pltpu.VMEM((OWN_ROWS, 4) + BLOCK, F32),
-            pltpu.VMEM((ALL_ROWS,) + LANES, F32),
+            pltpu.VMEM((REGION,) + LANES, F32),
+            pltpu.VMEM((REGION,) + LANES, F32),
         ],
         compiler_params=PARAMS,
-    )(total, items, reach, data, born)
-
-
-def run_force(total, items, reach, data, chain, force_in, d_self, d_pair):
+    )(total, items, reach, data, plain, *shares)
+
+
+def run_force(total, items, reach, data, slope, shares, force_in, d_self, d_pair):
     return pl.pallas_call(
         force_kernel,
         name="forces",
-        out_shape=f32(REGION, 3, ATOMS),
-        in_specs=[SMEM, SMEM, SMEM, VMEM, VMEM, VMEM, ANY, ANY],
-        out_specs=VMEM,
+        out_shape=(f32(TILES, ATOMS), f32(3, HALF, ATOMS), f32(3, HALF, ATOMS), f32(3, *LANES)),
+        in_specs=[SMEM] * 3 + [VMEM] * 7 + [ANY] * 2,
+        out_specs=(VMEM,) * 4,
         scratch_shapes=[
             pltpu.VMEM((OWN_ROWS, 4) + BLOCK, F32),
             pltpu.VMEM((OWN_ROWS, 3) + BLOCK, F32),
-            pltpu.VMEM((ALL_ROWS, 3) + LANES, F32),
+            pltpu.VMEM((REGION, 3) + LANES, F32),
+            pltpu.VMEM((REGION,) + LANES, F32),
             RING_BLOCKS,
             RING_SEMS,
         ],
         compiler_params=PARAMS,
-    )(total, items, reach, data, chain, force_in, d_self, d_pair)
+    )(total, items, reach, data, slope, *shares, force_in, d_self, d_pair)
 
 
 def born_radius(descreen_sum, radius, radius_in):
@@ -558,53 +671,52 @@
     return lax.ppermute(block, "tile", [(i, (i + 1) % count) for i in range(count)])
 
 
-def swap_sums(part):
-    to_next = jnp.concatenate([part[TILES:HALF], part[HALF + TILES :]])
-    to_last = jnp.concatenate([part[0:EDGE], part[HALF : HALF + EDGE]])
+def across_to_here(block):
+    slabs, count = lax.axis_size("slab"), lax.axis_size("tile")
+    pairs = [
+        ((slab + 1) * count + (tile + 1) % count, slab * count + tile)
+        for slab in range(slabs - 1)
+        for tile in range(count)
+    ]
+    return lax.ppermute(block, ("slab", "tile"), pairs)
+
+
+def placed(block, first, last):
+    return jnp.pad(block[first : first + EDGE], ((0, HALF - EDGE), (0, 0))) + jnp.pad(
+        last[first : first + EDGE], ((TILES, HALF - LIVE), (0, 0))
+    )
+
+
+def swap_sums(own, above, to_next, to_last):
     from_last = here_to_next(to_next)
     from_next = next_to_here(to_last)
-    column = jnp.concatenate(
-        [
-            part[0:EDGE] + from_last[0:EDGE],
-            part[EDGE:TILES],
-            part[TILES:HALF] + from_next[0:EDGE],
-            part[HALF : HALF + EDGE] + from_last[EDGE:],
-            part[HALF + EDGE : HALF + TILES],
-            part[HALF + TILES :] + from_next[EDGE:],
-        ]
+    own = own + placed(from_last, 0, from_next)
+    above = above + placed(from_last, EDGE, from_next)
+    own, above = lax.optimization_barrier((own, above))
+    return own, above, here_to_above(above), above_to_here(own)
+
+
+def whole_slab(component, block, edges):
+    first, edge = component * TILES, component * EDGE
+    return [block[first : first + TILES], edges[edge : edge + EDGE], jnp.zeros((HALF - LIVE, ATOMS), F32)]
+
+
+def chunk_reach(sent, edges, above, above_edges):
+    x, y, z = (
+        jnp.concatenate(whole_slab(axis, sent, edges) + whole_slab(axis, above, above_edges)) for axis in range(3)
     )
-    own, above = column[0:HALF], column[HALF:]
-    from_below = here_to_above(above)
-    from_above = above_to_here(own)
-    return jnp.concatenate([own + from_below, above + from_above])
-
-
-def pair_lists(neighbours, pad_mask):
-    cycle_count = lax.axis_size("tile")
-    cycle_tiles = cycle_count * TILES
-    slab_step = neighbours // cycle_tiles - lax.axis_index("slab")
-    within = neighbours % cycle_tiles
-    cycle_step = (within // TILES - lax.axis_index("tile")) % cycle_count
-    place = cycle_step * TILES + within % TILES
-    live = (pad_mask == 1) & (jnp.arange(neighbours.shape[1]) > 0)[None, :]
-    here = jnp.where(live & (slab_step >= 0), slab_step * HALF + place, -1)
-    below = jnp.where(live & (slab_step < 0), place, -1)
-    return here, below
-
-
-def chunk_reach(data, across, along):
+    across, along = sent[TILES // 2, 0], sent[TILES + TILES // 2, 0]
     inverse = lax.rsqrt(across * across + along * along)
     across, along = across * inverse, along * inverse
-    x, y, z = data[:, ROW_X], data[:, ROW_Y], data[:, ROW_Z]
     turned = jnp.stack([x * across + y * along, y * across - x * along, z])
     pieces = turned.reshape(3, REGION, CHUNKS, CHUNK)
     low, high = jnp.min(pieces, axis=3), jnp.max(pieces, axis=3)
     tile_low, tile_high = jnp.min(low, axis=2), jnp.max(high, axis=2)
     near = []
     for chunk in range(CHUNKS):
-        own_low, own_high = low[:, :HALF, chunk, None], high[:, :HALF, chunk, None]
+        own_low, own_high = low[:, :OWN_ROWS, chunk, None], high[:, :OWN_ROWS, chunk, None]
         gap = jnp.maximum(jnp.maximum(tile_low[:, None, :] - own_high, own_low - tile_high[:, None, :]), 0.0)
-        far = jnp.sum(gap * gap, axis=0) >= CUT * 1.001
+        far = jnp.sum(gap * gap, axis=0) >= cutoff_sq * 1.001
         near.append(jnp.logical_not(far).astype(jnp.int32))
     number = sum(near)
     code = number << (3 * CHUNKS)
@@ -613,14 +725,12 @@
         rank = jnp.where(near[chunk] == 1, before, number + chunk - before)
         code = code + (chunk << (3 * rank))
         before = before + near[chunk]
-    is_part = number <= CHUNKS // 2
-    edge = ((0, OWN_ROWS - HALF), (0, ALL_ROWS - REGION))
-    return jnp.pad(code, edge).reshape(-1), is_part
+    return code.reshape(-1), number <= CHUNKS // 2
 
 
 def packed(first, second, valid, is_part):
     first, second, valid = first.reshape(-1), second.reshape(-1), valid.reshape(-1)
-    mine = (first[:, None] == jnp.arange(HALF)[None, :]).astype(jnp.bfloat16)
+    mine = (first[:, None] == jnp.arange(OWN_ROWS)[None, :]).astype(jnp.bfloat16)
     rows = jnp.dot(mine, is_part.astype(jnp.bfloat16), preferred_element_type=F32)
     in_part = jnp.sum(jnp.where(second[:, None] == jnp.arange(REGION)[None, :], rows, 0.0), axis=1) > 0.5
     entry = jnp.arange(valid.shape[0])
@@ -637,54 +747,44 @@
     return jnp.stack([fulls, parts]), items.astype(jnp.int32)
 
 
-def region_data(own, above):
-    origin = jnp.pad(own[TILES // 2, 0:3, 0:1], ((0, 5), (0, 0)))
-    factor = np.ones((1, 8, 1), np.float32)
-    factor[0, [ROW_X, ROW_Y, ROW_Z, ROW_IN, ROW_SCALED]] = SCALE
-    return jnp.concatenate([own - origin, above - origin, jnp.zeros_like(own[0:1])]) * factor
-
-
-def body(positions, charges, radii, scales, neighbours, pad_mask):
-    coords = positions[0, 0]
-    charge = charges[0, 0]
-    radius = radii[0, 0]
-    radius_in = radius - radius_offset
-    here, below = pair_lists(neighbours[0, 0], pad_mask[0, 0])
-    code = jnp.pad(below.astype(jnp.float32), ((0, 0), (0, ATOMS - below.shape[1])))
-    own = jnp.concatenate(
-        [coords, jnp.stack([charge, radius_in, scales[0, 0] * radius_in, radius, code], axis=1)], axis=1
-    )
-    own = jnp.concatenate([own, next_to_here(own[0:EDGE])])
-    above = above_to_here(own)
-    data = region_data(own, above)
-    listed_above = above[0:TILES, ROW_CODE, 0 : below.shape[1]].astype(jnp.int32)
+def pair_items(here, above, is_part):
+    listed = above[6 * TILES :, 0:TILES].astype(jnp.int32)
     has_above = lax.axis_index("slab") < lax.axis_size("slab") - 1
-    tiles = jnp.broadcast_to(jnp.arange(TILES, dtype=jnp.int32)[:, None], here.shape)
-    reach, is_part = chunk_reach(data[0:REGION], coords[TILES // 2, 0, 0], coords[TILES // 2, 1, 0])
-    total, items = packed(
-        jnp.concatenate([tiles, listed_above]),
+    tiles = lax.broadcasted_iota(jnp.int32, here.shape, 1)
+    return packed(
+        jnp.concatenate([tiles, listed]),
         jnp.concatenate([here, HALF + tiles]),
-        jnp.concatenate([here >= 0, (listed_above >= 0) & has_above]),
+        jnp.concatenate([here >= 0, (listed >= 0) & has_above]),
         is_part,
     )
-    region_radius = jnp.concatenate([own[:, ROW_RADIUS], above[:, ROW_RADIUS]])
-    region_in = jnp.concatenate([own[:, ROW_IN], above[:, ROW_IN]])
-
-    part, d_self, d_pair = run_born(total, items, reach, data)
-    radii_born, radius_slope = born_radius(swap_sums(part), region_radius, region_in)
-    inverse = 1.0 / radii_born
-    born = jnp.stack([SCALE * radii_born, EXP_SCALE * inverse], axis=1)
-    part, force = run_energy(total, items, reach, data, jnp.pad(born, ((0, 1), (0, 0), (0, 0))))
-    own_charge = charge * inverse[0:TILES]
-    part = part * inverse + jnp.pad(0.5 * own_charge * own_charge, ((0, REGION - TILES), (0, 0)))
-    gradient = swap_sums(part)
-    chain = jnp.pad((gradient * radius_slope)[:, None], ((0, 1), (0, 0), (0, 0)))
-    force = run_force(total, items, reach, data, chain, force, d_self, d_pair)
-    back = here_to_above(force[HALF:])
-    mine = force[0:HALF] + back
-    last = here_to_next(mine[TILES:])
-    forces = jnp.concatenate([mine[0:EDGE] + last, mine[EDGE:TILES]])
-    return (radii_born[None, None, 0:TILES], gradient[None, None, 0:TILES], forces[None, None])
+
+
+def body(positions, charges, radii, scales, neighbours, pad_mask):
+    sent, edges, here = run_pack(
+        jnp.swapaxes(positions[0, 0], 0, 1),
+        charges[0, 0],
+        radii[0, 0],
+        scales[0, 0],
+        neighbours[0, 0].T,
+        pad_mask[0, 0].T,
+    )
+    above = above_to_here(sent)
+    next_edges = next_to_here(edges)
+    above_edges = across_to_here(edges)
+    reach, is_part = chunk_reach(sent, next_edges, above, above_edges)
+    total, items = pair_items(here, above, is_part)
+
+    *parts, data, plain, d_self, d_pair = run_born(total, items, reach, sent, next_edges, above, above_edges)
+    shares = swap_sums(*parts)
+    radii_born, slope, *parts, force = run_energy(total, items, reach, data, plain, shares)
+    shares = swap_sums(*parts)
+    gradient, own, over, to_next = run_force(total, items, reach, data, slope, shares, force, d_self, d_pair)
+    from_last = here_to_next(to_next)
+    edge = ((0, 0), (0, TILES - EDGE), (0, 0))
+    over = over[:, 0:TILES] + jnp.pad(from_last[:, EDGE : 2 * EDGE], edge)
+    own = own[:, 0:TILES] + jnp.pad(from_last[:, 0:EDGE], edge)
+    forces = own + here_to_above(over)
+    return (radii_born[None, None], gradient[None, None], jnp.swapaxes(forces, 0, 1)[None, None])
 
 
 def solution(mesh):

time: 223 us -> 202 us (0.906)
  the two profiles are of different devices: /device:TPU:24 before, /device:TPU:48 now
where the time goes in v3:
time: 202 us; the launch traced here: 201 us
  Pallas kernels  92.1 us (46%)
  starting transfers between devices  64.4 us (32%)
  waiting for transfers between devices  22 us (11%)
  other arithmetic  10.2 us (5%)
  between operations  6.51 us (3%)
  local copies, waits for them, and re-layouts  5.41 us (3%)
    pallas_call x1, Pallas kernels, run_born(): pl.pallas_call(born_kernel, name='born_sums', out_shape=(f32(HALF, ATOMS)...  40.4 us
    pallas_call x1, Pallas kernels, run_energy(): pl.pallas_call(energy_kernel, name='radius_gradient', out_shape=(f32(TILE...  31.1 us
    ppermute x3, starting transfers between devices, here_to_above(): return lax.ppermute(block, 'slab', [(i, i + 1) for i in range(ends)])  21.3 us
    pallas_call x1, Pallas kernels, run_force(): pl.pallas_call(force_kernel, name='forces', out_shape=(f32(TILES, ATOMS),...  19.2 us
    ppermute x3, starting transfers between devices, next_to_here(): lax.ppermute(block, 'tile', [((i + 1) % count, i) for i in range(count)])  14.3 us
    ppermute x1, starting transfers between devices, across_to_here(): return lax.ppermute(block, ('slab', 'tile'), pairs)  13.8 us
    ppermute x3, waiting for transfers between devices, here_to_above(): return lax.ppermute(block, 'slab', [(i, i + 1) for i in range(ends)])  10.4 us
    ppermute x3, starting transfers between devices, above_to_here(): return lax.ppermute(block, 'slab', [(i + 1, i) for i in range(ends)])  9.28 us
  transfers between devices with their start and end apart: 13, of which 7 were waited for; matrix products, arithmetic and copies ran while one was open for 2% of the time, Pallas kernels for 0%

profile of v3, /device:TPU:48, one launch (start us, length us, event | category | flops | bytes accessed | tf_op | source)
XLA Modules:
  0.0 201.0 jit_solution(11355412652642793601)
XLA Ops:
  0.6 1.5 pack_atoms.1
  2.1 13.8 %collective-permute-start.2 = (f32[16,128]{1,0:T(8,128)}, f32[16,128]{1,0:T(8,128)S(1)}, u32[]{:S(2)}, u32[]{:S(2)}) collective-permute-start(f32[16,128]{1,0:T(8,128)} %get-tuple-element.31), channel_id=1, source_target_pairs={{33,0},{34,1},{35,2},{36,3},{37,4},{38,5},{39,6},{40,7},{41,8},{42... | collective-permute-start | bytes 24584 | tf_op jit(solution)/shard_map/ppermute | solution.py:681
  15.9 2.8 %collective-permute-start.1 = (f32[16,128]{1,0:T(8,128)}, f32[16,128]{1,0:T(8,128)S(1)}, u32[]{:S(2)}, u32[]{:S(2)}) collective-permute-start(f32[16,128]{1,0:T(8,128)} %get-tuple-element.31), channel_id=1, source_target_pairs={{1,0},{2,1},{3,2},{4,3},{5,4},{6,5},{7,6},{8,7},{9,8},{10,9},{11,1... | collective-permute-start | bytes 24584 | tf_op jit(solution)/shard_map/ppermute | solution.py:666
  18.7 5.5 %collective-permute-start = (f32[200,128]{1,0:T(8,128)}, f32[200,128]{1,0:T(8,128)S(1)}, u32[]{:S(2)}, u32[]{:S(2)}) collective-permute-start(f32[200,128]{1,0:T(8,128)} %get-tuple-element.30.sent), channel_id=1, source_target_pairs={{32,0},{64,32},{96,64},{128,96},{160,128},{192,160},{224,192},{256... | collective-permute-start | bytes 307208 | tf_op jit(solution)/shard_map/ppermute | solution.py:656
  32.2 3.2 %collective-permute-done.above = f32[200,128]{1,0:T(8,128)S(1)} collective-permute-done((f32[200,128]{1,0:T(8,128)}, f32[200,128]{1,0:T(8,128)S(1)}, u32[]{:S(2)}, u32[]{:S(2)}) %collective-permute-start) | collective-permute-done | bytes 102432 | tf_op jit(solution)/shard_map/ppermute | solution.py:656
  42.6 40.4 %born_sums.1 = (f32[40,128]{1,0:T(8,128)}, f32[40,128]{1,0:T(8,128)}, f32[8,128]{1,0:T(8,128)}, f32[8,128]{1,0:T(8,128)}, f32[80,8,128]{2,1,0:T(8,128)}, /*index...) custom-call(s32[2]{0:T(128)} %pad_add_fusion.4.total, s32[512]{0:T(512)} %broadcast_add_fusion.items, ...), custom_call_target="tpu_custom_call" | custom-call | tf_op jit(solution)/shard_map/born_sums/pallas_call | solution.py:568
  83.0 1.9 collective-permute-start.3
  84.9 5.8 %collective-permute-start.4 = (f32[8,128]{1,0:T(8,128)}, f32[8,128]{1,0:T(8,128)S(1)}, u32[]{:S(2)}, u32[]{:S(2)}) collective-permute-start(f32[8,128]{1,0:T(8,128)} %get-tuple-element.36), channel_id=1, source_target_pairs={{1,0},{2,1},{3,2},{4,3},{5,4},{6,5},{7,6},{8,7},{9,8},{10,9},{11,1... | collective-permute-start | bytes 12296 | tf_op jit(solution)/shard_map/ppermute | solution.py:666
  90.7 1.5 collective-permute-done.4
  93.7 1.9 collective-permute-start.6
  95.6 7.8 %collective-permute-start.5 = (f32[40,128]{1,0:T(8,128)S(1)}, f32[40,128]{1,0:T(8,128)S(1)}, u32[]{:S(2)}, u32[]{:S(2)}) collective-permute-start(f32[40,128]{1,0:T(8,128)S(1)} %add_add_fusion.2.above_part), channel_id=1, source_target_pairs={{0,32},{32,64},{64,96},{96,128},{128,160},{160,192},{192,224},{224... | collective-permute-start | bytes 61448 | tf_op jit(solution)/shard_map/ppermute | solution.py:661
  103.5 2.6 %collective-permute-done.5.from_below = f32[40,128]{1,0:T(8,128)S(1)} collective-permute-done((f32[40,128]{1,0:T(8,128)S(1)}, f32[40,128]{1,0:T(8,128)S(1)}, u32[]{:S(2)}, u32[]{:S(2)}) %collective-permute-start.5) | collective-permute-done | bytes 20512 | tf_op jit(solution)/shard_map/ppermute | solution.py:661
  106.7 31.1 %radius_gradient.1 = (f32[32,128]{1,0:T(8,128)}, f32[80,128]{1,0:T(8,128)}, f32[40,128]{1,0:T(8,128)}, f32[40,128]{1,0:T(8,128)}, f32[8,128]{1,0:T(8,128)}, /*index=5*/f32[8,128]{1,0:T(8,128)}, f32[80,3,8,128]{3,2,1,0:T(8,128)}) custom-call(s32[2]{0:T(128)} %pad_add_fusion.4.total, s32[512]{0:T(512)} %broadcast_add_fusion.items, s32[2800]{0:T(1024)} %fusion.17.reach, ...), custom_call_target="tpu_custom_call" | custom-call | tf_op jit(solution)/shard_map/radius_gradient/pallas_call | solution.py:595
  137.8 1.9 collective-permute-start.7
  139.7 5.8 %collective-permute-start.8 = (f32[8,128]{1,0:T(8,128)}, f32[8,128]{1,0:T(8,128)S(1)}, u32[]{:S(2)}, u32[]{:S(2)}) collective-permute-start(f32[8,128]{1,0:T(8,128)} %get-tuple-element.44), channel_id=1, source_target_pairs={{1,0},{2,1},{3,2},{4,3},{5,4},{6,5},{7,6},{8,7},{9,8},{10,9},{11,1... | collective-permute-start | bytes 12296 | tf_op jit(solution)/shard_map/ppermute | solution.py:666
  145.5 1.5 collective-permute-done.8
  148.5 1.9 collective-permute-start.10
  150.4 7.8 %collective-permute-start.9 = (f32[40,128]{1,0:T(8,128)S(1)}, f32[40,128]{1,0:T(8,128)S(1)}, u32[]{:S(2)}, u32[]{:S(2)}) collective-permute-start(f32[40,128]{1,0:T(8,128)S(1)} %add_add_fusion.above_grad), channel_id=1, source_target_pairs={{0,32},{32,64},{64,96},{96,128},{128,160},{160,192},{192,224},{224... | collective-permute-start | bytes 61448 | tf_op jit(solution)/shard_map/ppermute | solution.py:661
  158.2 2.6 %collective-permute-done.9.from_below = f32[40,128]{1,0:T(8,128)S(1)} collective-permute-done((f32[40,128]{1,0:T(8,128)S(1)}, f32[40,128]{1,0:T(8,128)S(1)}, u32[]{:S(2)}, u32[]{:S(2)}) %collective-permute-start.9) | collective-permute-done | bytes 20512 | tf_op jit(solution)/shard_map/ppermute | solution.py:661
  161.4 19.2 %forces.1 = (f32[32,128]{1,0:T(8,128)}, f32[3,40,128]{2,1,0:T(8,128)}, f32[3,40,128]{2,1,0:T(8,128)}, f32[3,8,128]{2,1,0:T(8,128)}) custom-call(s32[2]{0:T(128)} %pad_add_fusion.4.total, s32[512]{0:T(512)} %broadcast_add_fusion.items, s32[2800]{0:T(1024)} %fusion.17.reach, f32[80,8,128]{2,1,0:T(8,128)} %get-tuple-element.32.data, ...), custom_call_target="tpu_custom_call" | custom-call | tf_op jit(solution)/shard_map/forces/pallas_call | solution.py:620
  180.6 1.9 collective-permute-start.11
  182.5 5.4 %collective-permute-done.11 = f32[3,8,128]{2,1,0:T(8,128)S(1)} collective-permute-done((f32[3,8,128]{2,1,0:T(8,128)}, f32[3,8,128]{2,1,0:T(8,128)S(1)}, u32[]{:S(2)}, u32[]{:S(2)}) %collective-permute-start.11) | collective-permute-done | bytes 12320 | tf_op jit(solution)/shard_map/ppermute | solution.py:671
  188.8 5.7 %collective-permute-start.12 = (f32[3,32,128]{2,1,0:T(8,128)S(1)}, f32[3,32,128]{2,1,0:T(8,128)S(1)}, u32[]{:S(2)}, u32[]{:S(2)}) collective-permute-start(f32[3,32,128]{2,1,0:T(8,128)S(1)} %pad_add_fusion), channel_id=1, source_target_pairs={{0,32},{32,64},{64,96},{96,128},{128,160},{160,192},{192,224},{224... | collective-permute-start | bytes 147464 | tf_op jit(solution)/shard_map/ppermute | solution.py:661
  194.4 5.1 %collective-permute-done.12 = f32[3,32,128]{2,1,0:T(8,128)S(1)} collective-permute-done((f32[3,32,128]{2,1,0:T(8,128)S(1)}, f32[3,32,128]{2,1,0:T(8,128)S(1)}, u32[]{:S(2)}, u32[]{:S(2)}) %collective-permute-start.12) | collective-permute-done | bytes 49184 | tf_op jit(solution)/shard_map/ppermute | solution.py:661
  (115 shorter events, 15.9 us)
Async XLA Ops:
  2.1 29.6 %collective-permute-start.2 = (f32[16,128]{1,0:T(8,128)}, f32[16,128]{1,0:T(8,128)S(1)}, u32[]{:S(2)}, u32[]{:S(2)}) collective-permute-start(f32[16,128]{1,0:T(8,128)} %get-tuple-element.31), channel_id=1, source_target_pairs={{33,0},{34,1},{35,2},{36,3},{37,4},{38,5},{39,6},{40,7},{41,8},{42... | collective-permute-start | bytes 24584 | tf_op jit(solution)/shard_map/ppermute | solution.py:681
  15.9 15.8 %collective-permute-start.1 = (f32[16,128]{1,0:T(8,128)}, f32[16,128]{1,0:T(8,128)S(1)}, u32[]{:S(2)}, u32[]{:S(2)}) collective-permute-start(f32[16,128]{1,0:T(8,128)} %get-tuple-element.31), channel_id=1, source_target_pairs={{1,0},{2,1},{3,2},{4,3},{5,4},{6,5},{7,6},{8,7},{9,8},{10,9},{11,1... | collective-permute-start | bytes 24584 | tf_op jit(solution)/shard_map/ppermute | solution.py:666
  18.7 16.8 %collective-permute-start = (f32[200,128]{1,0:T(8,128)}, f32[200,128]{1,0:T(8,128)S(1)}, u32[]{:S(2)}, u32[]{:S(2)}) collective-permute-start(f32[200,128]{1,0:T(8,128)} %get-tuple-element.30.sent), channel_id=1, source_target_pairs={{32,0},{64,32},{96,64},{128,96},{160,128},{192,160},{224,192},{256... | collective-permute-start | bytes 307208 | tf_op jit(solution)/shard_map/ppermute | solution.py:656
  31.7 10.9 %copy-start.9 = (f32[16,128]{1,0:T(8,128)}, f32[16,128]{1,0:T(8,128)S(1)}, u32[]{:S(2)}) copy-start(f32[16,128]{1,0:T(8,128)S(1)} %collective-permute-done.2.above_edges) | copy-start | bytes 24580
  31.8 10.8 %copy-start.10 = (f32[16,128]{1,0:T(8,128)}, f32[16,128]{1,0:T(8,128)S(1)}, u32[]{:S(2)}) copy-start(f32[16,128]{1,0:T(8,128)S(1)} %collective-permute-done.1.edges) | copy-start | bytes 24580
  35.5 7.1 %copy-start = (f32[200,128]{1,0:T(8,128)}, f32[200,128]{1,0:T(8,128)S(1)}, u32[]{:S(2)}) copy-start(f32[200,128]{1,0:T(8,128)S(1)} %collective-permute-done.above) | copy-start | bytes 307204
  83.0 7.7 %collective-permute-start.3 = (f32[8,128]{1,0:T(8,128)}, f32[8,128]{1,0:T(8,128)S(1)}, u32[]{:S(2)}, u32[]{:S(2)}) collective-permute-start(f32[8,128]{1,0:T(8,128)} %get-tuple-element.35), channel_id=1, source_target_pairs={{0,1},{1,2},{2,3},{3,4},{4,5},{5,6},{6,7},{7,8},{8,9},{9,10},{10,1... | collective-permute-start | bytes 12296 | tf_op jit(solution)/shard_map/ppermute | solution.py:671
  84.9 7.3 %collective-permute-start.4 = (f32[8,128]{1,0:T(8,128)}, f32[8,128]{1,0:T(8,128)S(1)}, u32[]{:S(2)}, u32[]{:S(2)}) collective-permute-start(f32[8,128]{1,0:T(8,128)} %get-tuple-element.36), channel_id=1, source_target_pairs={{1,0},{2,1},{3,2},{4,3},{5,4},{6,5},{7,6},{8,7},{9,8},{10,9},{11,1... | collective-permute-start | bytes 12296 | tf_op jit(solution)/shard_map/ppermute | solution.py:666
  92.9 13.2 %copy-start.1 = (f32[40,128]{1,0:T(8,128)}, f32[40,128]{1,0:T(8,128)S(1)}, u32[]{:S(2)}) copy-start(f32[40,128]{1,0:T(8,128)S(1)} %add_add_fusion.3.own_part) | copy-start | bytes 61444
  93.7 12.4 %copy-start.2 = (f32[40,128]{1,0:T(8,128)}, f32[40,128]{1,0:T(8,128)S(1)}, u32[]{:S(2)}) copy-start(f32[40,128]{1,0:T(8,128)S(1)} %add_add_fusion.2.above_part) | copy-start | bytes 61444
  93.7 9.8 %collective-permute-start.6 = (f32[40,128]{1,0:T(8,128)S(1)}, f32[40,128]{1,0:T(8,128)S(1)}, u32[]{:S(2)}, u32[]{:S(2)}) collective-permute-start(f32[40,128]{1,0:T(8,128)S(1)} %add_add_fusion.3.own_part), channel_id=1, source_target_pairs={{32,0},{64,32},{96,64},{128,96},{160,128},{192,160},{224,192},{256... | collective-permute-start | bytes 61448 | tf_op jit(solution)/shard_map/ppermute | solution.py:656
  95.6 10.5 %collective-permute-start.5 = (f32[40,128]{1,0:T(8,128)S(1)}, f32[40,128]{1,0:T(8,128)S(1)}, u32[]{:S(2)}, u32[]{:S(2)}) collective-permute-start(f32[40,128]{1,0:T(8,128)S(1)} %add_add_fusion.2.above_part), channel_id=1, source_target_pairs={{0,32},{32,64},{64,96},{96,128},{128,160},{160,192},{192,224},{224... | collective-permute-start | bytes 61448 | tf_op jit(solution)/shard_map/ppermute | solution.py:661
  103.5 2.6 %copy-start.5 = (f32[40,128]{1,0:T(8,128)}, f32[40,128]{1,0:T(8,128)S(1)}, u32[]{:S(2)}) copy-start(f32[40,128]{1,0:T(8,128)S(1)} %collective-permute-done.6.from_above) | copy-start | bytes 61444
  106.1 0.6 copy-start.6
  137.8 7.7 %collective-permute-start.7 = (f32[8,128]{1,0:T(8,128)}, f32[8,128]{1,0:T(8,128)S(1)}, u32[]{:S(2)}, u32[]{:S(2)}) collective-permute-start(f32[8,128]{1,0:T(8,128)} %get-tuple-element.43), channel_id=1, source_target_pairs={{0,1},{1,2},{2,3},{3,4},{4,5},{5,6},{6,7},{7,8},{8,9},{9,10},{10,1... | collective-permute-start | bytes 12296 | tf_op jit(solution)/shard_map/ppermute | solution.py:671
  139.7 7.3 %collective-permute-start.8 = (f32[8,128]{1,0:T(8,128)}, f32[8,128]{1,0:T(8,128)S(1)}, u32[]{:S(2)}, u32[]{:S(2)}) collective-permute-start(f32[8,128]{1,0:T(8,128)} %get-tuple-element.44), channel_id=1, source_target_pairs={{1,0},{2,1},{3,2},{4,3},{5,4},{6,5},{7,6},{8,7},{9,8},{10,9},{11,1... | collective-permute-start | bytes 12296 | tf_op jit(solution)/shard_map/ppermute | solution.py:666
  147.7 13.2 %copy-start.3 = (f32[40,128]{1,0:T(8,128)}, f32[40,128]{1,0:T(8,128)S(1)}, u32[]{:S(2)}) copy-start(f32[40,128]{1,0:T(8,128)S(1)} %add_add_fusion.1.own_grad) | copy-start | bytes 61444
  148.4 12.4 %copy-start.4 = (f32[40,128]{1,0:T(8,128)}, f32[40,128]{1,0:T(8,128)S(1)}, u32[]{:S(2)}) copy-start(f32[40,128]{1,0:T(8,128)S(1)} %add_add_fusion.above_grad) | copy-start | bytes 61444
  148.5 9.8 %collective-permute-start.10 = (f32[40,128]{1,0:T(8,128)S(1)}, f32[40,128]{1,0:T(8,128)S(1)}, u32[]{:S(2)}, u32[]{:S(2)}) collective-permute-start(f32[40,128]{1,0:T(8,128)S(1)} %add_add_fusion.1.own_grad), channel_id=1, source_target_pairs={{32,0},{64,32},{96,64},{128,96},{160,128},{192,160},{224,192},{256... | collective-permute-start | bytes 61448 | tf_op jit(solution)/shard_map/ppermute | solution.py:656
  150.4 10.5 %collective-permute-start.9 = (f32[40,128]{1,0:T(8,128)S(1)}, f32[40,128]{1,0:T(8,128)S(1)}, u32[]{:S(2)}, u32[]{:S(2)}) collective-permute-start(f32[40,128]{1,0:T(8,128)S(1)} %add_add_fusion.above_grad), channel_id=1, source_target_pairs={{0,32},{32,64},{64,96},{96,128},{128,160},{160,192},{192,224},{224... | collective-permute-start | bytes 61448 | tf_op jit(solution)/shard_map/ppermute | solution.py:661
  158.2 2.6 %copy-start.7 = (f32[40,128]{1,0:T(8,128)}, f32[40,128]{1,0:T(8,128)S(1)}, u32[]{:S(2)}) copy-start(f32[40,128]{1,0:T(8,128)S(1)} %collective-permute-done.10.from_above) | copy-start | bytes 61444
  160.9 0.6 copy-start.8
  180.6 7.3 %collective-permute-start.11 = (f32[3,8,128]{2,1,0:T(8,128)}, f32[3,8,128]{2,1,0:T(8,128)S(1)}, u32[]{:S(2)}, u32[]{:S(2)}) collective-permute-start(f32[3,8,128]{2,1,0:T(8,128)} %get-tuple-element.53), channel_id=1, source_target_pairs={{0,1},{1,2},{2,3},{3,4},{4,5},{5,6},{6,7},{7,8},{8,9},{9,10},{10,1... | collective-permute-start | bytes 36872 | tf_op jit(solution)/shard_map/ppermute | solution.py:671
  188.8 10.8 %collective-permute-start.12 = (f32[3,32,128]{2,1,0:T(8,128)S(1)}, f32[3,32,128]{2,1,0:T(8,128)S(1)}, u32[]{:S(2)}, u32[]{:S(2)}) collective-permute-start(f32[3,32,128]{2,1,0:T(8,128)S(1)} %pad_add_fusion), channel_id=1, source_target_pairs={{0,32},{32,64},{64,96},{96,128},{128,160},{160,192},{192,224},{224... | collective-permute-start | bytes 147464 | tf_op jit(solution)/shard_map/ppermute | solution.py:661

commit v4 on v3

--- a/solution.py
+++ b/solution.py
@@ -31,7 +31,6 @@
 PART_WIDTH = 4
 FULL_RING = 32
 PART_RING = 32
-SELF_WIDTH = 4
 PAIRS = 2 * TILES * LISTED + 4
 ITEMS = 512
 DUMMY = LIVE * ATOMS + LIVE
@@ -63,6 +62,31 @@
     return total
 
 
+def build_beside(build, work, table, fresh_a, fresh_b):
+    def keep(tile, fresh, k):
+        table[tile] = fresh[k]
+
+    def step(index, carry):
+        first = index * 4
+        for k in range(2):
+            build(first + 2 + k, fresh_b, k)
+            work(first + k, fresh_a, k)
+        for k in range(2):
+            keep(first + k, fresh_a, k)
+        for k in range(2):
+            build(first + 4 + k, fresh_a, k)
+            work(first + 2 + k, fresh_b, k)
+        for k in range(2):
+            keep(first + 2 + k, fresh_b, k)
+        return carry
+
+    for k in range(2):
+        build(k, fresh_a, k)
+    lax.fori_loop(0, TILES // 4, step, 0)
+    for k in range(EDGE):
+        keep(TILES + k, fresh_a, k)
+
+
 def by_fours(step):
     def fours(index, carry):
         start = jnp.minimum(index * 4, LIVE - 4)
@@ -73,12 +97,9 @@
     lax.fori_loop(0, (LIVE + 3) // 4, fours, 0)
 
 
-def fill_table(table, tile, first, ref, rows, factor=None):
+def fill_table(table, k, first, ref, tile, rows):
     for slot, row in enumerate(rows):
-        values = ref[tile, row : row + 1, :]
-        if factor is not None:
-            values = values * factor
-        table[tile, first + slot] = jnp.broadcast_to(values, BLOCK).T
+        table[k, first + slot] = jnp.broadcast_to(ref[tile, row : row + 1, :], BLOCK).T
 
 
 def fold_rows(own, target, index):
@@ -178,7 +199,7 @@
 def born_kernel(
     total, items, reach, sent, edges, above, above_edges,
     own_part, above_part, to_next, to_last, data, plain, d_self, d_pair,
-    table, own, far, rings, sems,
+    table, fresh_a, fresh_b, own, far, rings, sems,
 ):
     full_ring, part_ring, self_ring = rings
     full_sems, part_sems, self_sems = sems
@@ -207,27 +228,26 @@
                 else:
                     data[rows, ROW_SCALED, :] = values * SCALE
 
-    def prepare(tile):
-        fill_table(table, tile, 0, data, (ROW_X, ROW_Y, ROW_Z, ROW_IN, ROW_SCALED))
-
-    by_fours(prepare)
+    def build(tile, fresh, k):
+        fill_table(fresh, k, 0, data, tile, (ROW_X, ROW_Y, ROW_Z, ROW_IN, ROW_SCALED))
+
     for tile in range(TILES, OWN_ROWS):
         own[tile] = jnp.zeros(BLOCK, F32)
 
-    def shared(tile, rows, r2):
+    def shared(r2):
         inv = lax.rsqrt(r2)
         cut = jnp.maximum(1.0 - r2 * (1.0 / CUT), 0.0)
         cinv = cut * inv
         return r2 * inv, cut, cinv, cinv * cinv * inv
 
-    def self_pair(tile):
+    def self_pair(tile, fresh, k):
         far_xyz = [row_of(data, tile, axis) for axis in range(3)]
         bs = row_of(data, tile, ROW_SCALED)
         for start in range(0, ATOMS, CHUNK):
             rows = span(start)
-            r2 = distance_squared(differences(table, tile, rows, far_xyz)) + diagonal(start)
-            r, cut, cinv, g_deriv = shared(tile, rows, r2)
-            value, deriv = half_descreen(r, table[tile, 3, rows, :], bs)
+            r2 = distance_squared(differences(fresh, k, rows, far_xyz)) + diagonal(start)
+            r, cut, cinv, g_deriv = shared(r2)
+            value, deriv = half_descreen(r, fresh[k, 3, rows, :], bs)
             value = cinv * value
             own[tile, rows, :] = cut * value
             self_ring[tile, rows, :] = g_deriv * deriv - value
@@ -235,14 +255,11 @@
     def self_copy(tile):
         return pltpu.make_async_copy(self_ring.at[tile], d_self.at[tile], self_sems.at[tile])
 
-    def self_step(quad, carry):
-        for k in range(SELF_WIDTH):
-            self_pair(quad * SELF_WIDTH + k)
-        for k in range(SELF_WIDTH):
-            self_copy(quad * SELF_WIDTH + k).start()
-        return carry
-
-    lax.fori_loop(0, TILES // SELF_WIDTH, self_step, 0)
+    def self_step(tile, fresh, k):
+        self_pair(tile, fresh, k)
+        self_copy(tile).start()
+
+    build_beside(build, self_step, table, fresh_a, fresh_b)
 
     def pair(item, ring, slot, starts):
         first, second = item
@@ -253,7 +270,7 @@
             rows = span(start)
             kept = span(place * CHUNK)
             r2 = distance_squared(differences(table, first, rows, far_xyz))
-            r, cut, cinv, g_deriv = shared(first, rows, r2)
+            r, cut, cinv, g_deriv = shared(r2)
             value, deriv = half_descreen(r, table[first, 3, rows, :], bs)
             value = cinv * value
             own[first, rows, :] += cut * value
@@ -313,7 +330,7 @@
 def energy_kernel(
     total, items, reach, data, plain, own_part, above_part, from_below, from_above,
     radii_born, slope, own_grad, above_grad, to_next, to_last, force,
-    table, own, far, born,
+    table, fresh_a, fresh_b, own, far, born,
 ):
     far[...] = jnp.zeros_like(far)
     force[...] = jnp.zeros_like(force)
@@ -326,31 +343,31 @@
     born[:, 0, :] = SCALE * all_radii
     born[:, 1, :] = EXP_SCALE * inverse
 
-    def prepare(tile):
-        fill_table(table, tile, 0, data, (ROW_X, ROW_Y, ROW_Z, ROW_Q))
-        fill_table(table, tile, 4, born, (0, 1))
-
-    by_fours(prepare)
+    def build(tile, fresh, k):
+        fill_table(fresh, k, 0, data, tile, (ROW_X, ROW_Y, ROW_Z, ROW_Q))
+        fill_table(fresh, k, 4, born, tile, (0, 1))
+
     for tile in range(TILES, OWN_ROWS):
         own[tile] = jnp.zeros((4,) + BLOCK, F32)
 
-    def pair(first, second, starts, is_self):
+    def pair(first, second, starts, tables, k, is_self):
         far_xyz = [row_of(data, second, axis) for axis in range(3)]
         br, bi, bq = row_of(born, second, 0), -row_of(born, second, 1), row_of(data, second, ROW_Q)
         sums = [jnp.zeros(ROWS, F32)] * 4
         for start in starts:
             rows = span(start)
-            gaps = differences(table, first, rows, far_xyz)
+            gaps = differences(tables, k, rows, far_xyz)
             r2 = distance_squared(gaps)
             if is_self:
                 r2 = r2 + diagonal(start)
             cut = jnp.maximum(1.0 - r2 * (1.0 / CUT), 0.0)
-            power = r2 * (table[first, 5, rows, :] * bi)
+            power = r2 * (tables[k, 5, rows, :] * bi)
             decay = lax.exp2(power)
-            screen = (table[first, 4, rows, :] * br) * decay
+            screen = (tables[k, 4, rows, :] * br) * decay
             inv = lax.rsqrt(r2 + screen)
-            lead = (cut * (table[first, 3, rows, :] * bq)) * inv
-            square = cut * (inv * inv)
+            cinv = cut * inv
+            lead = (tables[k, 3, rows, :] * bq) * cinv
+            square = cinv * inv
             grad = (lead * square) * (screen * (1.0 - math.log(2.0) * power))
             pull = lead * (square * (4.0 - decay) + 16.0 / CUT)
             terms = [grad] + [pull * gap for gap in gaps]
@@ -365,23 +382,22 @@
             for axis in range(3):
                 force[second, axis] -= fold2(sums[1 + axis])
 
-    def self_step(quad, carry):
-        for k in range(2):
-            pair(quad * 2 + k, quad * 2 + k, range(0, ATOMS, CHUNK), True)
-        return carry
-
-    lax.fori_loop(0, TILES // 2, self_step, 0)
+    def self_step(tile, fresh, k):
+        pair(tile, tile, range(0, ATOMS, CHUNK), fresh, k, True)
+
+    build_beside(build, self_step, table, fresh_a, fresh_b)
 
     def full_step(index, carry):
         for k in range(FULL_WIDTH):
             first, second = decode(items[index * FULL_WIDTH + k])
-            pair(first, second, range(0, ATOMS, CHUNK), False)
+            pair(first, second, range(0, ATOMS, CHUNK), table, first, False)
         return carry
 
     def part_step(index, carry):
         for k in range(PART_WIDTH):
             first, second = decode(items[fulls + index * PART_WIDTH + k])
-            pair(first, second, part_starts(reach[first * REGION + second]), False)
+            starts = part_starts(reach[first * REGION + second])
+            pair(first, second, starts, table, first, False)
         return carry
 
     lax.fori_loop(0, lax.div(fulls, FULL_WIDTH), full_step, 0)
@@ -406,7 +422,7 @@
 
 def force_kernel(
     total, items, reach, data, slope, own_grad, above_grad, from_below, from_above, force_in, d_self, d_pair,
-    gradient, own_force, above_force, to_next,
+    gradient, own_force, above_force, to_next, to_across,
     table, own, far, chain, rings, sems,
 ):
     full_ring, part_ring, self_ring = rings
@@ -435,21 +451,21 @@
     gradient[...] = grads[0:TILES]
     chain[:, 0, :] = grads * slope[...]
 
-    def prepare(tile):
-        fill_table(table, tile, 0, data, (ROW_X, ROW_Y, ROW_Z))
-        fill_table(table, tile, 3, chain, (0,))
-
-    by_fours(prepare)
+    def build(tile):
+        fill_table(table, tile, 0, data, tile, (ROW_X, ROW_Y, ROW_Z))
+        fill_table(table, tile, 3, chain, tile, (0,))
+
+    by_fours(build)
     for tile in range(TILES, OWN_ROWS):
         own[tile] = jnp.zeros((3,) + BLOCK, F32)
 
-    def pair(first, second, starts, pull_of, is_self):
+    def pair(first, second, starts, tables, k, pull_of, is_self):
         far_xyz = [row_of(data, second, axis) for axis in range(3)]
         sums = [jnp.zeros(ROWS, F32)] * 3
         for place, start in enumerate(starts):
             rows = span(start)
             pull = pull_of(rows, span(place * CHUNK))
-            terms = [pull * gap for gap in differences(table, first, rows, far_xyz)]
+            terms = [pull * gap for gap in differences(tables, k, rows, far_xyz)]
             for which, term in enumerate(terms):
                 if is_self:
                     own[first, which, rows, :] = term
@@ -460,21 +476,23 @@
             far[second, axis] -= fold2(sums[axis])
 
     def self_step(quad, carry):
-        begin = quad * SELF_WIDTH
-        for k in range(SELF_WIDTH):
+        begin = quad * 4
+        for k in range(4):
             self_copy(begin + k).wait()
-        for k in range(SELF_WIDTH):
+        for k in range(4):
             tile = begin + k
             pair(
                 tile,
                 tile,
                 range(0, ATOMS, CHUNK),
+                table,
+                tile,
                 lambda rows, kept: table[tile, 3, rows, :] * self_ring[tile, kept, :],
                 True,
             )
         return carry
 
-    lax.fori_loop(0, TILES // SELF_WIDTH, self_step, 0)
+    lax.fori_loop(0, TILES // 4, self_step, 0)
 
     def run(width, size, ring, copy, base, number, starts_of):
         def body(index, carry):
@@ -489,6 +507,8 @@
                     first,
                     second,
                     starts_of(first, second),
+                    table,
+                    first,
                     lambda rows, kept: table[first, 3, rows, :] * ring[slot, 0, kept, :]
                     + factor * ring[slot, 1, kept, :],
                     False,
@@ -524,9 +544,10 @@
     lax.fori_loop(0, LIVE // 2, fold_step, 0)
     for axis in range(3):
         sums = jnp.sum(far[:, axis], axis=1) * (-SCALE * SCALE / 16.0)
-        own_force[axis] = sums[0:HALF]
-        above_force[axis] = sums[HALF:]
-        edge_rows(to_next.at[axis], sums, TILES, HALF + TILES)
+        own_force[axis] = sums[0:TILES]
+        above_force[axis] = sums[HALF : HALF + TILES]
+        to_next[axis] = sums[TILES : TILES + 8]
+        to_across[axis] = sums[HALF + TILES : HALF + TILES + 8]
 
 
 SMEM = pl.BlockSpec(memory_space=pltpu.SMEM)
@@ -582,6 +603,8 @@
         out_specs=(VMEM,) * 6 + (ANY,) * 2,
         scratch_shapes=[
             pltpu.VMEM((OWN_ROWS, 5) + BLOCK, F32),
+            pltpu.VMEM((2, 5) + BLOCK, F32),
+            pltpu.VMEM((2, 5) + BLOCK, F32),
             pltpu.VMEM((OWN_ROWS,) + BLOCK, F32),
             pltpu.VMEM((REGION,) + LANES, F32),
             RING_BLOCKS,
@@ -608,6 +631,8 @@
         out_specs=(VMEM,) * 7,
         scratch_shapes=[
             pltpu.VMEM((OWN_ROWS, 6) + BLOCK, F32),
+            pltpu.VMEM((2, 6) + BLOCK, F32),
+            pltpu.VMEM((2, 6) + BLOCK, F32),
             pltpu.VMEM((OWN_ROWS, 4) + BLOCK, F32),
             pltpu.VMEM((REGION,) + LANES, F32),
             pltpu.VMEM((REGION,) + LANES, F32),
@@ -620,9 +645,15 @@
     return pl.pallas_call(
         force_kernel,
         name="forces",
-        out_shape=(f32(TILES, ATOMS), f32(3, HALF, ATOMS), f32(3, HALF, ATOMS), f32(3, *LANES)),
+        out_shape=(
+            f32(TILES, ATOMS),
+            f32(3, TILES, ATOMS),
+            f32(3, TILES, ATOMS),
+            f32(3, *LANES),
+            f32(3, *LANES),
+        ),
         in_specs=[SMEM] * 3 + [VMEM] * 7 + [ANY] * 2,
-        out_specs=(VMEM,) * 4,
+        out_specs=(VMEM,) * 5,
         scratch_shapes=[
             pltpu.VMEM((OWN_ROWS, 4) + BLOCK, F32),
             pltpu.VMEM((OWN_ROWS, 3) + BLOCK, F32),
@@ -694,6 +725,16 @@
     above = above + placed(from_last, EDGE, from_next)
     own, above = lax.optimization_barrier((own, above))
     return own, above, here_to_above(above), above_to_here(own)
+
+
+def here_to_across(block):
+    slabs, count = lax.axis_size("slab"), lax.axis_size("tile")
+    pairs = [
+        (slab * count + tile, (slab + 1) * count + (tile + 1) % count)
+        for slab in range(slabs - 1)
+        for tile in range(count)
+    ]
+    return lax.ppermute(block, ("slab", "tile"), pairs)
 
 
 def whole_slab(component, block, edges):
@@ -778,12 +819,12 @@
     shares = swap_sums(*parts)
     radii_born, slope, *parts, force = run_energy(total, items, reach, data, plain, shares)
     shares = swap_sums(*parts)
-    gradient, own, over, to_next = run_force(total, items, reach, data, slope, shares, force, d_self, d_pair)
-    from_last = here_to_next(to_next)
-    edge = ((0, 0), (0, TILES - EDGE), (0, 0))
-    over = over[:, 0:TILES] + jnp.pad(from_last[:, EDGE : 2 * EDGE], edge)
-    own = own[:, 0:TILES] + jnp.pad(from_last[:, 0:EDGE], edge)
-    forces = own + here_to_above(over)
+    gradient, own, over, to_next, to_across = run_force(
+        total, items, reach, data, slope, shares, force, d_self, d_pair
+    )
+    from_below = here_to_above(over)
+    edge = here_to_next(to_next) + here_to_across(to_across)
+    forces = own + from_below + jnp.pad(edge[:, 0:EDGE], ((0, 0), (0, TILES - EDGE), (0, 0)))
     return (radii_born[None, None], gradient[None, None], jnp.swapaxes(forces, 0, 1)[None, None])
 
 

time: 202 us -> 202 us (level)
  the two profiles are of different devices: /device:TPU:48 before, /device:TPU:22 now
where the time goes in v4:
time: 202 us; the launch traced here: 201 us
  starting transfers between devices  70.8 us (35%)
  Pallas kernels  57.1 us (28%)
  waiting for transfers between devices  50.9 us (25%)
  other arithmetic  9.44 us (5%)
  between operations  6.54 us (3%)
  local copies, waits for them, and re-layouts  5.41 us (3%)
    ppermute x3, waiting for transfers between devices, next_to_here(): lax.ppermute(block, 'tile', [((i + 1) % count, i) for i in range(count)])  28.8 us
    pallas_call x1, Pallas kernels, run_born(): pl.pallas_call(born_kernel, name='born_sums', out_shape=(f32(HALF, ATOMS)...  22.8 us
    ppermute x3, waiting for transfers between devices, here_to_above(): return lax.ppermute(block, 'slab', [(i, i + 1) for i in range(ends)])  18.6 us
    pallas_call x1, Pallas kernels, run_energy(): pl.pallas_call(energy_kernel, name='radius_gradient', out_shape=(f32(TILE...  18.2 us
    pallas_call x1, Pallas kernels, run_force(): pl.pallas_call(force_kernel, name='forces', out_shape=(f32(TILES, ATOMS),...  14.6 us
    ppermute x3, starting transfers between devices, above_to_here(): return lax.ppermute(block, 'slab', [(i + 1, i) for i in range(ends)])  13.6 us
    ppermute x3, starting transfers between devices, here_to_above(): return lax.ppermute(block, 'slab', [(i, i + 1) for i in range(ends)])  13.3 us
    ppermute x3, starting transfers between devices, here_to_next(): lax.ppermute(block, 'tile', [(i, (i + 1) % count) for i in range(count)])  13 us
  transfers between devices with their start and end apart: 14, of which 6 were waited for; matrix products, arithmetic and copies ran while one was open for 2% of the time, Pallas kernels for 0%

profile of v4, /device:TPU:22, one launch (start us, length us, event | category | flops | bytes accessed | tf_op | source)
XLA Modules:
  0.0 200.5 jit_solution(17177938853754397007)
XLA Ops:
  0.6 1.5 pack_atoms.1
  2.1 12.3 %collective-permute-start.2 = (f32[16,128]{1,0:T(8,128)}, f32[16,128]{1,0:T(8,128)S(1)}, u32[]{:S(2)}, u32[]{:S(2)}) collective-permute-start(f32[16,128]{1,0:T(8,128)} %get-tuple-element.32), channel_id=1, source_target_pairs={{33,0},{34,1},{35,2},{36,3},{37,4},{38,5},{39,6},{40,7},{41,8},{42... | collective-permute-start | bytes 24584 | tf_op jit(solution)/shard_map/ppermute | solution.py:712
  14.5 2.8 %collective-permute-start.1 = (f32[16,128]{1,0:T(8,128)}, f32[16,128]{1,0:T(8,128)S(1)}, u32[]{:S(2)}, u32[]{:S(2)}) collective-permute-start(f32[16,128]{1,0:T(8,128)} %get-tuple-element.32), channel_id=1, source_target_pairs={{1,0},{2,1},{3,2},{4,3},{5,4},{6,5},{7,6},{8,7},{9,8},{10,9},{11,1... | collective-permute-start | bytes 24584 | tf_op jit(solution)/shard_map/ppermute | solution.py:697
  17.2 5.5 %collective-permute-start = (f32[200,128]{1,0:T(8,128)}, f32[200,128]{1,0:T(8,128)S(1)}, u32[]{:S(2)}, u32[]{:S(2)}) collective-permute-start(f32[200,128]{1,0:T(8,128)} %get-tuple-element.31.sent), channel_id=1, source_target_pairs={{32,0},{64,32},{96,64},{128,96},{160,128},{192,160},{224,192},{256... | collective-permute-start | bytes 307208 | tf_op jit(solution)/shard_map/ppermute | solution.py:687
  30.8 3.5 %collective-permute-done.above = f32[200,128]{1,0:T(8,128)S(1)} collective-permute-done((f32[200,128]{1,0:T(8,128)}, f32[200,128]{1,0:T(8,128)S(1)}, u32[]{:S(2)}, u32[]{:S(2)}) %collective-permute-start) | collective-permute-done | bytes 102432 | tf_op jit(solution)/shard_map/ppermute | solution.py:687
  41.4 22.8 %born_sums.1 = (f32[40,128]{1,0:T(8,128)}, f32[40,128]{1,0:T(8,128)}, f32[8,128]{1,0:T(8,128)}, f32[8,128]{1,0:T(8,128)}, f32[80,8,128]{2,1,0:T(8,128)}, /*index...) custom-call(s32[2]{0:T(128)} %pad_add_fusion.3.total, s32[512]{0:T(512)} %broadcast_add_fusion.items, ...), custom_call_target="tpu_custom_call" | custom-call | tf_op jit(solution)/shard_map/born_sums/pallas_call | solution.py:589
  64.3 1.9 collective-permute-start.3
  66.2 3.6 %collective-permute-start.4 = (f32[8,128]{1,0:T(8,128)}, f32[8,128]{1,0:T(8,128)S(1)}, u32[]{:S(2)}, u32[]{:S(2)}) collective-permute-start(f32[8,128]{1,0:T(8,128)} %get-tuple-element.37), channel_id=1, source_target_pairs={{1,0},{2,1},{3,2},{4,3},{5,4},{6,5},{7,6},{8,7},{9,8},{10,9},{11,1... | collective-permute-start | bytes 12296 | tf_op jit(solution)/shard_map/ppermute | solution.py:697
  69.9 17.7 %collective-permute-done.4 = f32[8,128]{1,0:T(8,128)S(1)} collective-permute-done((f32[8,128]{1,0:T(8,128)}, f32[8,128]{1,0:T(8,128)S(1)}, u32[]{:S(2)}, u32[]{:S(2)}) %collective-permute-start.4) | collective-permute-done | bytes 4128 | tf_op jit(solution)/shard_map/ppermute | solution.py:697
  89.1 6.2 %collective-permute-start.6 = (f32[40,128]{1,0:T(8,128)S(1)}, f32[40,128]{1,0:T(8,128)S(1)}, u32[]{:S(2)}, u32[]{:S(2)}) collective-permute-start(f32[40,128]{1,0:T(8,128)S(1)} %add_add_fusion.3.own_part), channel_id=1, source_target_pairs={{32,0},{64,32},{96,64},{128,96},{160,128},{192,160},{224,192},{256... | collective-permute-start | bytes 61448 | tf_op jit(solution)/shard_map/ppermute | solution.py:687
  95.3 3.5 %collective-permute-start.5 = (f32[40,128]{1,0:T(8,128)S(1)}, f32[40,128]{1,0:T(8,128)S(1)}, u32[]{:S(2)}, u32[]{:S(2)}) collective-permute-start(f32[40,128]{1,0:T(8,128)S(1)} %add_add_fusion.2.above_part), channel_id=1, source_target_pairs={{0,32},{32,64},{64,96},{96,128},{128,160},{160,192},{192,224},{224... | collective-permute-start | bytes 61448 | tf_op jit(solution)/shard_map/ppermute | solution.py:692
  98.8 7.0 %collective-permute-done.5.from_below = f32[40,128]{1,0:T(8,128)S(1)} collective-permute-done((f32[40,128]{1,0:T(8,128)S(1)}, f32[40,128]{1,0:T(8,128)S(1)}, u32[]{:S(2)}, u32[]{:S(2)}) %collective-permute-start.5) | collective-permute-done | bytes 20512 | tf_op jit(solution)/shard_map/ppermute | solution.py:692
  106.4 18.2 %radius_gradient.1 = (f32[32,128]{1,0:T(8,128)}, f32[80,128]{1,0:T(8,128)}, f32[40,128]{1,0:T(8,128)}, f32[40,128]{1,0:T(8,128)}, f32[8,128]{1,0:T(8,128)}, /*index=5*/f32[8,128]{1,0:T(8,128)}, f32[80,3,8,128]{3,2,1,0:T(8,128)}) custom-call(s32[2]{0:T(128)} %pad_add_fusion.3.total, s32[512]{0:T(512)} %broadcast_add_fusion.items, s32[2800]{0:T(1024)} %fusion.17.reach, ...), custom_call_target="tpu_custom_call" | custom-call | tf_op jit(solution)/shard_map/radius_gradient/pallas_call | solution.py:618
  124.6 5.5 %collective-permute-start.7 = (f32[8,128]{1,0:T(8,128)}, f32[8,128]{1,0:T(8,128)S(1)}, u32[]{:S(2)}, u32[]{:S(2)}) collective-permute-start(f32[8,128]{1,0:T(8,128)} %get-tuple-element.44), channel_id=1, source_target_pairs={{0,1},{1,2},{2,3},{3,4},{4,5},{5,6},{6,7},{7,8},{8,9},{9,10},{10,1... | collective-permute-start | bytes 12296 | tf_op jit(solution)/shard_map/ppermute | solution.py:702
  130.1 1.9 collective-permute-start.8
  132.1 11.1 %collective-permute-done.8 = f32[8,128]{1,0:T(8,128)S(1)} collective-permute-done((f32[8,128]{1,0:T(8,128)}, f32[8,128]{1,0:T(8,128)S(1)}, u32[]{:S(2)}, u32[]{:S(2)}) %collective-permute-start.8) | collective-permute-done | bytes 4128 | tf_op jit(solution)/shard_map/ppermute | solution.py:697
  144.6 1.9 collective-permute-start.10
  146.6 7.8 %collective-permute-start.9 = (f32[40,128]{1,0:T(8,128)S(1)}, f32[40,128]{1,0:T(8,128)S(1)}, u32[]{:S(2)}, u32[]{:S(2)}) collective-permute-start(f32[40,128]{1,0:T(8,128)S(1)} %add_add_fusion.above_grad), channel_id=1, source_target_pairs={{0,32},{32,64},{64,96},{96,128},{128,160},{160,192},{192,224},{224... | collective-permute-start | bytes 61448 | tf_op jit(solution)/shard_map/ppermute | solution.py:692
  154.4 2.6 %collective-permute-done.9.from_below = f32[40,128]{1,0:T(8,128)S(1)} collective-permute-done((f32[40,128]{1,0:T(8,128)S(1)}, f32[40,128]{1,0:T(8,128)S(1)}, u32[]{:S(2)}, u32[]{:S(2)}) %collective-permute-start.9) | collective-permute-done | bytes 20512 | tf_op jit(solution)/shard_map/ppermute | solution.py:692
  157.6 14.6 %forces.1 = (f32[32,128]{1,0:T(8,128)}, f32[3,32,128]{2,1,0:T(8,128)}, f32[3,32,128]{2,1,0:T(8,128)}, f32[3,8,128]{2,1,0:T(8,128)}, f32[3,8,128]{2,1,0:T(8,128)}) custom-call(s32[2]{0:T(128)} %pad_add_fusion.3.total, s32[512]{0:T(512)} %broadcast_add_fusion.items, s32[2800]{0:T(1024)} %fusion.17.reach, f32[80,8,128]{2,1,0:T(8,128)} %get-tuple-element.33.data, ...), custom_call_target="tpu_custom_call" | custom-call | tf_op jit(solution)/shard_map/forces/pallas_call | solution.py:645
  172.2 5.5 %collective-permute-start.12 = (f32[3,8,128]{2,1,0:T(8,128)}, f32[3,8,128]{2,1,0:T(8,128)S(1)}, u32[]{:S(2)}, u32[]{:S(2)}) collective-permute-start(f32[3,8,128]{2,1,0:T(8,128)} %get-tuple-element.55), channel_id=1, source_target_pairs={{0,1},{1,2},{2,3},{3,4},{4,5},{5,6},{6,7},{7,8},{8,9},{9,10},{10,1... | collective-permute-start | bytes 36872 | tf_op jit(solution)/shard_map/ppermute | solution.py:702
  177.8 10.3 %collective-permute-start.13 = (f32[3,8,128]{2,1,0:T(8,128)}, f32[3,8,128]{2,1,0:T(8,128)S(1)}, u32[]{:S(2)}, u32[]{:S(2)}) collective-permute-start(f32[3,8,128]{2,1,0:T(8,128)} %get-tuple-element.56), channel_id=1, source_target_pairs={{0,33},{1,34},{2,35},{3,36},{4,37},{5,38},{6,39},{7,40},{8,41},{9,... | collective-permute-start | bytes 36872 | tf_op jit(solution)/shard_map/ppermute | solution.py:737
  188.1 1.9 collective-permute-start.11
  190.1 9.0 %collective-permute-done.11 = f32[3,32,128]{2,1,0:T(8,128)S(1)} collective-permute-done((f32[3,32,128]{2,1,0:T(8,128)}, f32[3,32,128]{2,1,0:T(8,128)S(1)}, u32[]{:S(2)}, u32[]{:S(2)}) %collective-permute-start.11) | collective-permute-done | bytes 49184 | tf_op jit(solution)/shard_map/ppermute | solution.py:692
  (116 shorter events, 15.2 us)
Async XLA Ops:
  2.1 28.1 %collective-permute-start.2 = (f32[16,128]{1,0:T(8,128)}, f32[16,128]{1,0:T(8,128)S(1)}, u32[]{:S(2)}, u32[]{:S(2)}) collective-permute-start(f32[16,128]{1,0:T(8,128)} %get-tuple-element.32), channel_id=1, source_target_pairs={{33,0},{34,1},{35,2},{36,3},{37,4},{38,5},{39,6},{40,7},{41,8},{42... | collective-permute-start | bytes 24584 | tf_op jit(solution)/shard_map/ppermute | solution.py:712
  14.5 15.8 %collective-permute-start.1 = (f32[16,128]{1,0:T(8,128)}, f32[16,128]{1,0:T(8,128)S(1)}, u32[]{:S(2)}, u32[]{:S(2)}) collective-permute-start(f32[16,128]{1,0:T(8,128)} %get-tuple-element.32), channel_id=1, source_target_pairs={{1,0},{2,1},{3,2},{4,3},{5,4},{6,5},{7,6},{8,7},{9,8},{10,9},{11,1... | collective-permute-start | bytes 24584 | tf_op jit(solution)/shard_map/ppermute | solution.py:697
  17.2 17.0 %collective-permute-start = (f32[200,128]{1,0:T(8,128)}, f32[200,128]{1,0:T(8,128)S(1)}, u32[]{:S(2)}, u32[]{:S(2)}) collective-permute-start(f32[200,128]{1,0:T(8,128)} %get-tuple-element.31.sent), channel_id=1, source_target_pairs={{32,0},{64,32},{96,64},{128,96},{160,128},{192,160},{224,192},{256... | collective-permute-start | bytes 307208 | tf_op jit(solution)/shard_map/ppermute | solution.py:687
  30.3 11.2 %copy-start.9 = (f32[16,128]{1,0:T(8,128)}, f32[16,128]{1,0:T(8,128)S(1)}, u32[]{:S(2)}) copy-start(f32[16,128]{1,0:T(8,128)S(1)} %collective-permute-done.2.above_edges) | copy-start | bytes 24580
  30.3 11.1 %copy-start.10 = (f32[16,128]{1,0:T(8,128)}, f32[16,128]{1,0:T(8,128)S(1)}, u32[]{:S(2)}) copy-start(f32[16,128]{1,0:T(8,128)S(1)} %collective-permute-done.1.edges) | copy-start | bytes 24580
  34.3 7.2 %copy-start = (f32[200,128]{1,0:T(8,128)}, f32[200,128]{1,0:T(8,128)S(1)}, u32[]{:S(2)}) copy-start(f32[200,128]{1,0:T(8,128)S(1)} %collective-permute-done.above) | copy-start | bytes 307204
  64.3 5.6 %collective-permute-start.3 = (f32[8,128]{1,0:T(8,128)}, f32[8,128]{1,0:T(8,128)S(1)}, u32[]{:S(2)}, u32[]{:S(2)}) collective-permute-start(f32[8,128]{1,0:T(8,128)} %get-tuple-element.36), channel_id=1, source_target_pairs={{0,1},{1,2},{2,3},{3,4},{4,5},{5,6},{6,7},{7,8},{8,9},{9,10},{10,1... | collective-permute-start | bytes 12296 | tf_op jit(solution)/shard_map/ppermute | solution.py:702
  66.2 21.4 %collective-permute-start.4 = (f32[8,128]{1,0:T(8,128)}, f32[8,128]{1,0:T(8,128)S(1)}, u32[]{:S(2)}, u32[]{:S(2)}) collective-permute-start(f32[8,128]{1,0:T(8,128)} %get-tuple-element.37), channel_id=1, source_target_pairs={{1,0},{2,1},{3,2},{4,3},{5,4},{6,5},{7,6},{8,7},{9,8},{10,9},{11,1... | collective-permute-start | bytes 12296 | tf_op jit(solution)/shard_map/ppermute | solution.py:697
  88.3 17.5 %copy-start.1 = (f32[40,128]{1,0:T(8,128)}, f32[40,128]{1,0:T(8,128)S(1)}, u32[]{:S(2)}) copy-start(f32[40,128]{1,0:T(8,128)S(1)} %add_add_fusion.3.own_part) | copy-start | bytes 61444
  89.0 16.7 %copy-start.2 = (f32[40,128]{1,0:T(8,128)}, f32[40,128]{1,0:T(8,128)S(1)}, u32[]{:S(2)}) copy-start(f32[40,128]{1,0:T(8,128)S(1)} %add_add_fusion.2.above_part) | copy-start | bytes 61444
  89.1 9.8 %collective-permute-start.6 = (f32[40,128]{1,0:T(8,128)S(1)}, f32[40,128]{1,0:T(8,128)S(1)}, u32[]{:S(2)}, u32[]{:S(2)}) collective-permute-start(f32[40,128]{1,0:T(8,128)S(1)} %add_add_fusion.3.own_part), channel_id=1, source_target_pairs={{32,0},{64,32},{96,64},{128,96},{160,128},{192,160},{224,192},{256... | collective-permute-start | bytes 61448 | tf_op jit(solution)/shard_map/ppermute | solution.py:687
  95.3 10.5 %collective-permute-start.5 = (f32[40,128]{1,0:T(8,128)S(1)}, f32[40,128]{1,0:T(8,128)S(1)}, u32[]{:S(2)}, u32[]{:S(2)}) collective-permute-start(f32[40,128]{1,0:T(8,128)S(1)} %add_add_fusion.2.above_part), channel_id=1, source_target_pairs={{0,32},{32,64},{64,96},{96,128},{128,160},{160,192},{192,224},{224... | collective-permute-start | bytes 61448 | tf_op jit(solution)/shard_map/ppermute | solution.py:692
  98.8 7.0 %copy-start.5 = (f32[40,128]{1,0:T(8,128)}, f32[40,128]{1,0:T(8,128)S(1)}, u32[]{:S(2)}) copy-start(f32[40,128]{1,0:T(8,128)S(1)} %collective-permute-done.6.from_above) | copy-start | bytes 61444
  124.6 7.5 %collective-permute-start.7 = (f32[8,128]{1,0:T(8,128)}, f32[8,128]{1,0:T(8,128)S(1)}, u32[]{:S(2)}, u32[]{:S(2)}) collective-permute-start(f32[8,128]{1,0:T(8,128)} %get-tuple-element.44), channel_id=1, source_target_pairs={{0,1},{1,2},{2,3},{3,4},{4,5},{5,6},{6,7},{7,8},{8,9},{9,10},{10,1... | collective-permute-start | bytes 12296 | tf_op jit(solution)/shard_map/ppermute | solution.py:702
  130.1 13.0 %collective-permute-start.8 = (f32[8,128]{1,0:T(8,128)}, f32[8,128]{1,0:T(8,128)S(1)}, u32[]{:S(2)}, u32[]{:S(2)}) collective-permute-start(f32[8,128]{1,0:T(8,128)} %get-tuple-element.45), channel_id=1, source_target_pairs={{1,0},{2,1},{3,2},{4,3},{5,4},{6,5},{7,6},{8,7},{9,8},{10,9},{11,1... | collective-permute-start | bytes 12296 | tf_op jit(solution)/shard_map/ppermute | solution.py:697
  143.9 13.2 %copy-start.3 = (f32[40,128]{1,0:T(8,128)}, f32[40,128]{1,0:T(8,128)S(1)}, u32[]{:S(2)}) copy-start(f32[40,128]{1,0:T(8,128)S(1)} %add_add_fusion.1.own_grad) | copy-start | bytes 61444
  144.6 12.4 %copy-start.4 = (f32[40,128]{1,0:T(8,128)}, f32[40,128]{1,0:T(8,128)S(1)}, u32[]{:S(2)}) copy-start(f32[40,128]{1,0:T(8,128)S(1)} %add_add_fusion.above_grad) | copy-start | bytes 61444
  144.6 9.8 %collective-permute-start.10 = (f32[40,128]{1,0:T(8,128)S(1)}, f32[40,128]{1,0:T(8,128)S(1)}, u32[]{:S(2)}, u32[]{:S(2)}) collective-permute-start(f32[40,128]{1,0:T(8,128)S(1)} %add_add_fusion.1.own_grad), channel_id=1, source_target_pairs={{32,0},{64,32},{96,64},{128,96},{160,128},{192,160},{224,192},{256... | collective-permute-start | bytes 61448 | tf_op jit(solution)/shard_map/ppermute | solution.py:687
  146.6 10.5 %collective-permute-start.9 = (f32[40,128]{1,0:T(8,128)S(1)}, f32[40,128]{1,0:T(8,128)S(1)}, u32[]{:S(2)}, u32[]{:S(2)}) collective-permute-start(f32[40,128]{1,0:T(8,128)S(1)} %add_add_fusion.above_grad), channel_id=1, source_target_pairs={{0,32},{32,64},{64,96},{96,128},{128,160},{160,192},{192,224},{224... | collective-permute-start | bytes 61448 | tf_op jit(solution)/shard_map/ppermute | solution.py:692
  154.4 2.6 %copy-start.7 = (f32[40,128]{1,0:T(8,128)}, f32[40,128]{1,0:T(8,128)S(1)}, u32[]{:S(2)}) copy-start(f32[40,128]{1,0:T(8,128)S(1)} %collective-permute-done.10.from_above) | copy-start | bytes 61444
  157.0 0.6 copy-start.8
  172.2 17.8 %collective-permute-start.12 = (f32[3,8,128]{2,1,0:T(8,128)}, f32[3,8,128]{2,1,0:T(8,128)S(1)}, u32[]{:S(2)}, u32[]{:S(2)}) collective-permute-start(f32[3,8,128]{2,1,0:T(8,128)} %get-tuple-element.55), channel_id=1, source_target_pairs={{0,1},{1,2},{2,3},{3,4},{4,5},{5,6},{6,7},{7,8},{8,9},{9,10},{10,1... | collective-permute-start | bytes 36872 | tf_op jit(solution)/shard_map/ppermute | solution.py:702
  177.8 12.3 %collective-permute-start.13 = (f32[3,8,128]{2,1,0:T(8,128)}, f32[3,8,128]{2,1,0:T(8,128)S(1)}, u32[]{:S(2)}, u32[]{:S(2)}) collective-permute-start(f32[3,8,128]{2,1,0:T(8,128)} %get-tuple-element.56), channel_id=1, source_target_pairs={{0,33},{1,34},{2,35},{3,36},{4,37},{5,38},{6,39},{7,40},{8,41},{9,... | collective-permute-start | bytes 36872 | tf_op jit(solution)/shard_map/ppermute | solution.py:737
  188.1 11.0 %collective-permute-start.11 = (f32[3,32,128]{2,1,0:T(8,128)}, f32[3,32,128]{2,1,0:T(8,128)S(1)}, u32[]{:S(2)}, u32[]{:S(2)}) collective-permute-start(f32[3,32,128]{2,1,0:T(8,128)} %get-tuple-element.54), channel_id=1, source_target_pairs={{0,32},{32,64},{64,96},{96,128},{128,160},{160,192},{192,224},{224... | collective-permute-start | bytes 147464 | tf_op jit(solution)/shard_map/ppermute | solution.py:692
  (1 other events, 0.6 us)

commit v5 on v4

--- a/solution.py
+++ b/solution.py
@@ -102,16 +102,15 @@
         table[k, first + slot] = jnp.broadcast_to(ref[tile, row : row + 1, :], BLOCK).T
 
 
-def fold_rows(own, target, index):
-    def fours(quad, carry):
-        for k in range(4):
-            tile = quad * 4 + k
-            target[(tile,) + index] += fold_own(own[(tile,) + index])
+def fold_rows(fold, width):
+    def step(index, carry):
+        for k in range(width):
+            fold(index * width + k)
         return carry
 
-    lax.fori_loop(0, TILES // 4, fours, 0)
+    lax.fori_loop(0, TILES // width, step, 0)
     for tile in range(TILES, LIVE):
-        target[(tile,) + index] += fold_own(own[(tile,) + index])
+        fold(tile)
 
 
 def diagonal(start):
@@ -169,10 +168,16 @@
     return copy
 
 
-def edge_rows(target, values, first, second):
-    target[...] = jnp.zeros_like(target)
-    target[0:EDGE, :] = values[first : first + EDGE]
-    target[EDGE : 2 * EDGE, :] = values[second : second + EDGE]
+def edge_rows(values, first):
+    rest = jnp.zeros((8 - 2 * EDGE, ATOMS), F32)
+    return jnp.concatenate([values[first : first + EDGE], values[HALF + first : HALF + first + EDGE], rest])
+
+
+def edge_rounds(values, one, two):
+    to_next, to_last = edge_rows(values, TILES), edge_rows(values, 0)
+    is_even = lax.rem(lax.axis_index("tile"), 2) == 0
+    one[...] = jnp.where(is_even, to_next, to_last)
+    two[...] = jnp.where(is_even, to_last, to_next)
 
 
 def pack_kernel(positions, charges, radii, scales, neighbours, pad_mask, sent, edges, here):
@@ -198,7 +203,7 @@
 
 def born_kernel(
     total, items, reach, sent, edges, above, above_edges,
-    own_part, above_part, to_next, to_last, data, plain, d_self, d_pair,
+    own_part, above_part, round_one, round_two, data, plain, d_self, d_pair,
     table, fresh_a, fresh_b, own, far, rings, sems,
 ):
     full_ring, part_ring, self_ring = rings
@@ -315,21 +320,28 @@
 
     run(FULL_WIDTH, FULL_RING, full_ring, full_sems, 0, fulls, ATOMS, lambda item: range(0, ATOMS, CHUNK))
     run(PART_WIDTH, PART_RING, part_ring, part_sems, fulls, parts, PART, listed_starts)
-    fold_rows(own, far, ())
+
+    def fold(tile):
+        far[tile] += fold_own(own[tile])
+
+    fold_rows(fold, 8)
     sums = jnp.sum(far[...], axis=1) * (0.125 * SCALE)
     own_part[...] = sums[0:HALF]
     above_part[...] = sums[HALF:]
-    edge_rows(to_next, sums, TILES, HALF + TILES)
-    edge_rows(to_last, sums, 0, HALF)
-    for tile in range(TILES):
+    edge_rounds(sums, round_one, round_two)
+
+    def wait_self(tile, carry):
         self_copy(tile).wait()
+        return carry
+
+    lax.fori_loop(0, TILES, wait_self, 0)
     drain(FULL_RING, full_ring, full_sems, fulls, ATOMS)
     drain(PART_RING, part_ring, part_sems, parts, PART)
 
 
 def energy_kernel(
     total, items, reach, data, plain, own_part, above_part, from_below, from_above,
-    radii_born, slope, own_grad, above_grad, to_next, to_last, force,
+    radii_born, slope, own_grad, above_grad, round_one, round_two, force,
     table, fresh_a, fresh_b, own, far, born,
 ):
     far[...] = jnp.zeros_like(far)
@@ -403,21 +415,17 @@
     lax.fori_loop(0, lax.div(fulls, FULL_WIDTH), full_step, 0)
     lax.fori_loop(0, lax.div(parts, PART_WIDTH), part_step, 0)
 
-    def fold_step(pairs, carry):
-        for k in range(2):
-            tile = pairs * 2 + k
-            far[tile] += fold_own(own[tile, 0])
-            for axis in range(3):
-                force[tile, axis] += fold_own(own[tile, 1 + axis])
-        return carry
-
-    lax.fori_loop(0, LIVE // 2, fold_step, 0)
+    def fold(tile):
+        far[tile] += fold_own(own[tile, 0])
+        for axis in range(3):
+            force[tile, axis] += fold_own(own[tile, 1 + axis])
+
+    fold_rows(fold, 4)
     charge = plain[2] * inverse
     sums = jnp.sum(far[...], axis=1) * (0.5 * SCALE) * inverse + 0.5 * charge * charge
     own_grad[...] = sums[0:HALF]
     above_grad[...] = sums[HALF:]
-    edge_rows(to_next, sums, TILES, HALF + TILES)
-    edge_rows(to_last, sums, 0, HALF)
+    edge_rounds(sums, round_one, round_two)
 
 
 def force_kernel(
@@ -431,8 +439,7 @@
     full_copy = ring_copies(full_ring, d_pair, full_sems, FULL_RING, ATOMS)
     part_copy = ring_copies(part_ring, d_pair, part_sems, PART_RING, PART)
 
-    def self_copy(tile):
-        return pltpu.make_async_copy(d_self.at[tile], self_ring.at[tile], self_sems.at[tile])
+    self_copy = pltpu.make_async_copy(d_self, self_ring, self_sems.at[0])
 
     def start(copy, base):
         def step(index, carry):
@@ -441,8 +448,7 @@
 
         return step
 
-    for tile in range(TILES):
-        self_copy(tile).start()
+    self_copy.start()
     lax.fori_loop(0, jnp.minimum(fulls, FULL_RING), start(full_copy, 0), 0)
     lax.fori_loop(0, jnp.minimum(parts, PART_RING), start(part_copy, fulls), 0)
 
@@ -475,10 +481,10 @@
         for axis in range(3):
             far[second, axis] -= fold2(sums[axis])
 
+    self_copy.wait()
+
     def self_step(quad, carry):
         begin = quad * 4
-        for k in range(4):
-            self_copy(begin + k).wait()
         for k in range(4):
             tile = begin + k
             pair(
@@ -534,14 +540,11 @@
         lambda first, second: part_starts(reach[first * REGION + second]),
     )
 
-    def fold_step(pairs, carry):
-        for k in range(2):
-            tile = pairs * 2 + k
-            for axis in range(3):
-                far[tile, axis] += fold_own(own[tile, axis])
-        return carry
-
-    lax.fori_loop(0, LIVE // 2, fold_step, 0)
+    def fold(tile):
+        for axis in range(3):
+            far[tile, axis] += fold_own(own[tile, axis])
+
+    fold_rows(fold, 4)
     for axis in range(3):
         sums = jnp.sum(far[:, axis], axis=1) * (-SCALE * SCALE / 16.0)
         own_force[axis] = sums[0:TILES]
@@ -702,6 +705,12 @@
     return lax.ppermute(block, "tile", [(i, (i + 1) % count) for i in range(count)])
 
 
+def pairwise(block, last):
+    count = lax.axis_size("tile")
+    pairs = [(i, (i + (-1 if (i % 2 == 0) == last else 1)) % count) for i in range(count)]
+    return lax.ppermute(block, "tile", pairs)
+
+
 def across_to_here(block):
     slabs, count = lax.axis_size("slab"), lax.axis_size("tile")
     pairs = [
@@ -718,9 +727,10 @@
     )
 
 
-def swap_sums(own, above, to_next, to_last):
-    from_last = here_to_next(to_next)
-    from_next = next_to_here(to_last)
+def swap_sums(own, above, round_one, round_two):
+    one, two = pairwise(round_one, False), pairwise(round_two, True)
+    is_even = lax.axis_index("tile") % 2 == 0
+    from_next, from_last = jnp.where(is_even, one, two), jnp.where(is_even, two, one)
     own = own + placed(from_last, 0, from_next)
     above = above + placed(from_last, EDGE, from_next)
     own, above = lax.optimization_barrier((own, above))
@@ -737,22 +747,24 @@
     return lax.ppermute(block, ("slab", "tile"), pairs)
 
 
-def whole_slab(component, block, edges):
-    first, edge = component * TILES, component * EDGE
-    return [block[first : first + TILES], edges[edge : edge + EDGE], jnp.zeros((HALF - LIVE, ATOMS), F32)]
-
-
-def chunk_reach(sent, edges, above, above_edges):
-    x, y, z = (
-        jnp.concatenate(whole_slab(axis, sent, edges) + whole_slab(axis, above, above_edges)) for axis in range(3)
-    )
-    across, along = sent[TILES // 2, 0], sent[TILES + TILES // 2, 0]
-    inverse = lax.rsqrt(across * across + along * along)
-    across, along = across * inverse, along * inverse
-    turned = jnp.stack([x * across + y * along, y * across - x * along, z])
-    pieces = turned.reshape(3, REGION, CHUNKS, CHUNK)
+def slab_boxes(block, edges, across, along):
+    rows = [
+        jnp.concatenate(
+            [
+                block[axis * TILES : (axis + 1) * TILES],
+                edges[axis * EDGE : (axis + 1) * EDGE],
+                jnp.zeros((HALF - LIVE, ATOMS), F32),
+            ]
+        )
+        for axis in range(3)
+    ]
+    x, y, z = rows
+    pieces = jnp.stack([x * across + y * along, y * across - x * along, z]).reshape(3, HALF, CHUNKS, CHUNK)
     low, high = jnp.min(pieces, axis=3), jnp.max(pieces, axis=3)
-    tile_low, tile_high = jnp.min(low, axis=2), jnp.max(high, axis=2)
+    return low, high, jnp.min(low, axis=2), jnp.max(high, axis=2)
+
+
+def chunk_codes(low, high, tile_low, tile_high):
     near = []
     for chunk in range(CHUNKS):
         own_low, own_high = low[:, :OWN_ROWS, chunk, None], high[:, :OWN_ROWS, chunk, None]
@@ -766,7 +778,18 @@
         rank = jnp.where(near[chunk] == 1, before, number + chunk - before)
         code = code + (chunk << (3 * rank))
         before = before + near[chunk]
-    return code.reshape(-1), number <= CHUNKS // 2
+    return code
+
+
+def chunk_reach(sent, edges, above, above_edges):
+    across, along = sent[TILES // 2, 0], sent[TILES + TILES // 2, 0]
+    inverse = lax.rsqrt(across * across + along * along)
+    across, along = across * inverse, along * inverse
+    low, high, *tile = slab_boxes(sent, edges, across, along)
+    *_, above_low, above_high = slab_boxes(above, above_edges, across, along)
+    own_codes = chunk_codes(low, high, *tile)
+    code = jnp.concatenate([own_codes, chunk_codes(low, high, above_low, above_high)], axis=1)
+    return code.reshape(-1), (code >> (3 * CHUNKS)) <= CHUNKS // 2
 
 
 def packed(first, second, valid, is_part):

time: 202 us -> 191 us (0.946)
  the two profiles are of different devices: /device:TPU:22 before, /device:TPU:24 now
where the time goes in v5:
time: 191 us; the launch traced here: 189 us
  starting transfers between devices  78 us (41%)
  Pallas kernels  68.6 us (36%)
  waiting for transfers between devices  21.5 us (11%)
  other arithmetic  9.29 us (5%)
  between operations  6.45 us (3%)
  local copies, waits for them, and re-layouts  5.3 us (3%)
    pallas_call x1, Pallas kernels, run_born(): pl.pallas_call(born_kernel, name='born_sums', out_shape=(f32(HALF, ATOMS)...  29.6 us
    ppermute x4, starting transfers between devices, pairwise(): return lax.ppermute(block, 'tile', pairs)  24.2 us
    pallas_call x1, Pallas kernels, run_energy(): pl.pallas_call(energy_kernel, name='radius_gradient', out_shape=(f32(TILE...  21.7 us
    ppermute x3, waiting for transfers between devices, here_to_above(): return lax.ppermute(block, 'slab', [(i, i + 1) for i in range(ends)])  17.1 us
    pallas_call x1, Pallas kernels, run_force(): pl.pallas_call(force_kernel, name='forces', out_shape=(f32(TILES, ATOMS),...  15.8 us
    ppermute x3, starting transfers between devices, above_to_here(): return lax.ppermute(block, 'slab', [(i + 1, i) for i in range(ends)])  15.8 us
    ppermute x3, starting transfers between devices, here_to_above(): return lax.ppermute(block, 'slab', [(i, i + 1) for i in range(ends)])  13.6 us
    ppermute x1, starting transfers between devices, across_to_here(): return lax.ppermute(block, ('slab', 'tile'), pairs)  13.2 us
  transfers between devices with their start and end apart: 14, of which 6 were waited for; matrix products, arithmetic and copies ran while one was open for 2% of the time, Pallas kernels for 0%

profile of v5, /device:TPU:24, one launch (start us, length us, event | category | flops | bytes accessed | tf_op | source)
XLA Modules:
  0.0 189.5 jit_solution(2612953511640672090)
XLA Ops:
  0.6 1.5 pack_atoms.1
  2.1 13.2 %collective-permute-start.2 = (f32[16,128]{1,0:T(8,128)}, f32[16,128]{1,0:T(8,128)S(1)}, u32[]{:S(2)}, u32[]{:S(2)}) collective-permute-start(f32[16,128]{1,0:T(8,128)} %get-tuple-element.32), channel_id=1, source_target_pairs={{33,0},{34,1},{35,2},{36,3},{37,4},{38,5},{39,6},{40,7},{41,8},{42... | collective-permute-start | bytes 24584 | tf_op jit(solution)/shard_map/ppermute | solution.py:721
  15.4 5.4 %collective-permute-start.1 = (f32[16,128]{1,0:T(8,128)}, f32[16,128]{1,0:T(8,128)S(1)}, u32[]{:S(2)}, u32[]{:S(2)}) collective-permute-start(f32[16,128]{1,0:T(8,128)} %get-tuple-element.32), channel_id=1, source_target_pairs={{1,0},{2,1},{3,2},{4,3},{5,4},{6,5},{7,6},{8,7},{9,8},{10,9},{11,1... | collective-permute-start | bytes 24584 | tf_op jit(solution)/shard_map/ppermute | solution.py:700
  20.8 5.5 %collective-permute-start = (f32[200,128]{1,0:T(8,128)}, f32[200,128]{1,0:T(8,128)S(1)}, u32[]{:S(2)}, u32[]{:S(2)}) collective-permute-start(f32[200,128]{1,0:T(8,128)} %get-tuple-element.31.sent), channel_id=1, source_target_pairs={{32,0},{64,32},{96,64},{128,96},{160,128},{192,160},{224,192},{256... | collective-permute-start | bytes 307208 | tf_op jit(solution)/shard_map/ppermute | solution.py:690
  41.2 29.6 %born_sums.1 = (f32[40,128]{1,0:T(8,128)}, f32[40,128]{1,0:T(8,128)}, f32[8,128]{1,0:T(8,128)}, f32[8,128]{1,0:T(8,128)}, f32[80,8,128]{2,1,0:T(8,128)}, /*index...) custom-call(s32[2]{0:T(128)} %pad_add_fusion.4.total, s32[512]{0:T(512)} %broadcast_add_fusion.items, ...), custom_call_target="tpu_custom_call" | custom-call | tf_op jit(solution)/shard_map/born_sums/pallas_call | solution.py:592
  70.8 10.8 %collective-permute-start.3 = (f32[8,128]{1,0:T(8,128)}, f32[8,128]{1,0:T(8,128)S(1)}, u32[]{:S(2)}, u32[]{:S(2)}) collective-permute-start(f32[8,128]{1,0:T(8,128)} %get-tuple-element.36), channel_id=1, source_target_pairs={{0,31},{1,2},{2,1},{3,4},{4,3},{5,6},{6,5},{7,8},{8,7},{9,10},{10,... | collective-permute-start | bytes 12296 | tf_op jit(solution)/shard_map/ppermute | solution.py:711
  81.6 1.9 %collective-permute-start.4 = (f32[8,128]{1,0:T(8,128)}, f32[8,128]{1,0:T(8,128)S(1)}, u32[]{:S(2)}, u32[]{:S(2)}) collective-permute-start(f32[8,128]{1,0:T(8,128)} %get-tuple-element.37), channel_id=1, source_target_pairs={{0,1},{1,0},{2,3},{3,2},{4,5},{5,4},{6,7},{7,6},{8,9},{9,8},{10,11... | collective-permute-start | bytes 12296 | tf_op jit(solution)/shard_map/ppermute | solution.py:711
  86.4 8.4 %collective-permute-start.6 = (f32[40,128]{1,0:T(8,128)S(1)}, f32[40,128]{1,0:T(8,128)S(1)}, u32[]{:S(2)}, u32[]{:S(2)}) collective-permute-start(f32[40,128]{1,0:T(8,128)S(1)} %add_add_fusion.3.own_part), channel_id=1, source_target_pairs={{32,0},{64,32},{96,64},{128,96},{160,128},{192,160},{224,192},{256... | collective-permute-start | bytes 61448 | tf_op jit(solution)/shard_map/ppermute | solution.py:690
  94.8 1.9 %collective-permute-start.5 = (f32[40,128]{1,0:T(8,128)S(1)}, f32[40,128]{1,0:T(8,128)S(1)}, u32[]{:S(2)}, u32[]{:S(2)}) collective-permute-start(f32[40,128]{1,0:T(8,128)S(1)} %add_add_fusion.2.above_part), channel_id=1, source_target_pairs={{0,32},{32,64},{64,96},{96,128},{128,160},{160,192},{192,224},{224... | collective-permute-start | bytes 61448 | tf_op jit(solution)/shard_map/ppermute | solution.py:695
  96.7 8.5 %collective-permute-done.5.from_below = f32[40,128]{1,0:T(8,128)S(1)} collective-permute-done((f32[40,128]{1,0:T(8,128)S(1)}, f32[40,128]{1,0:T(8,128)S(1)}, u32[]{:S(2)}, u32[]{:S(2)}) %collective-permute-start.5) | collective-permute-done | bytes 20512 | tf_op jit(solution)/shard_map/ppermute | solution.py:695
  105.8 21.7 %radius_gradient.1 = (f32[32,128]{1,0:T(8,128)}, f32[80,128]{1,0:T(8,128)}, f32[40,128]{1,0:T(8,128)}, f32[40,128]{1,0:T(8,128)}, f32[8,128]{1,0:T(8,128)}, /*index=5*/f32[8,128]{1,0:T(8,128)}, f32[80,3,8,128]{3,2,1,0:T(8,128)}) custom-call(s32[2]{0:T(128)} %pad_add_fusion.4.total, s32[512]{0:T(512)} %broadcast_add_fusion.items, s32[2800]{0:T(1024)} %reshape.400.reach, ...), custom_call_target="tpu_custom_call" | custom-call | tf_op jit(solution)/shard_map/radius_gradient/pallas_call | solution.py:621
  127.6 9.5 %collective-permute-start.7 = (f32[8,128]{1,0:T(8,128)}, f32[8,128]{1,0:T(8,128)S(1)}, u32[]{:S(2)}, u32[]{:S(2)}) collective-permute-start(f32[8,128]{1,0:T(8,128)} %get-tuple-element.44), channel_id=1, source_target_pairs={{0,31},{1,2},{2,1},{3,4},{4,3},{5,6},{6,5},{7,8},{8,7},{9,10},{10,... | collective-permute-start | bytes 12296 | tf_op jit(solution)/shard_map/ppermute | solution.py:711
  137.1 1.9 %collective-permute-start.8 = (f32[8,128]{1,0:T(8,128)}, f32[8,128]{1,0:T(8,128)S(1)}, u32[]{:S(2)}, u32[]{:S(2)}) collective-permute-start(f32[8,128]{1,0:T(8,128)} %get-tuple-element.45), channel_id=1, source_target_pairs={{0,1},{1,0},{2,3},{3,2},{4,5},{5,4},{6,7},{7,6},{8,9},{9,8},{10,11... | collective-permute-start | bytes 12296 | tf_op jit(solution)/shard_map/ppermute | solution.py:711
  139.0 1.3 collective-permute-done.8
  141.9 1.9 %collective-permute-start.10 = (f32[40,128]{1,0:T(8,128)S(1)}, f32[40,128]{1,0:T(8,128)S(1)}, u32[]{:S(2)}, u32[]{:S(2)}) collective-permute-start(f32[40,128]{1,0:T(8,128)S(1)} %add_add_fusion.1.own_grad), channel_id=1, source_target_pairs={{32,0},{64,32},{96,64},{128,96},{160,128},{192,160},{224,192},{256... | collective-permute-start | bytes 61448 | tf_op jit(solution)/shard_map/ppermute | solution.py:690
  143.8 7.8 %collective-permute-start.9 = (f32[40,128]{1,0:T(8,128)S(1)}, f32[40,128]{1,0:T(8,128)S(1)}, u32[]{:S(2)}, u32[]{:S(2)}) collective-permute-start(f32[40,128]{1,0:T(8,128)S(1)} %add_add_fusion.above_grad), channel_id=1, source_target_pairs={{0,32},{32,64},{64,96},{96,128},{128,160},{160,192},{192,224},{224... | collective-permute-start | bytes 61448 | tf_op jit(solution)/shard_map/ppermute | solution.py:695
  151.6 2.6 %collective-permute-done.9.from_below = f32[40,128]{1,0:T(8,128)S(1)} collective-permute-done((f32[40,128]{1,0:T(8,128)S(1)}, f32[40,128]{1,0:T(8,128)S(1)}, u32[]{:S(2)}, u32[]{:S(2)}) %collective-permute-start.9) | collective-permute-done | bytes 20512 | tf_op jit(solution)/shard_map/ppermute | solution.py:695
  154.9 15.8 %forces.1 = (f32[32,128]{1,0:T(8,128)}, f32[3,32,128]{2,1,0:T(8,128)}, f32[3,32,128]{2,1,0:T(8,128)}, f32[3,8,128]{2,1,0:T(8,128)}, f32[3,8,128]{2,1,0:T(8,128)}) custom-call(s32[2]{0:T(128)} %pad_add_fusion.4.total, s32[512]{0:T(512)} %broadcast_add_fusion.items, s32[2800]{0:T(1024)} %reshape.400.reach, f32[80,8,128]{2,1,0:T(8,128)} %get-tuple-element.33.data, ...), custom_call_target="tpu_custom_call" | custom-call | tf_op jit(solution)/shard_map/forces/pallas_call | solution.py:648
  170.7 1.9 %collective-permute-start.12 = (f32[3,8,128]{2,1,0:T(8,128)}, f32[3,8,128]{2,1,0:T(8,128)S(1)}, u32[]{:S(2)}, u32[]{:S(2)}) collective-permute-start(f32[3,8,128]{2,1,0:T(8,128)} %get-tuple-element.55), channel_id=1, source_target_pairs={{0,1},{1,2},{2,3},{3,4},{4,5},{5,6},{6,7},{7,8},{8,9},{9,10},{10,1... | collective-permute-start | bytes 36872 | tf_op jit(solution)/shard_map/ppermute | solution.py:705
  172.6 3.9 %collective-permute-start.13 = (f32[3,8,128]{2,1,0:T(8,128)}, f32[3,8,128]{2,1,0:T(8,128)S(1)}, u32[]{:S(2)}, u32[]{:S(2)}) collective-permute-start(f32[3,8,128]{2,1,0:T(8,128)} %get-tuple-element.56), channel_id=1, source_target_pairs={{0,33},{1,34},{2,35},{3,36},{4,37},{5,38},{6,39},{7,40},{8,41},{9,... | collective-permute-start | bytes 36872 | tf_op jit(solution)/shard_map/ppermute | solution.py:747
  176.5 3.8 %collective-permute-start.11 = (f32[3,32,128]{2,1,0:T(8,128)}, f32[3,32,128]{2,1,0:T(8,128)S(1)}, u32[]{:S(2)}, u32[]{:S(2)}) collective-permute-start(f32[3,32,128]{2,1,0:T(8,128)} %get-tuple-element.54), channel_id=1, source_target_pairs={{0,32},{32,64},{64,96},{96,128},{128,160},{160,192},{192,224},{224... | collective-permute-start | bytes 147464 | tf_op jit(solution)/shard_map/ppermute | solution.py:695
  180.4 1.8 collective-permute-done.13
  182.2 5.9 %collective-permute-done.11 = f32[3,32,128]{2,1,0:T(8,128)S(1)} collective-permute-done((f32[3,32,128]{2,1,0:T(8,128)}, f32[3,32,128]{2,1,0:T(8,128)S(1)}, u32[]{:S(2)}, u32[]{:S(2)}) %collective-permute-start.11) | collective-permute-done | bytes 49184 | tf_op jit(solution)/shard_map/ppermute | solution.py:695
  188.1 1.4 add_bitcast_fusion
  (106 shorter events, 14.8 us)
Async XLA Ops:
  2.1 31.8 %collective-permute-start.2 = (f32[16,128]{1,0:T(8,128)}, f32[16,128]{1,0:T(8,128)S(1)}, u32[]{:S(2)}, u32[]{:S(2)}) collective-permute-start(f32[16,128]{1,0:T(8,128)} %get-tuple-element.32), channel_id=1, source_target_pairs={{33,0},{34,1},{35,2},{36,3},{37,4},{38,5},{39,6},{40,7},{41,8},{42... | collective-permute-start | bytes 24584 | tf_op jit(solution)/shard_map/ppermute | solution.py:721
  15.4 18.6 %collective-permute-start.1 = (f32[16,128]{1,0:T(8,128)}, f32[16,128]{1,0:T(8,128)S(1)}, u32[]{:S(2)}, u32[]{:S(2)}) collective-permute-start(f32[16,128]{1,0:T(8,128)} %get-tuple-element.32), channel_id=1, source_target_pairs={{1,0},{2,1},{3,2},{4,3},{5,4},{6,5},{7,6},{8,7},{9,8},{10,9},{11,1... | collective-permute-start | bytes 24584 | tf_op jit(solution)/shard_map/ppermute | solution.py:700
  20.8 13.6 %collective-permute-start = (f32[200,128]{1,0:T(8,128)}, f32[200,128]{1,0:T(8,128)S(1)}, u32[]{:S(2)}, u32[]{:S(2)}) collective-permute-start(f32[200,128]{1,0:T(8,128)} %get-tuple-element.31.sent), channel_id=1, source_target_pairs={{32,0},{64,32},{96,64},{128,96},{160,128},{192,160},{224,192},{256... | collective-permute-start | bytes 307208 | tf_op jit(solution)/shard_map/ppermute | solution.py:690
  33.9 7.2 %copy-start.9 = (f32[16,128]{1,0:T(8,128)}, f32[16,128]{1,0:T(8,128)S(1)}, u32[]{:S(2)}) copy-start(f32[16,128]{1,0:T(8,128)S(1)} %collective-permute-done.2.above_edges) | copy-start | bytes 24580
  33.9 7.2 %copy-start.10 = (f32[16,128]{1,0:T(8,128)}, f32[16,128]{1,0:T(8,128)S(1)}, u32[]{:S(2)}) copy-start(f32[16,128]{1,0:T(8,128)S(1)} %collective-permute-done.1.edges) | copy-start | bytes 24580
  34.4 6.8 %copy-start = (f32[200,128]{1,0:T(8,128)}, f32[200,128]{1,0:T(8,128)S(1)}, u32[]{:S(2)}) copy-start(f32[200,128]{1,0:T(8,128)S(1)} %collective-permute-done.above) | copy-start | bytes 307204
  70.8 12.8 %collective-permute-start.3 = (f32[8,128]{1,0:T(8,128)}, f32[8,128]{1,0:T(8,128)S(1)}, u32[]{:S(2)}, u32[]{:S(2)}) collective-permute-start(f32[8,128]{1,0:T(8,128)} %get-tuple-element.36), channel_id=1, source_target_pairs={{0,31},{1,2},{2,1},{3,4},{4,3},{5,6},{6,5},{7,8},{8,7},{9,10},{10,... | collective-permute-start | bytes 12296 | tf_op jit(solution)/shard_map/ppermute | solution.py:711
  81.6 3.3 %collective-permute-start.4 = (f32[8,128]{1,0:T(8,128)}, f32[8,128]{1,0:T(8,128)S(1)}, u32[]{:S(2)}, u32[]{:S(2)}) collective-permute-start(f32[8,128]{1,0:T(8,128)} %get-tuple-element.37), channel_id=1, source_target_pairs={{0,1},{1,0},{2,3},{3,2},{4,5},{5,4},{6,7},{7,6},{8,9},{9,8},{10,11... | collective-permute-start | bytes 12296 | tf_op jit(solution)/shard_map/ppermute | solution.py:711
  85.6 19.6 %copy-start.1 = (f32[40,128]{1,0:T(8,128)}, f32[40,128]{1,0:T(8,128)S(1)}, u32[]{:S(2)}) copy-start(f32[40,128]{1,0:T(8,128)S(1)} %add_add_fusion.3.own_part) | copy-start | bytes 61444
  86.4 18.9 %copy-start.2 = (f32[40,128]{1,0:T(8,128)}, f32[40,128]{1,0:T(8,128)S(1)}, u32[]{:S(2)}) copy-start(f32[40,128]{1,0:T(8,128)S(1)} %add_add_fusion.2.above_part) | copy-start | bytes 61444
  86.4 10.3 %collective-permute-start.6 = (f32[40,128]{1,0:T(8,128)S(1)}, f32[40,128]{1,0:T(8,128)S(1)}, u32[]{:S(2)}, u32[]{:S(2)}) collective-permute-start(f32[40,128]{1,0:T(8,128)S(1)} %add_add_fusion.3.own_part), channel_id=1, source_target_pairs={{32,0},{64,32},{96,64},{128,96},{160,128},{192,160},{224,192},{256... | collective-permute-start | bytes 61448 | tf_op jit(solution)/shard_map/ppermute | solution.py:690
  94.8 10.5 %collective-permute-start.5 = (f32[40,128]{1,0:T(8,128)S(1)}, f32[40,128]{1,0:T(8,128)S(1)}, u32[]{:S(2)}, u32[]{:S(2)}) collective-permute-start(f32[40,128]{1,0:T(8,128)S(1)} %add_add_fusion.2.above_part), channel_id=1, source_target_pairs={{0,32},{32,64},{64,96},{96,128},{128,160},{160,192},{192,224},{224... | collective-permute-start | bytes 61448 | tf_op jit(solution)/shard_map/ppermute | solution.py:695
  96.7 8.6 %copy-start.5 = (f32[40,128]{1,0:T(8,128)}, f32[40,128]{1,0:T(8,128)S(1)}, u32[]{:S(2)}) copy-start(f32[40,128]{1,0:T(8,128)S(1)} %collective-permute-done.6.from_above) | copy-start | bytes 61444
  127.6 11.5 %collective-permute-start.7 = (f32[8,128]{1,0:T(8,128)}, f32[8,128]{1,0:T(8,128)S(1)}, u32[]{:S(2)}, u32[]{:S(2)}) collective-permute-start(f32[8,128]{1,0:T(8,128)} %get-tuple-element.44), channel_id=1, source_target_pairs={{0,31},{1,2},{2,1},{3,4},{4,3},{5,6},{6,5},{7,8},{8,7},{9,10},{10,... | collective-permute-start | bytes 12296 | tf_op jit(solution)/shard_map/ppermute | solution.py:711
  137.1 3.3 %collective-permute-start.8 = (f32[8,128]{1,0:T(8,128)}, f32[8,128]{1,0:T(8,128)S(1)}, u32[]{:S(2)}, u32[]{:S(2)}) collective-permute-start(f32[8,128]{1,0:T(8,128)} %get-tuple-element.45), channel_id=1, source_target_pairs={{0,1},{1,0},{2,3},{3,2},{4,5},{5,4},{6,7},{7,6},{8,9},{9,8},{10,11... | collective-permute-start | bytes 12296 | tf_op jit(solution)/shard_map/ppermute | solution.py:711
  141.1 13.2 %copy-start.3 = (f32[40,128]{1,0:T(8,128)}, f32[40,128]{1,0:T(8,128)S(1)}, u32[]{:S(2)}) copy-start(f32[40,128]{1,0:T(8,128)S(1)} %add_add_fusion.1.own_grad) | copy-start | bytes 61444
  141.9 12.4 %copy-start.4 = (f32[40,128]{1,0:T(8,128)}, f32[40,128]{1,0:T(8,128)S(1)}, u32[]{:S(2)}) copy-start(f32[40,128]{1,0:T(8,128)S(1)} %add_add_fusion.above_grad) | copy-start | bytes 61444
  141.9 9.8 %collective-permute-start.10 = (f32[40,128]{1,0:T(8,128)S(1)}, f32[40,128]{1,0:T(8,128)S(1)}, u32[]{:S(2)}, u32[]{:S(2)}) collective-permute-start(f32[40,128]{1,0:T(8,128)S(1)} %add_add_fusion.1.own_grad), channel_id=1, source_target_pairs={{32,0},{64,32},{96,64},{128,96},{160,128},{192,160},{224,192},{256... | collective-permute-start | bytes 61448 | tf_op jit(solution)/shard_map/ppermute | solution.py:690
  143.8 10.5 %collective-permute-start.9 = (f32[40,128]{1,0:T(8,128)S(1)}, f32[40,128]{1,0:T(8,128)S(1)}, u32[]{:S(2)}, u32[]{:S(2)}) collective-permute-start(f32[40,128]{1,0:T(8,128)S(1)} %add_add_fusion.above_grad), channel_id=1, source_target_pairs={{0,32},{32,64},{64,96},{96,128},{128,160},{160,192},{192,224},{224... | collective-permute-start | bytes 61448 | tf_op jit(solution)/shard_map/ppermute | solution.py:695
  151.6 2.7 %copy-start.7 = (f32[40,128]{1,0:T(8,128)}, f32[40,128]{1,0:T(8,128)S(1)}, u32[]{:S(2)}) copy-start(f32[40,128]{1,0:T(8,128)S(1)} %collective-permute-done.10.from_above) | copy-start | bytes 61444
  154.3 0.6 copy-start.8
  170.7 9.7 %collective-permute-start.12 = (f32[3,8,128]{2,1,0:T(8,128)}, f32[3,8,128]{2,1,0:T(8,128)S(1)}, u32[]{:S(2)}, u32[]{:S(2)}) collective-permute-start(f32[3,8,128]{2,1,0:T(8,128)} %get-tuple-element.55), channel_id=1, source_target_pairs={{0,1},{1,2},{2,3},{3,4},{4,5},{5,6},{6,7},{7,8},{8,9},{9,10},{10,1... | collective-permute-start | bytes 36872 | tf_op jit(solution)/shard_map/ppermute | solution.py:705
  172.6 9.5 %collective-permute-start.13 = (f32[3,8,128]{2,1,0:T(8,128)}, f32[3,8,128]{2,1,0:T(8,128)S(1)}, u32[]{:S(2)}, u32[]{:S(2)}) collective-permute-start(f32[3,8,128]{2,1,0:T(8,128)} %get-tuple-element.56), channel_id=1, source_target_pairs={{0,33},{1,34},{2,35},{3,36},{4,37},{5,38},{6,39},{7,40},{8,41},{9,... | collective-permute-start | bytes 36872 | tf_op jit(solution)/shard_map/ppermute | solution.py:747
  176.5 11.6 %collective-permute-start.11 = (f32[3,32,128]{2,1,0:T(8,128)}, f32[3,32,128]{2,1,0:T(8,128)S(1)}, u32[]{:S(2)}, u32[]{:S(2)}) collective-permute-start(f32[3,32,128]{2,1,0:T(8,128)} %get-tuple-element.54), channel_id=1, source_target_pairs={{0,32},{32,64},{64,96},{96,128},{128,160},{160,192},{192,224},{224... | collective-permute-start | bytes 147464 | tf_op jit(solution)/shard_map/ppermute | solution.py:695
  (1 other events, 0.6 us)

commit v6 on v5

--- a/solution.py
+++ b/solution.py
@@ -27,11 +27,11 @@
 ATOMS = 128
 CHUNK = 16
 CHUNKS = ATOMS // CHUNK
-FULL_WIDTH = 2
+FULL_WIDTH = 4
 PART_WIDTH = 4
 FULL_RING = 32
 PART_RING = 32
-PAIRS = 2 * TILES * LISTED + 4
+PAIRS = 2 * TILES * LISTED + 6
 ITEMS = 512
 DUMMY = LIVE * ATOMS + LIVE
 ROW = (1, ATOMS)
@@ -845,9 +845,10 @@
     gradient, own, over, to_next, to_across = run_force(
         total, items, reach, data, slope, shares, force, d_self, d_pair
     )
-    from_below = here_to_above(over)
-    edge = here_to_next(to_next) + here_to_across(to_across)
-    forces = own + from_below + jnp.pad(edge[:, 0:EDGE], ((0, 0), (0, TILES - EDGE), (0, 0)))
+    forces, to_next, to_across = lax.optimization_barrier(
+        (own + here_to_above(over), here_to_next(to_next), here_to_across(to_across))
+    )
+    forces = forces + jnp.pad((to_next + to_across)[:, 0:EDGE], ((0, 0), (0, TILES - EDGE), (0, 0)))
     return (radii_born[None, None], gradient[None, None], jnp.swapaxes(forces, 0, 1)[None, None])
 
 

time: 191 us -> 193 us (1.010)
  starting transfers between devices: 78 us -> 59.9 us
  Pallas kernels: 68.6 us -> 83.1 us
  waiting for transfers between devices: 21.5 us -> 27.8 us
    ppermute x4, starting transfers between devices: 24.2 us -> 7.67 us  [pairwise(): return lax.ppermute(block, 'tile', pairs)]
    ppermute x4, waiting for transfers between devices: 2.66 us -> 10.6 us  [pairwise(): return lax.ppermute(block, 'tile', pairs)]
    pallas_call x1, Pallas kernels: 29.6 us -> 37 us  [run_born(): pl.pallas_call(born_kernel, name='born_sums', out_shape=(f32(HALF, ATOMS)...]
    pallas_call x1, Pallas kernels: 21.7 us -> 26.4 us  [run_energy(): pl.pallas_call(energy_kernel, name='radius_gradient', out_shape=(f32(TILE...]
    ppermute x3, waiting for transfers between devices: 17.1 us -> 12.5 us  [here_to_above(): return lax.ppermute(block, 'slab', [(i, i + 1) for i in range(ends)])]
    pallas_call x1, Pallas kernels: 15.8 us -> 18.2 us  [run_force(): pl.pallas_call(force_kernel, name='forces', out_shape=(f32(TILES, ATOMS),...]
    ppermute x1, waiting for transfers between devices: 0.01 us -> 2.09 us  [here_to_next(): lax.ppermute(block, 'tile', [(i, (i + 1) % count) for i in range(count)])]
    ppermute x3, starting transfers between devices: 13.6 us -> 15.5 us  [here_to_above(): return lax.ppermute(block, 'slab', [(i, i + 1) for i in range(ends)])]
  transfers between devices with their start and end apart: 14 -> 14, of which waited for: 6 -> 7; matrix products, arithmetic and copies ran while one was open for 2% -> 3% of each run, Pallas kernels for 0% -> 0%
where the time goes in v6:
time: 193 us; the launch traced here: 192 us
  Pallas kernels  83.1 us (43%)
  starting transfers between devices  59.9 us (31%)
  waiting for transfers between devices  27.8 us (14%)
  other arithmetic  9.19 us (5%)
  between operations  6.31 us (3%)
  local copies, waits for them, and re-layouts  5.32 us (3%)
    pallas_call x1, Pallas kernels, run_born(): pl.pallas_call(born_kernel, name='born_sums', out_shape=(f32(HALF, ATOMS)...  37 us
    pallas_call x1, Pallas kernels, run_energy(): pl.pallas_call(energy_kernel, name='radius_gradient', out_shape=(f32(TILE...  26.4 us
    pallas_call x1, Pallas kernels, run_force(): pl.pallas_call(force_kernel, name='forces', out_shape=(f32(TILES, ATOMS),...  18.2 us
    ppermute x3, starting transfers between devices, here_to_above(): return lax.ppermute(block, 'slab', [(i, i + 1) for i in range(ends)])  15.5 us
    ppermute x3, starting transfers between devices, above_to_here(): return lax.ppermute(block, 'slab', [(i + 1, i) for i in range(ends)])  14.2 us
    ppermute x1, starting transfers between devices, across_to_here(): return lax.ppermute(block, ('slab', 'tile'), pairs)  13.2 us
    ppermute x3, waiting for transfers between devices, here_to_above(): return lax.ppermute(block, 'slab', [(i, i + 1) for i in range(ends)])  12.5 us
    ppermute x4, waiting for transfers between devices, pairwise(): return lax.ppermute(block, 'tile', pairs)  10.6 us
  transfers between devices with their start and end apart: 14, of which 7 were waited for; matrix products, arithmetic and copies ran while one was open for 3% of the time, Pallas kernels for 0%

profile of v6, /device:TPU:24, one launch (start us, length us, event | category | flops | bytes accessed | tf_op | source)
XLA Modules:
  0.0 191.9 jit_solution(17594272934333093239)
XLA Ops:
  2.1 13.2 %collective-permute-start.2 = (f32[16,128]{1,0:T(8,128)}, f32[16,128]{1,0:T(8,128)S(1)}, u32[]{:S(2)}, u32[]{:S(2)}) collective-permute-start(f32[16,128]{1,0:T(8,128)} %get-tuple-element.35), channel_id=1, source_target_pairs={{33,0},{34,1},{35,2},{36,3},{37,4},{38,5},{39,6},{40,7},{41,8},{42... | collective-permute-start | bytes 24584 | tf_op jit(solution)/shard_map/ppermute | solution.py:721
  15.4 5.4 %collective-permute-start.1 = (f32[16,128]{1,0:T(8,128)}, f32[16,128]{1,0:T(8,128)S(1)}, u32[]{:S(2)}, u32[]{:S(2)}) collective-permute-start(f32[16,128]{1,0:T(8,128)} %get-tuple-element.35), channel_id=1, source_target_pairs={{1,0},{2,1},{3,2},{4,3},{5,4},{6,5},{7,6},{8,7},{9,8},{10,9},{11,1... | collective-permute-start | bytes 24584 | tf_op jit(solution)/shard_map/ppermute | solution.py:700
  20.8 5.5 %collective-permute-start = (f32[200,128]{1,0:T(8,128)}, f32[200,128]{1,0:T(8,128)S(1)}, u32[]{:S(2)}, u32[]{:S(2)}) collective-permute-start(f32[200,128]{1,0:T(8,128)} %get-tuple-element.34.sent), channel_id=1, source_target_pairs={{32,0},{64,32},{96,64},{128,96},{160,128},{192,160},{224,192},{256... | collective-permute-start | bytes 307208 | tf_op jit(solution)/shard_map/ppermute | solution.py:690
  40.9 37.0 %born_sums.1 = (f32[40,128]{1,0:T(8,128)}, f32[40,128]{1,0:T(8,128)}, f32[8,128]{1,0:T(8,128)}, f32[8,128]{1,0:T(8,128)}, f32[80,8,128]{2,1,0:T(8,128)}, /*index...) custom-call(s32[2]{0:T(128)} %pad_add_fusion.4.total, s32[512]{0:T(512)} %broadcast_add_fusion.items, ...), custom_call_target="tpu_custom_call" | custom-call | tf_op jit(solution)/shard_map/born_sums/pallas_call | solution.py:592
  78.0 1.9 %collective-permute-start.3 = (f32[8,128]{1,0:T(8,128)}, f32[8,128]{1,0:T(8,128)S(1)}, u32[]{:S(2)}, u32[]{:S(2)}) collective-permute-start(f32[8,128]{1,0:T(8,128)} %get-tuple-element.39), channel_id=1, source_target_pairs={{0,31},{1,2},{2,1},{3,4},{4,3},{5,6},{6,5},{7,8},{8,7},{9,10},{10,... | collective-permute-start | bytes 12296 | tf_op jit(solution)/shard_map/ppermute | solution.py:711
  79.9 1.9 %collective-permute-start.4 = (f32[8,128]{1,0:T(8,128)}, f32[8,128]{1,0:T(8,128)S(1)}, u32[]{:S(2)}, u32[]{:S(2)}) collective-permute-start(f32[8,128]{1,0:T(8,128)} %get-tuple-element.40), channel_id=1, source_target_pairs={{0,1},{1,0},{2,3},{3,2},{4,5},{5,4},{6,7},{7,6},{8,9},{9,8},{10,11... | collective-permute-start | bytes 12296 | tf_op jit(solution)/shard_map/ppermute | solution.py:711
  81.9 5.2 %collective-permute-done.3 = f32[8,128]{1,0:T(8,128)S(1)} collective-permute-done((f32[8,128]{1,0:T(8,128)}, f32[8,128]{1,0:T(8,128)S(1)}, u32[]{:S(2)}, u32[]{:S(2)}) %collective-permute-start.3) | collective-permute-done | bytes 4128 | tf_op jit(solution)/shard_map/ppermute | solution.py:711
  88.5 6.8 %collective-permute-start.6 = (f32[40,128]{1,0:T(8,128)S(1)}, f32[40,128]{1,0:T(8,128)S(1)}, u32[]{:S(2)}, u32[]{:S(2)}) collective-permute-start(f32[40,128]{1,0:T(8,128)S(1)} %add_add_fusion.3.own_part), channel_id=1, source_target_pairs={{32,0},{64,32},{96,64},{128,96},{160,128},{192,160},{224,192},{256... | collective-permute-start | bytes 61448 | tf_op jit(solution)/shard_map/ppermute | solution.py:690
  95.3 2.9 %collective-permute-start.5 = (f32[40,128]{1,0:T(8,128)S(1)}, f32[40,128]{1,0:T(8,128)S(1)}, u32[]{:S(2)}, u32[]{:S(2)}) collective-permute-start(f32[40,128]{1,0:T(8,128)S(1)} %add_add_fusion.2.above_part), channel_id=1, source_target_pairs={{0,32},{32,64},{64,96},{96,128},{128,160},{160,192},{192,224},{224... | collective-permute-start | bytes 61448 | tf_op jit(solution)/shard_map/ppermute | solution.py:695
  98.3 7.5 %collective-permute-done.5.from_below = f32[40,128]{1,0:T(8,128)S(1)} collective-permute-done((f32[40,128]{1,0:T(8,128)S(1)}, f32[40,128]{1,0:T(8,128)S(1)}, u32[]{:S(2)}, u32[]{:S(2)}) %collective-permute-start.5) | collective-permute-done | bytes 20512 | tf_op jit(solution)/shard_map/ppermute | solution.py:695
  106.4 26.4 %radius_gradient.1 = (f32[32,128]{1,0:T(8,128)}, f32[80,128]{1,0:T(8,128)}, f32[40,128]{1,0:T(8,128)}, f32[40,128]{1,0:T(8,128)}, f32[8,128]{1,0:T(8,128)}, /*index=5*/f32[8,128]{1,0:T(8,128)}, f32[80,3,8,128]{3,2,1,0:T(8,128)}) custom-call(s32[2]{0:T(128)} %pad_add_fusion.4.total, s32[512]{0:T(512)} %broadcast_add_fusion.items, s32[2800]{0:T(1024)} %reshape.400.reach, ...), custom_call_target="tpu_custom_call" | custom-call | tf_op jit(solution)/shard_map/radius_gradient/pallas_call | solution.py:621
  132.8 1.9 collective-permute-start.7
  134.7 1.9 %collective-permute-start.8 = (f32[8,128]{1,0:T(8,128)}, f32[8,128]{1,0:T(8,128)S(1)}, u32[]{:S(2)}, u32[]{:S(2)}) collective-permute-start(f32[8,128]{1,0:T(8,128)} %get-tuple-element.48), channel_id=1, source_target_pairs={{0,1},{1,0},{2,3},{3,2},{4,5},{5,4},{6,7},{7,6},{8,9},{9,8},{10,11... | collective-permute-start | bytes 12296 | tf_op jit(solution)/shard_map/ppermute | solution.py:711
  136.6 5.4 %collective-permute-done.7 = f32[8,128]{1,0:T(8,128)S(1)} collective-permute-done((f32[8,128]{1,0:T(8,128)}, f32[8,128]{1,0:T(8,128)S(1)}, u32[]{:S(2)}, u32[]{:S(2)}) %collective-permute-start.7) | collective-permute-done | bytes 4128 | tf_op jit(solution)/shard_map/ppermute | solution.py:711
  143.5 1.9 collective-permute-start.10
  145.4 7.8 %collective-permute-start.9 = (f32[40,128]{1,0:T(8,128)S(1)}, f32[40,128]{1,0:T(8,128)S(1)}, u32[]{:S(2)}, u32[]{:S(2)}) collective-permute-start(f32[40,128]{1,0:T(8,128)S(1)} %add_add_fusion.above_grad), channel_id=1, source_target_pairs={{0,32},{32,64},{64,96},{96,128},{128,160},{160,192},{192,224},{224... | collective-permute-start | bytes 61448 | tf_op jit(solution)/shard_map/ppermute | solution.py:695
  153.3 2.6 %collective-permute-done.9.from_below = f32[40,128]{1,0:T(8,128)S(1)} collective-permute-done((f32[40,128]{1,0:T(8,128)S(1)}, f32[40,128]{1,0:T(8,128)S(1)}, u32[]{:S(2)}, u32[]{:S(2)}) %collective-permute-start.9) | collective-permute-done | bytes 20512 | tf_op jit(solution)/shard_map/ppermute | solution.py:695
  156.5 18.2 %forces.1 = (f32[32,128]{1,0:T(8,128)}, f32[3,32,128]{2,1,0:T(8,128)}, f32[3,32,128]{2,1,0:T(8,128)}, f32[3,8,128]{2,1,0:T(8,128)}, f32[3,8,128]{2,1,0:T(8,128)}) custom-call(s32[2]{0:T(128)} %pad_add_fusion.4.total, s32[512]{0:T(512)} %broadcast_add_fusion.items, s32[2800]{0:T(1024)} %reshape.400.reach, f32[80,8,128]{2,1,0:T(8,128)} %get-tuple-element.36.data, ...), custom_call_target="tpu_custom_call" | custom-call | tf_op jit(solution)/shard_map/forces/pallas_call | solution.py:648
  174.7 4.8 %collective-permute-start.11 = (f32[3,32,128]{2,1,0:T(8,128)}, f32[3,32,128]{2,1,0:T(8,128)S(1)}, u32[]{:S(2)}, u32[]{:S(2)}) collective-permute-start(f32[3,32,128]{2,1,0:T(8,128)} %get-tuple-element.57), channel_id=1, source_target_pairs={{0,32},{32,64},{64,96},{96,128},{128,160},{160,192},{192,224},{224... | collective-permute-start | bytes 147464 | tf_op jit(solution)/shard_map/ppermute | solution.py:695
  179.5 1.9 %collective-permute-start.12 = (f32[3,8,128]{2,1,0:T(8,128)}, f32[3,8,128]{2,1,0:T(8,128)S(1)}, u32[]{:S(2)}, u32[]{:S(2)}) collective-permute-start(f32[3,8,128]{2,1,0:T(8,128)} %get-tuple-element.58), channel_id=1, source_target_pairs={{0,1},{1,2},{2,3},{3,4},{4,5},{5,6},{6,7},{7,8},{8,9},{9,10},{10,1... | collective-permute-start | bytes 36872 | tf_op jit(solution)/shard_map/ppermute | solution.py:705
  181.4 1.9 %collective-permute-start.13 = (f32[3,8,128]{2,1,0:T(8,128)}, f32[3,8,128]{2,1,0:T(8,128)S(1)}, u32[]{:S(2)}, u32[]{:S(2)}) collective-permute-start(f32[3,8,128]{2,1,0:T(8,128)} %get-tuple-element.59), channel_id=1, source_target_pairs={{0,33},{1,34},{2,35},{3,36},{4,37},{5,38},{6,39},{7,40},{8,41},{9,... | collective-permute-start | bytes 36872 | tf_op jit(solution)/shard_map/ppermute | solution.py:747
  183.3 2.4 %collective-permute-done.11 = f32[3,32,128]{2,1,0:T(8,128)S(1)} collective-permute-done((f32[3,32,128]{2,1,0:T(8,128)}, f32[3,32,128]{2,1,0:T(8,128)S(1)}, u32[]{:S(2)}, u32[]{:S(2)}) %collective-permute-start.11) | collective-permute-done | bytes 49184 | tf_op jit(solution)/shard_map/ppermute | solution.py:695
  186.5 2.1 %collective-permute-done.12 = f32[3,8,128]{2,1,0:T(8,128)S(1)} collective-permute-done((f32[3,8,128]{2,1,0:T(8,128)}, f32[3,8,128]{2,1,0:T(8,128)S(1)}, u32[]{:S(2)}, u32[]{:S(2)}) %collective-permute-start.12) | collective-permute-done | bytes 12320 | tf_op jit(solution)/shard_map/ppermute | solution.py:705
  188.6 2.7 %collective-permute-done.13 = f32[3,8,128]{2,1,0:T(8,128)S(1)} collective-permute-done((f32[3,8,128]{2,1,0:T(8,128)}, f32[3,8,128]{2,1,0:T(8,128)S(1)}, u32[]{:S(2)}, u32[]{:S(2)}) %collective-permute-start.13) | collective-permute-done | bytes 12320 | tf_op jit(solution)/shard_map/ppermute | solution.py:747
  (107 shorter events, 16.4 us)
Async XLA Ops:
  2.1 31.8 %collective-permute-start.2 = (f32[16,128]{1,0:T(8,128)}, f32[16,128]{1,0:T(8,128)S(1)}, u32[]{:S(2)}, u32[]{:S(2)}) collective-permute-start(f32[16,128]{1,0:T(8,128)} %get-tuple-element.35), channel_id=1, source_target_pairs={{33,0},{34,1},{35,2},{36,3},{37,4},{38,5},{39,6},{40,7},{41,8},{42... | collective-permute-start | bytes 24584 | tf_op jit(solution)/shard_map/ppermute | solution.py:721
  15.4 18.6 %collective-permute-start.1 = (f32[16,128]{1,0:T(8,128)}, f32[16,128]{1,0:T(8,128)S(1)}, u32[]{:S(2)}, u32[]{:S(2)}) collective-permute-start(f32[16,128]{1,0:T(8,128)} %get-tuple-element.35), channel_id=1, source_target_pairs={{1,0},{2,1},{3,2},{4,3},{5,4},{6,5},{7,6},{8,7},{9,8},{10,9},{11,1... | collective-permute-start | bytes 24584 | tf_op jit(solution)/shard_map/ppermute | solution.py:700
  20.8 13.6 %collective-permute-start = (f32[200,128]{1,0:T(8,128)}, f32[200,128]{1,0:T(8,128)S(1)}, u32[]{:S(2)}, u32[]{:S(2)}) collective-permute-start(f32[200,128]{1,0:T(8,128)} %get-tuple-element.34.sent), channel_id=1, source_target_pairs={{32,0},{64,32},{96,64},{128,96},{160,128},{192,160},{224,192},{256... | collective-permute-start | bytes 307208 | tf_op jit(solution)/shard_map/ppermute | solution.py:690
  33.9 7.0 %copy-start.9 = (f32[16,128]{1,0:T(8,128)}, f32[16,128]{1,0:T(8,128)S(1)}, u32[]{:S(2)}) copy-start(f32[16,128]{1,0:T(8,128)S(1)} %collective-permute-done.2.above_edges) | copy-start | bytes 24580
  33.9 7.0 %copy-start.10 = (f32[16,128]{1,0:T(8,128)}, f32[16,128]{1,0:T(8,128)S(1)}, u32[]{:S(2)}) copy-start(f32[16,128]{1,0:T(8,128)S(1)} %collective-permute-done.1.edges) | copy-start | bytes 24580
  34.4 6.5 %copy-start = (f32[200,128]{1,0:T(8,128)}, f32[200,128]{1,0:T(8,128)S(1)}, u32[]{:S(2)}) copy-start(f32[200,128]{1,0:T(8,128)S(1)} %collective-permute-done.above) | copy-start | bytes 307204
  78.0 9.0 %collective-permute-start.3 = (f32[8,128]{1,0:T(8,128)}, f32[8,128]{1,0:T(8,128)S(1)}, u32[]{:S(2)}, u32[]{:S(2)}) collective-permute-start(f32[8,128]{1,0:T(8,128)} %get-tuple-element.39), channel_id=1, source_target_pairs={{0,31},{1,2},{2,1},{3,4},{4,3},{5,6},{6,5},{7,8},{8,7},{9,10},{10,... | collective-permute-start | bytes 12296 | tf_op jit(solution)/shard_map/ppermute | solution.py:711
  79.9 7.1 %collective-permute-start.4 = (f32[8,128]{1,0:T(8,128)}, f32[8,128]{1,0:T(8,128)S(1)}, u32[]{:S(2)}, u32[]{:S(2)}) collective-permute-start(f32[8,128]{1,0:T(8,128)} %get-tuple-element.40), channel_id=1, source_target_pairs={{0,1},{1,0},{2,3},{3,2},{4,5},{5,4},{6,7},{7,6},{8,9},{9,8},{10,11... | collective-permute-start | bytes 12296 | tf_op jit(solution)/shard_map/ppermute | solution.py:711
  87.8 18.0 %copy-start.1 = (f32[40,128]{1,0:T(8,128)}, f32[40,128]{1,0:T(8,128)S(1)}, u32[]{:S(2)}) copy-start(f32[40,128]{1,0:T(8,128)S(1)} %add_add_fusion.3.own_part) | copy-start | bytes 61444
  88.5 17.3 %copy-start.2 = (f32[40,128]{1,0:T(8,128)}, f32[40,128]{1,0:T(8,128)S(1)}, u32[]{:S(2)}) copy-start(f32[40,128]{1,0:T(8,128)S(1)} %add_add_fusion.2.above_part) | copy-start | bytes 61444
  88.5 9.8 %collective-permute-start.6 = (f32[40,128]{1,0:T(8,128)S(1)}, f32[40,128]{1,0:T(8,128)S(1)}, u32[]{:S(2)}, u32[]{:S(2)}) collective-permute-start(f32[40,128]{1,0:T(8,128)S(1)} %add_add_fusion.3.own_part), channel_id=1, source_target_pairs={{32,0},{64,32},{96,64},{128,96},{160,128},{192,160},{224,192},{256... | collective-permute-start | bytes 61448 | tf_op jit(solution)/shard_map/ppermute | solution.py:690
  95.3 10.5 %collective-permute-start.5 = (f32[40,128]{1,0:T(8,128)S(1)}, f32[40,128]{1,0:T(8,128)S(1)}, u32[]{:S(2)}, u32[]{:S(2)}) collective-permute-start(f32[40,128]{1,0:T(8,128)S(1)} %add_add_fusion.2.above_part), channel_id=1, source_target_pairs={{0,32},{32,64},{64,96},{96,128},{128,160},{160,192},{192,224},{224... | collective-permute-start | bytes 61448 | tf_op jit(solution)/shard_map/ppermute | solution.py:695
  98.3 7.5 %copy-start.5 = (f32[40,128]{1,0:T(8,128)}, f32[40,128]{1,0:T(8,128)S(1)}, u32[]{:S(2)}) copy-start(f32[40,128]{1,0:T(8,128)S(1)} %collective-permute-done.6.from_above) | copy-start | bytes 61444
  105.8 0.6 copy-start.6
  132.8 9.2 %collective-permute-start.7 = (f32[8,128]{1,0:T(8,128)}, f32[8,128]{1,0:T(8,128)S(1)}, u32[]{:S(2)}, u32[]{:S(2)}) collective-permute-start(f32[8,128]{1,0:T(8,128)} %get-tuple-element.47), channel_id=1, source_target_pairs={{0,31},{1,2},{2,1},{3,4},{4,3},{5,6},{6,5},{7,8},{8,7},{9,10},{10,... | collective-permute-start | bytes 12296 | tf_op jit(solution)/shard_map/ppermute | solution.py:711
  134.7 7.3 %collective-permute-start.8 = (f32[8,128]{1,0:T(8,128)}, f32[8,128]{1,0:T(8,128)S(1)}, u32[]{:S(2)}, u32[]{:S(2)}) collective-permute-start(f32[8,128]{1,0:T(8,128)} %get-tuple-element.48), channel_id=1, source_target_pairs={{0,1},{1,0},{2,3},{3,2},{4,5},{5,4},{6,7},{7,6},{8,9},{9,8},{10,11... | collective-permute-start | bytes 12296 | tf_op jit(solution)/shard_map/ppermute | solution.py:711
  142.8 13.2 %copy-start.3 = (f32[40,128]{1,0:T(8,128)}, f32[40,128]{1,0:T(8,128)S(1)}, u32[]{:S(2)}) copy-start(f32[40,128]{1,0:T(8,128)S(1)} %add_add_fusion.1.own_grad) | copy-start | bytes 61444
  143.5 12.4 %copy-start.4 = (f32[40,128]{1,0:T(8,128)}, f32[40,128]{1,0:T(8,128)S(1)}, u32[]{:S(2)}) copy-start(f32[40,128]{1,0:T(8,128)S(1)} %add_add_fusion.above_grad) | copy-start | bytes 61444
  143.5 9.8 %collective-permute-start.10 = (f32[40,128]{1,0:T(8,128)S(1)}, f32[40,128]{1,0:T(8,128)S(1)}, u32[]{:S(2)}, u32[]{:S(2)}) collective-permute-start(f32[40,128]{1,0:T(8,128)S(1)} %add_add_fusion.1.own_grad), channel_id=1, source_target_pairs={{32,0},{64,32},{96,64},{128,96},{160,128},{192,160},{224,192},{256... | collective-permute-start | bytes 61448 | tf_op jit(solution)/shard_map/ppermute | solution.py:690
  145.4 10.5 %collective-permute-start.9 = (f32[40,128]{1,0:T(8,128)S(1)}, f32[40,128]{1,0:T(8,128)S(1)}, u32[]{:S(2)}, u32[]{:S(2)}) collective-permute-start(f32[40,128]{1,0:T(8,128)S(1)} %add_add_fusion.above_grad), channel_id=1, source_target_pairs={{0,32},{32,64},{64,96},{96,128},{128,160},{160,192},{192,224},{224... | collective-permute-start | bytes 61448 | tf_op jit(solution)/shard_map/ppermute | solution.py:695
  153.3 2.6 %copy-start.7 = (f32[40,128]{1,0:T(8,128)}, f32[40,128]{1,0:T(8,128)S(1)}, u32[]{:S(2)}) copy-start(f32[40,128]{1,0:T(8,128)S(1)} %collective-permute-done.10.from_above) | copy-start | bytes 61444
  174.7 11.0 %collective-permute-start.11 = (f32[3,32,128]{2,1,0:T(8,128)}, f32[3,32,128]{2,1,0:T(8,128)S(1)}, u32[]{:S(2)}, u32[]{:S(2)}) collective-permute-start(f32[3,32,128]{2,1,0:T(8,128)} %get-tuple-element.57), channel_id=1, source_target_pairs={{0,32},{32,64},{64,96},{96,128},{128,160},{160,192},{192,224},{224... | collective-permute-start | bytes 147464 | tf_op jit(solution)/shard_map/ppermute | solution.py:695
  179.5 9.1 %collective-permute-start.12 = (f32[3,8,128]{2,1,0:T(8,128)}, f32[3,8,128]{2,1,0:T(8,128)S(1)}, u32[]{:S(2)}, u32[]{:S(2)}) collective-permute-start(f32[3,8,128]{2,1,0:T(8,128)} %get-tuple-element.58), channel_id=1, source_target_pairs={{0,1},{1,2},{2,3},{3,4},{4,5},{5,6},{6,7},{7,8},{8,9},{9,10},{10,1... | collective-permute-start | bytes 36872 | tf_op jit(solution)/shard_map/ppermute | solution.py:705
  181.4 9.9 %collective-permute-start.13 = (f32[3,8,128]{2,1,0:T(8,128)}, f32[3,8,128]{2,1,0:T(8,128)S(1)}, u32[]{:S(2)}, u32[]{:S(2)}) collective-permute-start(f32[3,8,128]{2,1,0:T(8,128)} %get-tuple-element.59), channel_id=1, source_target_pairs={{0,33},{1,34},{2,35},{3,36},{4,37},{5,38},{6,39},{7,40},{8,41},{9,... | collective-permute-start | bytes 36872 | tf_op jit(solution)/shard_map/ppermute | solution.py:747
  (1 other events, 0.6 us)

commit v7 on v6

--- a/solution.py
+++ b/solution.py
@@ -202,7 +202,7 @@
 
 
 def born_kernel(
-    total, items, reach, sent, edges, above, above_edges,
+    items, reach, sent, edges, above, above_edges,
     own_part, above_part, round_one, round_two, data, plain, d_self, d_pair,
     table, fresh_a, fresh_b, own, far, rings, sems,
 ):
@@ -211,7 +211,7 @@
     far[...] = jnp.zeros_like(far)
     data[...] = jnp.zeros_like(data)
     plain[...] = jnp.ones_like(plain)
-    fulls, parts = total[0], total[1]
+    fulls, parts = items[ITEMS - 2], items[ITEMS - 1]
 
     for index in range(6):
         origin = sent[index * TILES + TILES // 2 : index * TILES + TILES // 2 + 1, 0:1]
@@ -316,7 +316,7 @@
         lax.fori_loop(0, jnp.minimum(number, size), wait, 0)
 
     def listed_starts(item):
-        return part_starts(reach[item[0] * REGION + item[1]])
+        return part_starts(reach[item[0], item[1]])
 
     run(FULL_WIDTH, FULL_RING, full_ring, full_sems, 0, fulls, ATOMS, lambda item: range(0, ATOMS, CHUNK))
     run(PART_WIDTH, PART_RING, part_ring, part_sems, fulls, parts, PART, listed_starts)
@@ -340,13 +340,13 @@
 
 
 def energy_kernel(
-    total, items, reach, data, plain, own_part, above_part, from_below, from_above,
-    radii_born, slope, own_grad, above_grad, round_one, round_two, force,
-    table, fresh_a, fresh_b, own, far, born,
+    items, reach, data, plain, own_part, above_part, from_below, from_above,
+    radii_born, slope, own_grad, above_grad, round_one, round_two, force_out,
+    table, fresh_a, fresh_b, own, far, born, force,
 ):
     far[...] = jnp.zeros_like(far)
     force[...] = jnp.zeros_like(force)
-    fulls, parts = total[0], total[1]
+    fulls, parts = items[ITEMS - 2], items[ITEMS - 1]
     sums = jnp.concatenate([own_part[...] + from_below[...], above_part[...] + from_above[...]])
     all_radii, all_slopes = born_radius(sums, plain[0], plain[1])
     inverse = 1.0 / all_radii
@@ -408,7 +408,7 @@
     def part_step(index, carry):
         for k in range(PART_WIDTH):
             first, second = decode(items[fulls + index * PART_WIDTH + k])
-            starts = part_starts(reach[first * REGION + second])
+            starts = part_starts(reach[first, second])
             pair(first, second, starts, table, first, False)
         return carry
 
@@ -421,6 +421,8 @@
             force[tile, axis] += fold_own(own[tile, 1 + axis])
 
     fold_rows(fold, 4)
+    for axis in range(3):
+        force_out[axis] = jnp.sum(force[:, axis], axis=1)
     charge = plain[2] * inverse
     sums = jnp.sum(far[...], axis=1) * (0.5 * SCALE) * inverse + 0.5 * charge * charge
     own_grad[...] = sums[0:HALF]
@@ -429,13 +431,13 @@
 
 
 def force_kernel(
-    total, items, reach, data, slope, own_grad, above_grad, from_below, from_above, force_in, d_self, d_pair,
+    items, reach, data, slope, own_grad, above_grad, from_below, from_above, force_in, d_self, d_pair,
     gradient, own_force, above_force, to_next, to_across,
     table, own, far, chain, rings, sems,
 ):
     full_ring, part_ring, self_ring = rings
     full_sems, part_sems, self_sems = sems
-    fulls, parts = total[0], total[1]
+    fulls, parts = items[ITEMS - 2], items[ITEMS - 1]
     full_copy = ring_copies(full_ring, d_pair, full_sems, FULL_RING, ATOMS)
     part_copy = ring_copies(part_ring, d_pair, part_sems, PART_RING, PART)
 
@@ -452,7 +454,7 @@
     lax.fori_loop(0, jnp.minimum(fulls, FULL_RING), start(full_copy, 0), 0)
     lax.fori_loop(0, jnp.minimum(parts, PART_RING), start(part_copy, fulls), 0)
 
-    far[...] = force_in[...] * 4.0
+    far[...] = jnp.zeros_like(far)
     grads = jnp.concatenate([own_grad[...] + from_below[...], above_grad[...] + from_above[...]])
     gradient[...] = grads[0:TILES]
     chain[:, 0, :] = grads * slope[...]
@@ -537,7 +539,7 @@
         part_copy,
         fulls,
         parts,
-        lambda first, second: part_starts(reach[first * REGION + second]),
+        lambda first, second: part_starts(reach[first, second]),
     )
 
     def fold(tile):
@@ -546,7 +548,7 @@
 
     fold_rows(fold, 4)
     for axis in range(3):
-        sums = jnp.sum(far[:, axis], axis=1) * (-SCALE * SCALE / 16.0)
+        sums = (jnp.sum(far[:, axis], axis=1) + 4.0 * force_in[axis]) * (-SCALE * SCALE / 16.0)
         own_force[axis] = sums[0:TILES]
         above_force[axis] = sums[HALF : HALF + TILES]
         to_next[axis] = sums[TILES : TILES + 8]
@@ -588,7 +590,7 @@
     )(positions, charges, radii, scales, neighbours, pad_mask)
 
 
-def run_born(total, items, reach, sent, edges, above, above_edges):
+def run_born(items, reach, sent, edges, above, above_edges):
     return pl.pallas_call(
         born_kernel,
         name="born_sums",
@@ -602,7 +604,7 @@
             f32(TILES, *BLOCK),
             f32(PAIRS, 2, *BLOCK),
         ),
-        in_specs=[SMEM] * 3 + [VMEM] * 4,
+        in_specs=[SMEM] * 2 + [VMEM] * 4,
         out_specs=(VMEM,) * 6 + (ANY,) * 2,
         scratch_shapes=[
             pltpu.VMEM((OWN_ROWS, 5) + BLOCK, F32),
@@ -614,10 +616,10 @@
             RING_SEMS,
         ],
         compiler_params=PARAMS,
-    )(total, items, reach, sent, edges, above, above_edges)
-
-
-def run_energy(total, items, reach, data, plain, shares):
+    )(items, reach, sent, edges, above, above_edges)
+
+
+def run_energy(items, reach, data, plain, shares):
     return pl.pallas_call(
         energy_kernel,
         name="radius_gradient",
@@ -628,9 +630,9 @@
             f32(HALF, ATOMS),
             f32(*LANES),
             f32(*LANES),
-            f32(REGION, 3, *LANES),
+            f32(3, REGION, ATOMS),
         ),
-        in_specs=[SMEM] * 3 + [VMEM] * 6,
+        in_specs=[SMEM] * 2 + [VMEM] * 6,
         out_specs=(VMEM,) * 7,
         scratch_shapes=[
             pltpu.VMEM((OWN_ROWS, 6) + BLOCK, F32),
@@ -639,12 +641,13 @@
             pltpu.VMEM((OWN_ROWS, 4) + BLOCK, F32),
             pltpu.VMEM((REGION,) + LANES, F32),
             pltpu.VMEM((REGION,) + LANES, F32),
+            pltpu.VMEM((REGION, 3) + LANES, F32),
         ],
         compiler_params=PARAMS,
-    )(total, items, reach, data, plain, *shares)
-
-
-def run_force(total, items, reach, data, slope, shares, force_in, d_self, d_pair):
+    )(items, reach, data, plain, *shares)
+
+
+def run_force(items, reach, data, slope, shares, force_in, d_self, d_pair):
     return pl.pallas_call(
         force_kernel,
         name="forces",
@@ -655,7 +658,7 @@
             f32(3, *LANES),
             f32(3, *LANES),
         ),
-        in_specs=[SMEM] * 3 + [VMEM] * 7 + [ANY] * 2,
+        in_specs=[SMEM] * 2 + [VMEM] * 7 + [ANY] * 2,
         out_specs=(VMEM,) * 5,
         scratch_shapes=[
             pltpu.VMEM((OWN_ROWS, 4) + BLOCK, F32),
@@ -666,7 +669,7 @@
             RING_SEMS,
         ],
         compiler_params=PARAMS,
-    )(total, items, reach, data, slope, *shares, force_in, d_self, d_pair)
+    )(items, reach, data, slope, *shares, force_in, d_self, d_pair)
 
 
 def born_radius(descreen_sum, radius, radius_in):
@@ -789,7 +792,7 @@
     *_, above_low, above_high = slab_boxes(above, above_edges, across, along)
     own_codes = chunk_codes(low, high, *tile)
     code = jnp.concatenate([own_codes, chunk_codes(low, high, above_low, above_high)], axis=1)
-    return code.reshape(-1), (code >> (3 * CHUNKS)) <= CHUNKS // 2
+    return code, (code >> (3 * CHUNKS)) <= CHUNKS // 2
 
 
 def packed(first, second, valid, is_part):
@@ -808,7 +811,9 @@
     chosen = valid[None, :] & (rank[None, :] == jnp.arange(ITEMS)[:, None])
     value = first * ATOMS + second - DUMMY
     items = DUMMY + jnp.sum(jnp.where(chosen, value[None, :], 0), axis=1)
-    return jnp.stack([fulls, parts]), items.astype(jnp.int32)
+    slot = jnp.arange(ITEMS)
+    items = jnp.where(slot == ITEMS - 2, fulls, jnp.where(slot == ITEMS - 1, parts, items))
+    return items.astype(jnp.int32)
 
 
 def pair_items(here, above, is_part):
@@ -836,14 +841,14 @@
     next_edges = next_to_here(edges)
     above_edges = across_to_here(edges)
     reach, is_part = chunk_reach(sent, next_edges, above, above_edges)
-    total, items = pair_items(here, above, is_part)
-
-    *parts, data, plain, d_self, d_pair = run_born(total, items, reach, sent, next_edges, above, above_edges)
+    items = pair_items(here, above, is_part)
+
+    *parts, data, plain, d_self, d_pair = run_born(items, reach, sent, next_edges, above, above_edges)
     shares = swap_sums(*parts)
-    radii_born, slope, *parts, force = run_energy(total, items, reach, data, plain, shares)
+    radii_born, slope, *parts, force = run_energy(items, reach, data, plain, shares)
     shares = swap_sums(*parts)
     gradient, own, over, to_next, to_across = run_force(
-        total, items, reach, data, slope, shares, force, d_self, d_pair
+        items, reach, data, slope, shares, force, d_self, d_pair
     )
     forces, to_next, to_across = lax.optimization_barrier(
         (own + here_to_above(over), here_to_next(to_next), here_to_across(to_across))

time: 193 us -> 190 us (0.984)
  the two profiles are of different devices: /device:TPU:24 before, /device:TPU:48 now
where the time goes in v7:
time: 190 us; the launch traced here: 193 us
  Pallas kernels  83.6 us (44%)
  starting transfers between devices  59.9 us (32%)
  waiting for transfers between devices  29.8 us (16%)
  other arithmetic  8.61 us (5%)
  between operations  6.36 us (3%)
  local copies, waits for them, and re-layouts  4.63 us (2%)
    pallas_call x1, Pallas kernels, run_born(): pl.pallas_call(born_kernel, name='born_sums', out_shape=(f32(HALF, ATOMS)...  37.6 us
    pallas_call x1, Pallas kernels, run_energy(): pl.pallas_call(energy_kernel, name='radius_gradient', out_shape=(f32(TILE...  26.5 us
    ppermute x3, starting transfers between devices, here_to_above(): return lax.ppermute(block, 'slab', [(i, i + 1) for i in range(ends)])  18.3 us
    pallas_call x1, Pallas kernels, run_force(): pl.pallas_call(force_kernel, name='forces', out_shape=(f32(TILES, ATOMS),...  18 us
    ppermute x1, starting transfers between devices, across_to_here(): return lax.ppermute(block, ('slab', 'tile'), pairs)  13.8 us
    ppermute x3, starting transfers between devices, above_to_here(): return lax.ppermute(block, 'slab', [(i + 1, i) for i in range(ends)])  13.6 us
    ppermute x3, waiting for transfers between devices, here_to_above(): return lax.ppermute(block, 'slab', [(i, i + 1) for i in range(ends)])  9.78 us
    ppermute x4, starting transfers between devices, pairwise(): return lax.ppermute(block, 'tile', pairs)  7.67 us
  transfers between devices with their start and end apart: 14, of which 8 were waited for; matrix products, arithmetic and copies ran while one was open for 3% of the time, Pallas kernels for 0%

profile of v7, /device:TPU:48, one launch (start us, length us, event | category | flops | bytes accessed | tf_op | source)
XLA Modules:
  0.0 193.3 jit_solution(5013530166604987919)
XLA Ops:
  2.1 13.8 %collective-permute-start.2 = (f32[16,128]{1,0:T(8,128)}, f32[16,128]{1,0:T(8,128)S(1)}, u32[]{:S(2)}, u32[]{:S(2)}) collective-permute-start(f32[16,128]{1,0:T(8,128)} %get-tuple-element.35), channel_id=1, source_target_pairs={{33,0},{34,1},{35,2},{36,3},{37,4},{38,5},{39,6},{40,7},{41,8},{42... | collective-permute-start | bytes 24584 | tf_op jit(solution)/shard_map/ppermute | solution.py:724
  15.9 2.8 %collective-permute-start.1 = (f32[16,128]{1,0:T(8,128)}, f32[16,128]{1,0:T(8,128)S(1)}, u32[]{:S(2)}, u32[]{:S(2)}) collective-permute-start(f32[16,128]{1,0:T(8,128)} %get-tuple-element.35), channel_id=1, source_target_pairs={{1,0},{2,1},{3,2},{4,3},{5,4},{6,5},{7,6},{8,7},{9,8},{10,9},{11,1... | collective-permute-start | bytes 24584 | tf_op jit(solution)/shard_map/ppermute | solution.py:703
  18.7 5.5 %collective-permute-start = (f32[200,128]{1,0:T(8,128)}, f32[200,128]{1,0:T(8,128)S(1)}, u32[]{:S(2)}, u32[]{:S(2)}) collective-permute-start(f32[200,128]{1,0:T(8,128)} %get-tuple-element.34.sent), channel_id=1, source_target_pairs={{32,0},{64,32},{96,64},{128,96},{160,128},{192,160},{224,192},{256... | collective-permute-start | bytes 307208 | tf_op jit(solution)/shard_map/ppermute | solution.py:693
  32.3 3.2 %collective-permute-done.above = f32[200,128]{1,0:T(8,128)S(1)} collective-permute-done((f32[200,128]{1,0:T(8,128)}, f32[200,128]{1,0:T(8,128)S(1)}, u32[]{:S(2)}, u32[]{:S(2)}) %collective-permute-start) | collective-permute-done | bytes 102432 | tf_op jit(solution)/shard_map/ppermute | solution.py:693
  40.8 37.6 %born_sums.1 = (f32[40,128]{1,0:T(8,128)}, f32[40,128]{1,0:T(8,128)}, f32[8,128]{1,0:T(8,128)}, f32[8,128]{1,0:T(8,128)}, f32[80,8,128]{2,1,0:T(8,128)}, /*index...) custom-call(s32[512]{0:T(512)} %select_select_fusion.items, s32[35,80]{1,0:T(8,128)} %copy-done, ...), custom_call_target="tpu_custom_call" | custom-call | tf_op jit(solution)/shard_map/born_sums/pallas_call | solution.py:594
  78.4 1.9 collective-permute-start.3
  80.3 1.9 collective-permute-start.4
  82.2 3.4 %collective-permute-done.3 = f32[8,128]{1,0:T(8,128)S(1)} collective-permute-done((f32[8,128]{1,0:T(8,128)}, f32[8,128]{1,0:T(8,128)S(1)}, u32[]{:S(2)}, u32[]{:S(2)}) %collective-permute-start.3) | collective-permute-done | bytes 4128 | tf_op jit(solution)/shard_map/ppermute | solution.py:714
  87.1 6.2 %collective-permute-start.6 = (f32[40,128]{1,0:T(8,128)S(1)}, f32[40,128]{1,0:T(8,128)S(1)}, u32[]{:S(2)}, u32[]{:S(2)}) collective-permute-start(f32[40,128]{1,0:T(8,128)S(1)} %add_add_fusion.3.own_part), channel_id=1, source_target_pairs={{32,0},{64,32},{96,64},{128,96},{160,128},{192,160},{224,192},{256... | collective-permute-start | bytes 61448 | tf_op jit(solution)/shard_map/ppermute | solution.py:693
  93.4 3.5 %collective-permute-start.5 = (f32[40,128]{1,0:T(8,128)S(1)}, f32[40,128]{1,0:T(8,128)S(1)}, u32[]{:S(2)}, u32[]{:S(2)}) collective-permute-start(f32[40,128]{1,0:T(8,128)S(1)} %add_add_fusion.2.above_part), channel_id=1, source_target_pairs={{0,32},{32,64},{64,96},{96,128},{128,160},{160,192},{192,224},{224... | collective-permute-start | bytes 61448 | tf_op jit(solution)/shard_map/ppermute | solution.py:698
  96.9 7.0 %collective-permute-done.5.from_below = f32[40,128]{1,0:T(8,128)S(1)} collective-permute-done((f32[40,128]{1,0:T(8,128)S(1)}, f32[40,128]{1,0:T(8,128)S(1)}, u32[]{:S(2)}, u32[]{:S(2)}) %collective-permute-start.5) | collective-permute-done | bytes 20512 | tf_op jit(solution)/shard_map/ppermute | solution.py:698
  104.4 26.5 %radius_gradient.1 = (f32[32,128]{1,0:T(8,128)}, f32[80,128]{1,0:T(8,128)}, f32[40,128]{1,0:T(8,128)}, f32[40,128]{1,0:T(8,128)}, f32[8,128]{1,0:T(8,128)}, /*index=5*/f32[8,128]{1,0:T(8,128)}, f32[3,80,128]{2,1,0:T(8,128)}) custom-call(s32[512]{0:T(512)} %select_select_fusion.items, s32[35,80]{1,0:T(8,128)} %copy-done, ...), custom_call_target="tpu_custom_call" | custom-call | tf_op jit(solution)/shard_map/radius_gradient/pallas_call | solution.py:623
  131.0 1.9 collective-permute-start.7
  132.9 1.9 collective-permute-start.8
  134.8 3.4 %collective-permute-done.7 = f32[8,128]{1,0:T(8,128)S(1)} collective-permute-done((f32[8,128]{1,0:T(8,128)}, f32[8,128]{1,0:T(8,128)S(1)}, u32[]{:S(2)}, u32[]{:S(2)}) %collective-permute-start.7) | collective-permute-done | bytes 4128 | tf_op jit(solution)/shard_map/ppermute | solution.py:714
  139.7 1.9 collective-permute-start.10
  141.6 7.8 %collective-permute-start.9 = (f32[40,128]{1,0:T(8,128)S(1)}, f32[40,128]{1,0:T(8,128)S(1)}, u32[]{:S(2)}, u32[]{:S(2)}) collective-permute-start(f32[40,128]{1,0:T(8,128)S(1)} %add_add_fusion.above_grad), channel_id=1, source_target_pairs={{0,32},{32,64},{64,96},{96,128},{128,160},{160,192},{192,224},{224... | collective-permute-start | bytes 61448 | tf_op jit(solution)/shard_map/ppermute | solution.py:698
  149.5 2.6 %collective-permute-done.9.from_below = f32[40,128]{1,0:T(8,128)S(1)} collective-permute-done((f32[40,128]{1,0:T(8,128)S(1)}, f32[40,128]{1,0:T(8,128)S(1)}, u32[]{:S(2)}, u32[]{:S(2)}) %collective-permute-start.9) | collective-permute-done | bytes 20512 | tf_op jit(solution)/shard_map/ppermute | solution.py:698
  152.7 18.0 %forces.1 = (f32[32,128]{1,0:T(8,128)}, f32[3,32,128]{2,1,0:T(8,128)}, f32[3,32,128]{2,1,0:T(8,128)}, f32[3,8,128]{2,1,0:T(8,128)}, f32[3,8,128]{2,1,0:T(8,128)}) custom-call(s32[512]{0:T(512)} %select_select_fusion.items, s32[35,80]{1,0:T(8,128)} %copy-done, f32[80,8,128]{2,1,0:T(8,128)} %get-tuple-element.36.data, f32[80,128]{1,0:T(8,128)} %get-tuple-element.45.slope, ...), custom_call_target="tpu_custom_call" | custom-call | tf_op jit(solution)/shard_map/forces/pallas_call | solution.py:651
  170.7 6.9 %collective-permute-start.11 = (f32[3,32,128]{2,1,0:T(8,128)}, f32[3,32,128]{2,1,0:T(8,128)S(1)}, u32[]{:S(2)}, u32[]{:S(2)}) collective-permute-start(f32[3,32,128]{2,1,0:T(8,128)} %get-tuple-element.57), channel_id=1, source_target_pairs={{0,32},{32,64},{64,96},{96,128},{128,160},{160,192},{192,224},{224... | collective-permute-start | bytes 147464 | tf_op jit(solution)/shard_map/ppermute | solution.py:698
  177.7 1.9 collective-permute-start.12
  179.6 1.9 collective-permute-start.13
  182.6 2.5 %collective-permute-done.12 = f32[3,8,128]{2,1,0:T(8,128)S(1)} collective-permute-done((f32[3,8,128]{2,1,0:T(8,128)}, f32[3,8,128]{2,1,0:T(8,128)S(1)}, u32[]{:S(2)}, u32[]{:S(2)}) %collective-permute-start.12) | collective-permute-done | bytes 12320 | tf_op jit(solution)/shard_map/ppermute | solution.py:708
  185.0 7.6 %collective-permute-done.13 = f32[3,8,128]{2,1,0:T(8,128)S(1)} collective-permute-done((f32[3,8,128]{2,1,0:T(8,128)}, f32[3,8,128]{2,1,0:T(8,128)S(1)}, u32[]{:S(2)}, u32[]{:S(2)}) %collective-permute-start.13) | collective-permute-done | bytes 12320 | tf_op jit(solution)/shard_map/ppermute | solution.py:750
  (107 shorter events, 15.3 us)
Async XLA Ops:
  2.1 29.7 %collective-permute-start.2 = (f32[16,128]{1,0:T(8,128)}, f32[16,128]{1,0:T(8,128)S(1)}, u32[]{:S(2)}, u32[]{:S(2)}) collective-permute-start(f32[16,128]{1,0:T(8,128)} %get-tuple-element.35), channel_id=1, source_target_pairs={{33,0},{34,1},{35,2},{36,3},{37,4},{38,5},{39,6},{40,7},{41,8},{42... | collective-permute-start | bytes 24584 | tf_op jit(solution)/shard_map/ppermute | solution.py:724
  15.9 15.9 %collective-permute-start.1 = (f32[16,128]{1,0:T(8,128)}, f32[16,128]{1,0:T(8,128)S(1)}, u32[]{:S(2)}, u32[]{:S(2)}) collective-permute-start(f32[16,128]{1,0:T(8,128)} %get-tuple-element.35), channel_id=1, source_target_pairs={{1,0},{2,1},{3,2},{4,3},{5,4},{6,5},{7,6},{8,7},{9,8},{10,9},{11,1... | collective-permute-start | bytes 24584 | tf_op jit(solution)/shard_map/ppermute | solution.py:703
  18.7 16.8 %collective-permute-start = (f32[200,128]{1,0:T(8,128)}, f32[200,128]{1,0:T(8,128)S(1)}, u32[]{:S(2)}, u32[]{:S(2)}) collective-permute-start(f32[200,128]{1,0:T(8,128)} %get-tuple-element.34.sent), channel_id=1, source_target_pairs={{32,0},{64,32},{96,64},{128,96},{160,128},{192,160},{224,192},{256... | collective-permute-start | bytes 307208 | tf_op jit(solution)/shard_map/ppermute | solution.py:693
  31.8 9.0 %copy-start.10 = (f32[16,128]{1,0:T(8,128)}, f32[16,128]{1,0:T(8,128)S(1)}, u32[]{:S(2)}) copy-start(f32[16,128]{1,0:T(8,128)S(1)} %collective-permute-done.2.above_edges) | copy-start | bytes 24580
  31.8 9.0 %copy-start.11 = (f32[16,128]{1,0:T(8,128)}, f32[16,128]{1,0:T(8,128)S(1)}, u32[]{:S(2)}) copy-start(f32[16,128]{1,0:T(8,128)S(1)} %collective-permute-done.1.edges) | copy-start | bytes 24580
  35.5 5.3 %copy-start.1 = (f32[200,128]{1,0:T(8,128)}, f32[200,128]{1,0:T(8,128)S(1)}, u32[]{:S(2)}) copy-start(f32[200,128]{1,0:T(8,128)S(1)} %collective-permute-done.above) | copy-start | bytes 307204
  37.4 3.4 %copy-start = (s32[35,80]{1,0:T(8,128)}, s32[35,80]{1,0:T(8,128)S(1)}, u32[]{:S(2)}) copy-start(s32[35,80]{1,0:T(8,128)S(1)} %pad_add_fusion.reach) | copy-start | bytes 33604
  78.4 7.2 %collective-permute-start.3 = (f32[8,128]{1,0:T(8,128)}, f32[8,128]{1,0:T(8,128)S(1)}, u32[]{:S(2)}, u32[]{:S(2)}) collective-permute-start(f32[8,128]{1,0:T(8,128)} %get-tuple-element.39), channel_id=1, source_target_pairs={{0,31},{1,2},{2,1},{3,4},{4,3},{5,6},{6,5},{7,8},{8,7},{9,10},{10,... | collective-permute-start | bytes 12296 | tf_op jit(solution)/shard_map/ppermute | solution.py:714
  80.3 5.3 %collective-permute-start.4 = (f32[8,128]{1,0:T(8,128)}, f32[8,128]{1,0:T(8,128)S(1)}, u32[]{:S(2)}, u32[]{:S(2)}) collective-permute-start(f32[8,128]{1,0:T(8,128)} %get-tuple-element.40), channel_id=1, source_target_pairs={{0,1},{1,0},{2,3},{3,2},{4,5},{5,4},{6,7},{7,6},{8,9},{9,8},{10,11... | collective-permute-start | bytes 12296 | tf_op jit(solution)/shard_map/ppermute | solution.py:714
  86.4 17.5 %copy-start.2 = (f32[40,128]{1,0:T(8,128)}, f32[40,128]{1,0:T(8,128)S(1)}, u32[]{:S(2)}) copy-start(f32[40,128]{1,0:T(8,128)S(1)} %add_add_fusion.3.own_part) | copy-start | bytes 61444
  87.1 16.7 %copy-start.3 = (f32[40,128]{1,0:T(8,128)}, f32[40,128]{1,0:T(8,128)S(1)}, u32[]{:S(2)}) copy-start(f32[40,128]{1,0:T(8,128)S(1)} %add_add_fusion.2.above_part) | copy-start | bytes 61444
  87.1 9.8 %collective-permute-start.6 = (f32[40,128]{1,0:T(8,128)S(1)}, f32[40,128]{1,0:T(8,128)S(1)}, u32[]{:S(2)}, u32[]{:S(2)}) collective-permute-start(f32[40,128]{1,0:T(8,128)S(1)} %add_add_fusion.3.own_part), channel_id=1, source_target_pairs={{32,0},{64,32},{96,64},{128,96},{160,128},{192,160},{224,192},{256... | collective-permute-start | bytes 61448 | tf_op jit(solution)/shard_map/ppermute | solution.py:693
  93.4 10.5 %collective-permute-start.5 = (f32[40,128]{1,0:T(8,128)S(1)}, f32[40,128]{1,0:T(8,128)S(1)}, u32[]{:S(2)}, u32[]{:S(2)}) collective-permute-start(f32[40,128]{1,0:T(8,128)S(1)} %add_add_fusion.2.above_part), channel_id=1, source_target_pairs={{0,32},{32,64},{64,96},{96,128},{128,160},{160,192},{192,224},{224... | collective-permute-start | bytes 61448 | tf_op jit(solution)/shard_map/ppermute | solution.py:698
  96.9 7.0 %copy-start.6 = (f32[40,128]{1,0:T(8,128)}, f32[40,128]{1,0:T(8,128)S(1)}, u32[]{:S(2)}) copy-start(f32[40,128]{1,0:T(8,128)S(1)} %collective-permute-done.6.from_above) | copy-start | bytes 61444
  131.0 7.2 %collective-permute-start.7 = (f32[8,128]{1,0:T(8,128)}, f32[8,128]{1,0:T(8,128)S(1)}, u32[]{:S(2)}, u32[]{:S(2)}) collective-permute-start(f32[8,128]{1,0:T(8,128)} %get-tuple-element.47), channel_id=1, source_target_pairs={{0,31},{1,2},{2,1},{3,4},{4,3},{5,6},{6,5},{7,8},{8,7},{9,10},{10,... | collective-permute-start | bytes 12296 | tf_op jit(solution)/shard_map/ppermute | solution.py:714
  132.9 5.3 %collective-permute-start.8 = (f32[8,128]{1,0:T(8,128)}, f32[8,128]{1,0:T(8,128)S(1)}, u32[]{:S(2)}, u32[]{:S(2)}) collective-permute-start(f32[8,128]{1,0:T(8,128)} %get-tuple-element.48), channel_id=1, source_target_pairs={{0,1},{1,0},{2,3},{3,2},{4,5},{5,4},{6,7},{7,6},{8,9},{9,8},{10,11... | collective-permute-start | bytes 12296 | tf_op jit(solution)/shard_map/ppermute | solution.py:714
  139.0 13.2 %copy-start.4 = (f32[40,128]{1,0:T(8,128)}, f32[40,128]{1,0:T(8,128)S(1)}, u32[]{:S(2)}) copy-start(f32[40,128]{1,0:T(8,128)S(1)} %add_add_fusion.1.own_grad) | copy-start | bytes 61444
  139.7 12.4 %copy-start.5 = (f32[40,128]{1,0:T(8,128)}, f32[40,128]{1,0:T(8,128)S(1)}, u32[]{:S(2)}) copy-start(f32[40,128]{1,0:T(8,128)S(1)} %add_add_fusion.above_grad) | copy-start | bytes 61444
  139.7 9.8 %collective-permute-start.10 = (f32[40,128]{1,0:T(8,128)S(1)}, f32[40,128]{1,0:T(8,128)S(1)}, u32[]{:S(2)}, u32[]{:S(2)}) collective-permute-start(f32[40,128]{1,0:T(8,128)S(1)} %add_add_fusion.1.own_grad), channel_id=1, source_target_pairs={{32,0},{64,32},{96,64},{128,96},{160,128},{192,160},{224,192},{256... | collective-permute-start | bytes 61448 | tf_op jit(solution)/shard_map/ppermute | solution.py:693
  141.6 10.5 %collective-permute-start.9 = (f32[40,128]{1,0:T(8,128)S(1)}, f32[40,128]{1,0:T(8,128)S(1)}, u32[]{:S(2)}, u32[]{:S(2)}) collective-permute-start(f32[40,128]{1,0:T(8,128)S(1)} %add_add_fusion.above_grad), channel_id=1, source_target_pairs={{0,32},{32,64},{64,96},{96,128},{128,160},{160,192},{192,224},{224... | collective-permute-start | bytes 61448 | tf_op jit(solution)/shard_map/ppermute | solution.py:698
  149.5 2.6 %copy-start.8 = (f32[40,128]{1,0:T(8,128)}, f32[40,128]{1,0:T(8,128)S(1)}, u32[]{:S(2)}) copy-start(f32[40,128]{1,0:T(8,128)S(1)} %collective-permute-done.10.from_above) | copy-start | bytes 61444
  170.7 11.0 %collective-permute-start.11 = (f32[3,32,128]{2,1,0:T(8,128)}, f32[3,32,128]{2,1,0:T(8,128)S(1)}, u32[]{:S(2)}, u32[]{:S(2)}) collective-permute-start(f32[3,32,128]{2,1,0:T(8,128)} %get-tuple-element.57), channel_id=1, source_target_pairs={{0,32},{32,64},{64,96},{96,128},{128,160},{160,192},{192,224},{224... | collective-permute-start | bytes 147464 | tf_op jit(solution)/shard_map/ppermute | solution.py:698
  177.7 7.3 %collective-permute-start.12 = (f32[3,8,128]{2,1,0:T(8,128)}, f32[3,8,128]{2,1,0:T(8,128)S(1)}, u32[]{:S(2)}, u32[]{:S(2)}) collective-permute-start(f32[3,8,128]{2,1,0:T(8,128)} %get-tuple-element.58), channel_id=1, source_target_pairs={{0,1},{1,2},{2,3},{3,4},{4,5},{5,6},{6,7},{7,8},{8,9},{9,10},{10,1... | collective-permute-start | bytes 36872 | tf_op jit(solution)/shard_map/ppermute | solution.py:708
  179.6 13.0 %collective-permute-start.13 = (f32[3,8,128]{2,1,0:T(8,128)}, f32[3,8,128]{2,1,0:T(8,128)S(1)}, u32[]{:S(2)}, u32[]{:S(2)}) collective-permute-start(f32[3,8,128]{2,1,0:T(8,128)} %get-tuple-element.59), channel_id=1, source_target_pairs={{0,33},{1,34},{2,35},{3,36},{4,37},{5,38},{6,39},{7,40},{8,41},{9,... | collective-permute-start | bytes 36872 | tf_op jit(solution)/shard_map/ppermute | solution.py:750
  (2 other events, 1.2 us)

commit v8 on v7

--- a/solution.py
+++ b/solution.py
@@ -590,6 +590,28 @@
     )(positions, charges, radii, scales, neighbours, pad_mask)
 
 
+def merge_kernel(own, above, one, two, own_out, above_out):
+    is_even = lax.rem(lax.axis_index("tile"), 2) == 0
+    from_next = jnp.where(is_even, one[...], two[...])
+    from_last = jnp.where(is_even, two[...], one[...])
+    for place, (source, target) in enumerate(((own, own_out), (above, above_out))):
+        rows = slice(place * EDGE, (place + 1) * EDGE)
+        target[...] = source[...]
+        target[0:EDGE, :] = source[0:EDGE, :] + from_last[rows]
+        target[TILES:LIVE, :] = source[TILES:LIVE, :] + from_next[rows]
+
+
+def run_merge(own, above, one, two):
+    return pl.pallas_call(
+        merge_kernel,
+        name="merge_edges",
+        out_shape=(f32(HALF, ATOMS),) * 2,
+        in_specs=[VMEM] * 4,
+        out_specs=(VMEM,) * 2,
+        compiler_params=PARAMS,
+    )(own, above, one, two)
+
+
 def run_born(items, reach, sent, edges, above, above_edges):
     return pl.pallas_call(
         born_kernel,
@@ -724,19 +746,8 @@
     return lax.ppermute(block, ("slab", "tile"), pairs)
 
 
-def placed(block, first, last):
-    return jnp.pad(block[first : first + EDGE], ((0, HALF - EDGE), (0, 0))) + jnp.pad(
-        last[first : first + EDGE], ((TILES, HALF - LIVE), (0, 0))
-    )
-
-
 def swap_sums(own, above, round_one, round_two):
-    one, two = pairwise(round_one, False), pairwise(round_two, True)
-    is_even = lax.axis_index("tile") % 2 == 0
-    from_next, from_last = jnp.where(is_even, one, two), jnp.where(is_even, two, one)
-    own = own + placed(from_last, 0, from_next)
-    above = above + placed(from_last, EDGE, from_next)
-    own, above = lax.optimization_barrier((own, above))
+    own, above = run_merge(own, above, pairwise(round_one, False), pairwise(round_two, True))
     return own, above, here_to_above(above), above_to_here(own)
 
 

time: 190 us -> 193 us (1.016)
  the two profiles are of different devices: /device:TPU:48 before, /device:TPU:24 now
where the time goes in v8:
time: 193 us; the launch traced here: 192 us
  Pallas kernels  86.4 us (45%)
  starting transfers between devices  60.5 us (31%)
  waiting for transfers between devices  26.8 us (14%)
  between operations  6.34 us (3%)
  local copies, waits for them, and re-layouts  5.81 us (3%)
  other arithmetic  5.65 us (3%)
    pallas_call x1, Pallas kernels, run_born(): pl.pallas_call(born_kernel, name='born_sums', out_shape=(f32(HALF, ATOMS)...  37.6 us
    pallas_call x1, Pallas kernels, run_energy(): pl.pallas_call(energy_kernel, name='radius_gradient', out_shape=(f32(TILE...  26.5 us
    ppermute x3, starting transfers between devices, here_to_above(): return lax.ppermute(block, 'slab', [(i, i + 1) for i in range(ends)])  21.1 us
    pallas_call x1, Pallas kernels, run_force(): pl.pallas_call(force_kernel, name='forces', out_shape=(f32(TILES, ATOMS),...  18 us
    ppermute x4, waiting for transfers between devices, pairwise(): return lax.ppermute(block, 'tile', pairs)  14.3 us
    ppermute x1, starting transfers between devices, across_to_here(): return lax.ppermute(block, ('slab', 'tile'), pairs)  13.2 us
    ppermute x3, starting transfers between devices, above_to_here(): return lax.ppermute(block, 'slab', [(i + 1, i) for i in range(ends)])  9.27 us
    ppermute x4, starting transfers between devices, pairwise(): return lax.ppermute(block, 'tile', pairs)  7.67 us
  transfers between devices with their start and end apart: 14, of which 7 were waited for; matrix products, arithmetic and copies ran while one was open for 3% of the time, Pallas kernels for 0%

profile of v8, /device:TPU:24, one launch (start us, length us, event | category | flops | bytes accessed | tf_op | source)
XLA Modules:
  0.0 191.9 jit_solution(14229552294254087180)
XLA Ops:
  2.1 13.2 %collective-permute-start.2 = (f32[16,128]{1,0:T(8,128)}, f32[16,128]{1,0:T(8,128)S(1)}, u32[]{:S(2)}, u32[]{:S(2)}) collective-permute-start(f32[16,128]{1,0:T(8,128)} %get-tuple-element.35), channel_id=1, source_target_pairs={{33,0},{34,1},{35,2},{36,3},{37,4},{38,5},{39,6},{40,7},{41,8},{42... | collective-permute-start | bytes 24584 | tf_op jit(solution)/shard_map/ppermute | solution.py:746
  15.4 5.4 %collective-permute-start.1 = (f32[16,128]{1,0:T(8,128)}, f32[16,128]{1,0:T(8,128)S(1)}, u32[]{:S(2)}, u32[]{:S(2)}) collective-permute-start(f32[16,128]{1,0:T(8,128)} %get-tuple-element.35), channel_id=1, source_target_pairs={{1,0},{2,1},{3,2},{4,3},{5,4},{6,5},{7,6},{8,7},{9,8},{10,9},{11,1... | collective-permute-start | bytes 24584 | tf_op jit(solution)/shard_map/ppermute | solution.py:725
  20.8 5.5 %collective-permute-start = (f32[200,128]{1,0:T(8,128)}, f32[200,128]{1,0:T(8,128)S(1)}, u32[]{:S(2)}, u32[]{:S(2)}) collective-permute-start(f32[200,128]{1,0:T(8,128)} %get-tuple-element.34.sent), channel_id=1, source_target_pairs={{32,0},{64,32},{96,64},{128,96},{160,128},{192,160},{224,192},{256... | collective-permute-start | bytes 307208 | tf_op jit(solution)/shard_map/ppermute | solution.py:715
  39.8 37.6 %born_sums.1 = (f32[40,128]{1,0:T(8,128)}, f32[40,128]{1,0:T(8,128)}, f32[8,128]{1,0:T(8,128)}, f32[8,128]{1,0:T(8,128)}, f32[80,8,128]{2,1,0:T(8,128)}, /*index...) custom-call(s32[512]{0:T(512)} %select_select_fusion.items, s32[35,80]{1,0:T(8,128)} %copy-done, ...), custom_call_target="tpu_custom_call" | custom-call | tf_op jit(solution)/shard_map/born_sums/pallas_call | solution.py:616
  77.3 1.9 %collective-permute-start.3 = (f32[8,128]{1,0:T(8,128)}, f32[8,128]{1,0:T(8,128)S(1)}, u32[]{:S(2)}, u32[]{:S(2)}) collective-permute-start(f32[8,128]{1,0:T(8,128)} %get-tuple-element.40), channel_id=1, source_target_pairs={{0,1},{1,0},{2,3},{3,2},{4,5},{5,4},{6,7},{7,6},{8,9},{9,8},{10,11... | collective-permute-start | bytes 12296 | tf_op jit(solution)/shard_map/ppermute | solution.py:736
  79.2 1.9 %collective-permute-start.4 = (f32[8,128]{1,0:T(8,128)}, f32[8,128]{1,0:T(8,128)S(1)}, u32[]{:S(2)}, u32[]{:S(2)}) collective-permute-start(f32[8,128]{1,0:T(8,128)} %get-tuple-element.41), channel_id=1, source_target_pairs={{0,31},{1,2},{2,1},{3,4},{4,3},{5,6},{6,5},{7,8},{8,7},{9,10},{10,... | collective-permute-start | bytes 12296 | tf_op jit(solution)/shard_map/ppermute | solution.py:736
  81.2 7.2 %collective-permute-done.4.two = f32[8,128]{1,0:T(8,128)S(1)} collective-permute-done((f32[8,128]{1,0:T(8,128)}, f32[8,128]{1,0:T(8,128)S(1)}, u32[]{:S(2)}, u32[]{:S(2)}) %collective-permute-start.4) | collective-permute-done | bytes 4128 | tf_op jit(solution)/shard_map/ppermute | solution.py:736
  90.4 1.9 collective-permute-start.6
  92.3 7.8 %collective-permute-start.5 = (f32[40,128]{1,0:T(8,128)}, f32[40,128]{1,0:T(8,128)S(1)}, u32[]{:S(2)}, u32[]{:S(2)}) collective-permute-start(f32[40,128]{1,0:T(8,128)} %get-tuple-element.43.above_part), channel_id=1, source_target_pairs={{0,32},{32,64},{64,96},{96,128},{128,160},{160,192},{192,224},{224... | collective-permute-start | bytes 61448 | tf_op jit(solution)/shard_map/ppermute | solution.py:720
  100.2 2.8 %collective-permute-done.5.from_below = f32[40,128]{1,0:T(8,128)S(1)} collective-permute-done((f32[40,128]{1,0:T(8,128)}, f32[40,128]{1,0:T(8,128)S(1)}, u32[]{:S(2)}, u32[]{:S(2)}) %collective-permute-start.5) | collective-permute-done | bytes 20512 | tf_op jit(solution)/shard_map/ppermute | solution.py:720
  103.6 26.5 %radius_gradient.1 = (f32[32,128]{1,0:T(8,128)}, f32[80,128]{1,0:T(8,128)}, f32[40,128]{1,0:T(8,128)}, f32[40,128]{1,0:T(8,128)}, f32[8,128]{1,0:T(8,128)}, /*index=5*/f32[8,128]{1,0:T(8,128)}, f32[3,80,128]{2,1,0:T(8,128)}) custom-call(s32[512]{0:T(512)} %select_select_fusion.items, s32[35,80]{1,0:T(8,128)} %copy-done, ...), custom_call_target="tpu_custom_call" | custom-call | tf_op jit(solution)/shard_map/radius_gradient/pallas_call | solution.py:645
  130.1 1.9 collective-permute-start.7
  132.0 1.9 %collective-permute-start.8 = (f32[8,128]{1,0:T(8,128)}, f32[8,128]{1,0:T(8,128)S(1)}, u32[]{:S(2)}, u32[]{:S(2)}) collective-permute-start(f32[8,128]{1,0:T(8,128)} %get-tuple-element.49), channel_id=1, source_target_pairs={{0,31},{1,2},{2,1},{3,4},{4,3},{5,6},{6,5},{7,8},{8,7},{9,10},{10,... | collective-permute-start | bytes 12296 | tf_op jit(solution)/shard_map/ppermute | solution.py:736
  134.0 7.1 %collective-permute-done.8.two = f32[8,128]{1,0:T(8,128)S(1)} collective-permute-done((f32[8,128]{1,0:T(8,128)}, f32[8,128]{1,0:T(8,128)S(1)}, u32[]{:S(2)}, u32[]{:S(2)}) %collective-permute-start.8) | collective-permute-done | bytes 4128 | tf_op jit(solution)/shard_map/ppermute | solution.py:736
  143.1 1.9 collective-permute-start.10
  145.0 7.8 %collective-permute-start.9 = (f32[40,128]{1,0:T(8,128)}, f32[40,128]{1,0:T(8,128)S(1)}, u32[]{:S(2)}, u32[]{:S(2)}) collective-permute-start(f32[40,128]{1,0:T(8,128)} %get-tuple-element.51.above_grad), channel_id=1, source_target_pairs={{0,32},{32,64},{64,96},{96,128},{128,160},{160,192},{192,224},{224... | collective-permute-start | bytes 61448 | tf_op jit(solution)/shard_map/ppermute | solution.py:720
  152.8 2.9 %collective-permute-done.9.from_below = f32[40,128]{1,0:T(8,128)S(1)} collective-permute-done((f32[40,128]{1,0:T(8,128)}, f32[40,128]{1,0:T(8,128)S(1)}, u32[]{:S(2)}, u32[]{:S(2)}) %collective-permute-start.9) | collective-permute-done | bytes 20512 | tf_op jit(solution)/shard_map/ppermute | solution.py:720
  156.4 18.0 %forces.1 = (f32[32,128]{1,0:T(8,128)}, f32[3,32,128]{2,1,0:T(8,128)}, f32[3,32,128]{2,1,0:T(8,128)}, f32[3,8,128]{2,1,0:T(8,128)}, f32[3,8,128]{2,1,0:T(8,128)}) custom-call(s32[512]{0:T(512)} %select_select_fusion.items, s32[35,80]{1,0:T(8,128)} %copy-done, f32[80,8,128]{2,1,0:T(8,128)} %get-tuple-element.36.data, f32[80,128]{1,0:T(8,128)} %get-tuple-element.45.slope, ...), custom_call_target="tpu_custom_call" | custom-call | tf_op jit(solution)/shard_map/forces/pallas_call | solution.py:673
  174.4 5.4 %collective-permute-start.11 = (f32[3,32,128]{2,1,0:T(8,128)}, f32[3,32,128]{2,1,0:T(8,128)S(1)}, u32[]{:S(2)}, u32[]{:S(2)}) collective-permute-start(f32[3,32,128]{2,1,0:T(8,128)} %get-tuple-element.57), channel_id=1, source_target_pairs={{0,32},{32,64},{64,96},{96,128},{128,160},{160,192},{192,224},{224... | collective-permute-start | bytes 147464 | tf_op jit(solution)/shard_map/ppermute | solution.py:720
  179.9 1.9 %collective-permute-start.12 = (f32[3,8,128]{2,1,0:T(8,128)}, f32[3,8,128]{2,1,0:T(8,128)S(1)}, u32[]{:S(2)}, u32[]{:S(2)}) collective-permute-start(f32[3,8,128]{2,1,0:T(8,128)} %get-tuple-element.58), channel_id=1, source_target_pairs={{0,1},{1,2},{2,3},{3,4},{4,5},{5,6},{6,7},{7,8},{8,9},{9,10},{10,1... | collective-permute-start | bytes 36872 | tf_op jit(solution)/shard_map/ppermute | solution.py:730
  181.8 1.9 %collective-permute-start.13 = (f32[3,8,128]{2,1,0:T(8,128)}, f32[3,8,128]{2,1,0:T(8,128)S(1)}, u32[]{:S(2)}, u32[]{:S(2)}) collective-permute-start(f32[3,8,128]{2,1,0:T(8,128)} %get-tuple-element.59), channel_id=1, source_target_pairs={{0,33},{1,34},{2,35},{3,36},{4,37},{5,38},{6,39},{7,40},{8,41},{9,... | collective-permute-start | bytes 36872 | tf_op jit(solution)/shard_map/ppermute | solution.py:761
  183.7 1.8 collective-permute-done.11
  186.3 2.7 %collective-permute-done.12 = f32[3,8,128]{2,1,0:T(8,128)S(1)} collective-permute-done((f32[3,8,128]{2,1,0:T(8,128)}, f32[3,8,128]{2,1,0:T(8,128)S(1)}, u32[]{:S(2)}, u32[]{:S(2)}) %collective-permute-start.12) | collective-permute-done | bytes 12320 | tf_op jit(solution)/shard_map/ppermute | solution.py:730
  189.0 2.2 %collective-permute-done.13 = f32[3,8,128]{2,1,0:T(8,128)S(1)} collective-permute-done((f32[3,8,128]{2,1,0:T(8,128)}, f32[3,8,128]{2,1,0:T(8,128)S(1)}, u32[]{:S(2)}, u32[]{:S(2)}) %collective-permute-start.13) | collective-permute-done | bytes 12320 | tf_op jit(solution)/shard_map/ppermute | solution.py:761
  (99 shorter events, 16.1 us)
Async XLA Ops:
  2.1 31.8 %collective-permute-start.2 = (f32[16,128]{1,0:T(8,128)}, f32[16,128]{1,0:T(8,128)S(1)}, u32[]{:S(2)}, u32[]{:S(2)}) collective-permute-start(f32[16,128]{1,0:T(8,128)} %get-tuple-element.35), channel_id=1, source_target_pairs={{33,0},{34,1},{35,2},{36,3},{37,4},{38,5},{39,6},{40,7},{41,8},{42... | collective-permute-start | bytes 24584 | tf_op jit(solution)/shard_map/ppermute | solution.py:746
  15.4 18.6 %collective-permute-start.1 = (f32[16,128]{1,0:T(8,128)}, f32[16,128]{1,0:T(8,128)S(1)}, u32[]{:S(2)}, u32[]{:S(2)}) collective-permute-start(f32[16,128]{1,0:T(8,128)} %get-tuple-element.35), channel_id=1, source_target_pairs={{1,0},{2,1},{3,2},{4,3},{5,4},{6,5},{7,6},{8,7},{9,8},{10,9},{11,1... | collective-permute-start | bytes 24584 | tf_op jit(solution)/shard_map/ppermute | solution.py:725
  20.8 13.6 %collective-permute-start = (f32[200,128]{1,0:T(8,128)}, f32[200,128]{1,0:T(8,128)S(1)}, u32[]{:S(2)}, u32[]{:S(2)}) collective-permute-start(f32[200,128]{1,0:T(8,128)} %get-tuple-element.34.sent), channel_id=1, source_target_pairs={{32,0},{64,32},{96,64},{128,96},{160,128},{192,160},{224,192},{256... | collective-permute-start | bytes 307208 | tf_op jit(solution)/shard_map/ppermute | solution.py:715
  33.9 5.8 %copy-start.6 = (f32[16,128]{1,0:T(8,128)}, f32[16,128]{1,0:T(8,128)S(1)}, u32[]{:S(2)}) copy-start(f32[16,128]{1,0:T(8,128)S(1)} %collective-permute-done.2.above_edges) | copy-start | bytes 24580
  33.9 5.8 %copy-start.7 = (f32[16,128]{1,0:T(8,128)}, f32[16,128]{1,0:T(8,128)S(1)}, u32[]{:S(2)}) copy-start(f32[16,128]{1,0:T(8,128)S(1)} %collective-permute-done.1.edges) | copy-start | bytes 24580
  34.4 5.3 %copy-start.1 = (f32[200,128]{1,0:T(8,128)}, f32[200,128]{1,0:T(8,128)S(1)}, u32[]{:S(2)}) copy-start(f32[200,128]{1,0:T(8,128)S(1)} %collective-permute-done.above) | copy-start | bytes 307204
  36.3 3.4 %copy-start = (s32[35,80]{1,0:T(8,128)}, s32[35,80]{1,0:T(8,128)S(1)}, u32[]{:S(2)}) copy-start(s32[35,80]{1,0:T(8,128)S(1)} %pad_add_fusion.reach) | copy-start | bytes 33604
  77.3 3.9 %collective-permute-start.3 = (f32[8,128]{1,0:T(8,128)}, f32[8,128]{1,0:T(8,128)S(1)}, u32[]{:S(2)}, u32[]{:S(2)}) collective-permute-start(f32[8,128]{1,0:T(8,128)} %get-tuple-element.40), channel_id=1, source_target_pairs={{0,1},{1,0},{2,3},{3,2},{4,5},{5,4},{6,7},{7,6},{8,9},{9,8},{10,11... | collective-permute-start | bytes 12296 | tf_op jit(solution)/shard_map/ppermute | solution.py:736
  79.2 9.2 %collective-permute-start.4 = (f32[8,128]{1,0:T(8,128)}, f32[8,128]{1,0:T(8,128)S(1)}, u32[]{:S(2)}, u32[]{:S(2)}) collective-permute-start(f32[8,128]{1,0:T(8,128)} %get-tuple-element.41), channel_id=1, source_target_pairs={{0,31},{1,2},{2,1},{3,4},{4,3},{5,6},{6,5},{7,8},{8,7},{9,10},{10,... | collective-permute-start | bytes 12296 | tf_op jit(solution)/shard_map/ppermute | solution.py:736
  81.2 7.2 %copy-start.8 = (f32[8,128]{1,0:T(8,128)}, f32[8,128]{1,0:T(8,128)S(1)}, u32[]{:S(2)}) copy-start(f32[8,128]{1,0:T(8,128)S(1)} %collective-permute-done.3.one) | copy-start | bytes 12292
  90.4 9.8 %collective-permute-start.6 = (f32[40,128]{1,0:T(8,128)}, f32[40,128]{1,0:T(8,128)S(1)}, u32[]{:S(2)}, u32[]{:S(2)}) collective-permute-start(f32[40,128]{1,0:T(8,128)} %get-tuple-element.42.own_part), channel_id=1, source_target_pairs={{32,0},{64,32},{96,64},{128,96},{160,128},{192,160},{224,192},{256... | collective-permute-start | bytes 61448 | tf_op jit(solution)/shard_map/ppermute | solution.py:715
  92.3 10.7 %collective-permute-start.5 = (f32[40,128]{1,0:T(8,128)}, f32[40,128]{1,0:T(8,128)S(1)}, u32[]{:S(2)}, u32[]{:S(2)}) collective-permute-start(f32[40,128]{1,0:T(8,128)} %get-tuple-element.43.above_part), channel_id=1, source_target_pairs={{0,32},{32,64},{64,96},{96,128},{128,160},{160,192},{192,224},{224... | collective-permute-start | bytes 61448 | tf_op jit(solution)/shard_map/ppermute | solution.py:720
  100.2 2.8 %copy-start.2 = (f32[40,128]{1,0:T(8,128)}, f32[40,128]{1,0:T(8,128)S(1)}, u32[]{:S(2)}) copy-start(f32[40,128]{1,0:T(8,128)S(1)} %collective-permute-done.6.from_above) | copy-start | bytes 61444
  103.0 0.6 copy-start.3
  130.1 3.8 %collective-permute-start.7 = (f32[8,128]{1,0:T(8,128)}, f32[8,128]{1,0:T(8,128)S(1)}, u32[]{:S(2)}, u32[]{:S(2)}) collective-permute-start(f32[8,128]{1,0:T(8,128)} %get-tuple-element.48), channel_id=1, source_target_pairs={{0,1},{1,0},{2,3},{3,2},{4,5},{5,4},{6,7},{7,6},{8,9},{9,8},{10,11... | collective-permute-start | bytes 12296 | tf_op jit(solution)/shard_map/ppermute | solution.py:736
  132.0 9.0 %collective-permute-start.8 = (f32[8,128]{1,0:T(8,128)}, f32[8,128]{1,0:T(8,128)S(1)}, u32[]{:S(2)}, u32[]{:S(2)}) collective-permute-start(f32[8,128]{1,0:T(8,128)} %get-tuple-element.49), channel_id=1, source_target_pairs={{0,31},{1,2},{2,1},{3,4},{4,3},{5,6},{6,5},{7,8},{8,7},{9,10},{10,... | collective-permute-start | bytes 12296 | tf_op jit(solution)/shard_map/ppermute | solution.py:736
  134.0 7.1 %copy-start.9 = (f32[8,128]{1,0:T(8,128)}, f32[8,128]{1,0:T(8,128)S(1)}, u32[]{:S(2)}) copy-start(f32[8,128]{1,0:T(8,128)S(1)} %collective-permute-done.7.one) | copy-start | bytes 12292
  143.1 9.8 %collective-permute-start.10 = (f32[40,128]{1,0:T(8,128)}, f32[40,128]{1,0:T(8,128)S(1)}, u32[]{:S(2)}, u32[]{:S(2)}) collective-permute-start(f32[40,128]{1,0:T(8,128)} %get-tuple-element.50.own_grad), channel_id=1, source_target_pairs={{32,0},{64,32},{96,64},{128,96},{160,128},{192,160},{224,192},{256... | collective-permute-start | bytes 61448 | tf_op jit(solution)/shard_map/ppermute | solution.py:715
  145.0 10.8 %collective-permute-start.9 = (f32[40,128]{1,0:T(8,128)}, f32[40,128]{1,0:T(8,128)S(1)}, u32[]{:S(2)}, u32[]{:S(2)}) collective-permute-start(f32[40,128]{1,0:T(8,128)} %get-tuple-element.51.above_grad), channel_id=1, source_target_pairs={{0,32},{32,64},{64,96},{96,128},{128,160},{160,192},{192,224},{224... | collective-permute-start | bytes 61448 | tf_op jit(solution)/shard_map/ppermute | solution.py:720
  152.8 2.9 %copy-start.4 = (f32[40,128]{1,0:T(8,128)}, f32[40,128]{1,0:T(8,128)S(1)}, u32[]{:S(2)}) copy-start(f32[40,128]{1,0:T(8,128)S(1)} %collective-permute-done.10.from_above) | copy-start | bytes 61444
  155.8 0.6 copy-start.5
  174.4 11.0 %collective-permute-start.11 = (f32[3,32,128]{2,1,0:T(8,128)}, f32[3,32,128]{2,1,0:T(8,128)S(1)}, u32[]{:S(2)}, u32[]{:S(2)}) collective-permute-start(f32[3,32,128]{2,1,0:T(8,128)} %get-tuple-element.57), channel_id=1, source_target_pairs={{0,32},{32,64},{64,96},{96,128},{128,160},{160,192},{192,224},{224... | collective-permute-start | bytes 147464 | tf_op jit(solution)/shard_map/ppermute | solution.py:720
  179.9 9.1 %collective-permute-start.12 = (f32[3,8,128]{2,1,0:T(8,128)}, f32[3,8,128]{2,1,0:T(8,128)S(1)}, u32[]{:S(2)}, u32[]{:S(2)}) collective-permute-start(f32[3,8,128]{2,1,0:T(8,128)} %get-tuple-element.58), channel_id=1, source_target_pairs={{0,1},{1,2},{2,3},{3,4},{4,5},{5,6},{6,7},{7,8},{8,9},{9,10},{10,1... | collective-permute-start | bytes 36872 | tf_op jit(solution)/shard_map/ppermute | solution.py:730
  181.8 9.4 %collective-permute-start.13 = (f32[3,8,128]{2,1,0:T(8,128)}, f32[3,8,128]{2,1,0:T(8,128)S(1)}, u32[]{:S(2)}, u32[]{:S(2)}) collective-permute-start(f32[3,8,128]{2,1,0:T(8,128)} %get-tuple-element.59), channel_id=1, source_target_pairs={{0,33},{1,34},{2,35},{3,36},{4,37},{5,38},{6,39},{7,40},{8,41},{9,... | collective-permute-start | bytes 36872 | tf_op jit(solution)/shard_map/ppermute | solution.py:761
  (2 other events, 1.2 us)
